TPU v7x, 128 devices: a whole 4x4x4 slice. The times are simulated.
128 devices in a mesh: band: 16 (over y_lo, z, core), grid: 8 (over x, y_hi).
Axes of the slice: x: 4, y: 4 (y_hi: 2, y_lo: 2; y = y_hi * 2 + y_lo), z: 4, core: 2. Of those that a mesh axis runs over, the one named last changes fastest.
Arguments:
- orbitals: bfloat16 [32, 192, 192, 192], P('band', 'grid'), may hold values from -6 to 6
- plan: int32 [2, 32], P(None, 'band'), may hold values from 0 to 1
Outputs:
- exchange_image: bfloat16 [32, 192, 192, 192], P('band', 'grid')
Inputs may be any that keep to these rules, and one draw needn't show every extreme that they name: plan[s, i] is the position, within the partner group of band i at shift s + 1, of the band that band i pairs with.
All inputs are finite; a program needn't handle non-finite values.
Results may differ from a plain program's by a relative error of at most 0.0095.
Values may be sent and summed in bfloat16 or wider, within the bound.
No kernel may reach another device: no remote copies, remote signals or barrier semaphores. Data moves between devices by JAX's collectives and lax.ppermute only.
A program may use at most 128 MiB of HBM per device.

v0:
```python
import jax
import jax.numpy as jnp
from jax import lax
from jax.sharding import PartitionSpec as P

SHIFTS = 2


screening = 0.0005


def shifted(block, axis, distance):
    devices = range(lax.axis_size(axis))
    route = [((i - distance) % len(devices), i) for i in devices]
    return lax.ppermute(block, axis, route)


def sine_table(length):
    counts = jnp.arange(1, length + 1, dtype=jnp.float32)
    return jnp.sin(jnp.pi * counts[:, None] * counts[None, :] / (length + 1)).astype(jnp.bfloat16)


def eigen_line(modes, length):
    return 2.0 - 2.0 * jnp.cos(jnp.pi * modes / (length + 1))


def shards(orbitals, plan):
    per_group, slab_planes, _, length = orbitals.shape
    columns = length // lax.axis_size("grid")
    sines = sine_table(length)
    modes = jnp.arange(1, length + 1, dtype=jnp.float32)
    local_modes = (
        lax.axis_index("grid") * columns + jnp.arange(1, columns + 1, dtype=jnp.int32)
    ).astype(jnp.float32)
    along_full = eigen_line(modes, length)
    along_local = eigen_line(local_modes, length)
    kernel = (2.0 / (length + 1)) ** 3 / (
        along_full[:, None, None]
        + along_local[None, :, None]
        + along_full[None, None, :]
        + screening
    )
    positions = jnp.arange(per_group, dtype=jnp.int32)
    own_sums = jnp.zeros(orbitals.shape, jnp.float32)
    for offset in range(1, SHIFTS + 1):
        partner_block = shifted(orbitals, "band", -offset)
        picker = (plan[offset - 1][:, None] == positions[None, :]).astype(jnp.bfloat16)
        chosen = jnp.einsum(
            "ip,pxyz->ixyz", picker, partner_block, preferred_element_type=jnp.float32
        ).astype(jnp.bfloat16)
        density = (orbitals.astype(jnp.float32) * chosen.astype(jnp.float32)).astype(jnp.bfloat16)
        section = jnp.dot(density, sines, preferred_element_type=jnp.float32).astype(jnp.bfloat16)
        section = jnp.einsum(
            "pxyz,ky->pxkz", section, sines, preferred_element_type=jnp.float32
        ).astype(jnp.bfloat16)
        spectrum = jnp.einsum(
            "pxyz,kx->pkyz",
            lax.all_to_all(section, "grid", split_axis=2, concat_axis=1, tiled=True),
            sines,
            preferred_element_type=jnp.float32,
        )
        scaled = (spectrum * kernel).astype(jnp.bfloat16)
        inverse = jnp.einsum(
            "pxyz,kx->pkyz", scaled, sines, preferred_element_type=jnp.float32
        ).astype(jnp.bfloat16)
        planes = jnp.einsum(
            "pxyz,ky->pxkz",
            lax.all_to_all(inverse, "grid", split_axis=1, concat_axis=2, tiled=True),
            sines,
            preferred_element_type=jnp.float32,
        ).astype(jnp.bfloat16)
        potential = jnp.dot(planes, sines, preferred_element_type=jnp.float32)
        own_term = potential * chosen.astype(jnp.float32)
        weighted = potential * orbitals.astype(jnp.float32)
        partner_term = jnp.einsum("ip,ixyz->pxyz", picker.astype(jnp.float32), weighted)
        own_term, partner_term = (own_term, partner_term)
        own_sums = own_sums + own_term
        returned = shifted(partner_term.astype(jnp.bfloat16), "band", offset)
        own_sums = own_sums + returned.astype(jnp.float32)
    return (-own_sums).astype(jnp.bfloat16)


def solution(mesh):
    return jax.shard_map(
        shards,
        mesh=mesh,
        in_specs=(P("band", "grid", None, None), P(None, "band")),
        out_specs=P("band", "grid", None, None),
        check_vma=False,
    )
```

profile of v0, /device:TPU:1, one launch (start us, length us, event | category | flops | bytes accessed | tf_op | source)
XLA Modules:
  0.0 634.1 jit_solution(820555954861824620)
XLA Ops:
  0.0 9.4 %copy.71 = bf16[2,24,192,192]{3,0,2,1:T(2,128)(2,1)} copy(bf16[2,24,192,192]{3,2,1,0:T(8,128)(2,1)} %param.2) | data formatting | bytes 7077888 | tf_op args[0]
  16.5 99.3 %collective-permute-done.2 = bf16[2,24,192,192]{3,0,2,1:T(2,128)(2,1)S(1)} collective-permute-done((bf16[2,24,192,192]{3,0,2,1:T(2,128)(2,1)}, bf16[2,24,192,192]{3,0,2,1:T(2,128)(2,1)S(1)}, u32[]{:S(2)}, u32[]{:S(2)}) %collective-permute-start.2) | collective-permute-done | bytes 3538976 | tf_op jit(solution)/shard_map/ppermute | solution.py:15
  115.8 8.0 %fusion.118 = bf16[2,24,192,192]{3,0,2,1:T(2,128)(2,1)} fusion(bf16[2,24,192,192]{3,0,2,1:T(2,128)(2,1)S(1)} %collective-permute-done.2, s32[2]{0:T(128)S(1)} %get-tuple-element.7), kind=kOutput, calls=%fused_computation.75 | convolution fusion | flops 7077892 | bytes 7077896 | tf_op jit(solution)/shard_map/ip,pxyz->ixyz/dot_general | solution.py:48
  123.8 10.0 %convert_bitcast_fusion.1 = bf16[2,24,192,192]{3,2,1,0:T(8,128)(2,1)} fusion(bf16[2,24,192,192]{3,2,1,0:T(8,128)(2,1)} %param.2, bf16[2,24,192,192]{3,0,2,1:T(2,128)(2,1)} %fusion.118, f32[192]{0:T(256)S(1)} %get-tuple-element.10, f32[192]{0:T(256)S(1)} %get-tuple-element.11), kind=kOutput, calls=%fused_computation.39 | convolution fusion | flops 1369792512 | bytes 10618368 | tf_op jit(solution)/shard_map/pxyz,ky->pxkz/dot_general | solution.py:53
  133.8 7.1 %copy.86 = bf16[2,24,192,192]{3,1,0,2:T(8,128)(2,1)} copy(bf16[2,24,192,192]{3,2,1,0:T(8,128)(2,1)} %convert_bitcast_fusion.1) | data formatting | bytes 7077888 | tf_op jit(solution)/shard_map/convert_element_type | solution.py:55
  147.6 17.6 %collective-permute-done = bf16[2,24,192,192]{3,0,2,1:T(2,128)(2,1)} collective-permute-done((bf16[2,24,192,192]{3,0,2,1:T(2,128)(2,1)}, bf16[2,24,192,192]{3,0,2,1:T(2,128)(2,1)}, u32[]{:S(2)}, u32[]{:S(2)}) %collective-permute-start) | collective-permute-done | bytes 3538976 | tf_op jit(solution)/shard_map/ppermute | solution.py:15
  165.2 9.8 %fusion.119 = bf16[2,24,192,192]{3,0,2,1:T(2,128)(2,1)} fusion(bf16[2,24,192,192]{3,0,2,1:T(2,128)(2,1)} %collective-permute-done, s32[2]{0:T(128)S(1)} %get-tuple-element.8), kind=kOutput, calls=%fused_computation.77 | convolution fusion | flops 7077892 | bytes 7077896 | tf_op jit(solution)/shard_map/ip,pxyz->ixyz/dot_general | solution.py:48
  175.0 10.0 %convert_bitcast_fusion.3 = bf16[2,24,192,192]{3,2,1,0:T(8,128)(2,1)} fusion(bf16[2,24,192,192]{3,2,1,0:T(8,128)(2,1)} %param.2, bf16[2,24,192,192]{3,0,2,1:T(2,128)(2,1)} %fusion.119, f32[192]{0:T(256)S(1)} %get-tuple-element.10, f32[192]{0:T(256)S(1)} %get-tuple-element.11), kind=kOutput, calls=%fused_computation.47 | convolution fusion | flops 1369792512 | bytes 10618368 | tf_op jit(solution)/shard_map/pxyz,ky->pxkz/dot_general | solution.py:53
  185.0 7.2 %copy.74 = bf16[2,24,192,192]{3,1,0,2:T(8,128)(2,1)} copy(bf16[2,24,192,192]{3,2,1,0:T(8,128)(2,1)} %convert_bitcast_fusion.3) | data formatting | bytes 7077888 | tf_op jit(solution)/shard_map/convert_element_type | solution.py:55
  192.3 20.7 %all-to-all-done.2 = bf16[2,24,192,192]{3,1,0,2:T(8,128)(2,1)} async-done(((bf16[2,24,192,192]{3,1,0,2:T(8,128)(2,1)}), bf16[2,24,192,192]{3,1,0,2:T(8,128)(2,1)}, u32[]{:S(2)}, u32[]{:S(2)}) %all-to-all-start.2) | async-done | bytes 3538976 | tf_op jit(solution)/shard_map/all_to_all | solution.py:58
  226.7 10.2 %convert_bitcast_fusion = bf16[2,192,24,192]{3,1,2,0:T(8,128)(2,1)} fusion(f32[192,24,192]{2,0,1:T(8,128)} %add_divide_fusion, bf16[2,192,24,192]{3,2,1,0:T(8,128)(2,1)} %bitcast.90, f32[192]{0:T(256)S(1)} %get-tuple-element.10, f32[192]{0:T(256)S(1)} %get-tuple-element.11), kind=kOutput, calls=%fused_computation.38 | convolution fusion | flops 1364484096 | bytes 10618368 | tf_op jit(solution)/shard_map/pxyz,kx->pkyz/dot_general | solution.py:63
  236.9 7.2 %copy.90 = bf16[2,192,24,192]{3,2,0,1:T(8,128)(2,1)} copy(bf16[2,192,24,192]{3,1,2,0:T(8,128)(2,1)} %convert_bitcast_fusion) | data formatting | bytes 7077888 | tf_op jit(solution)/shard_map/convert_element_type | solution.py:65
  244.1 11.4 %all-to-all-done = bf16[2,24,192,192]{3,1,0,2:T(8,128)(2,1)} async-done(((bf16[2,24,192,192]{3,1,0,2:T(8,128)(2,1)}), bf16[2,24,192,192]{3,1,0,2:T(8,128)(2,1)}, u32[]{:S(2)}, u32[]{:S(2)}) %all-to-all-start) | async-done | bytes 3538976 | tf_op jit(solution)/shard_map/all_to_all | solution.py:58
  266.9 10.2 %convert_bitcast_fusion.2 = bf16[2,192,24,192]{3,1,2,0:T(8,128)(2,1)} fusion(f32[192,24,192]{2,0,1:T(8,128)} %add_divide_fusion, bf16[2,192,24,192]{3,2,1,0:T(8,128)(2,1)} %bitcast.89, f32[192]{0:T(256)S(1)} %get-tuple-element.10, f32[192]{0:T(256)S(1)} %get-tuple-element.11), kind=kOutput, calls=%fused_computation.43 | convolution fusion | flops 1364484096 | bytes 10618368 | tf_op jit(solution)/shard_map/pxyz,kx->pkyz/dot_general | solution.py:63
  277.1 7.1 %copy.78 = bf16[2,192,24,192]{3,2,0,1:T(8,128)(2,1)} copy(bf16[2,192,24,192]{3,1,2,0:T(8,128)(2,1)} %convert_bitcast_fusion.2) | data formatting | bytes 7077888 | tf_op jit(solution)/shard_map/convert_element_type | solution.py:65
  284.2 23.8 %all-to-all-done.3 = bf16[2,192,24,192]{3,2,0,1:T(8,128)(2,1)} async-done(((bf16[2,192,24,192]{3,2,0,1:T(8,128)(2,1)}), bf16[2,192,24,192]{3,2,0,1:T(8,128)(2,1)}, u32[]{:S(2)}, u32[]{:S(2)}) %all-to-all-start.3) | async-done | bytes 3538976 | tf_op jit(solution)/shard_map/all_to_all | solution.py:68
  320.2 9.8 %fusion.21 = f32[2,24,192,192]{3,2,1,0:T(8,128)} fusion(bf16[2,24,192,192]{3,2,1,0:T(8,128)(2,1)} %bitcast.91, f32[192]{0:T(256)S(1)} %get-tuple-element.10, f32[192]{0:T(256)S(1)} %get-tuple-element.11), kind=kOutput, calls=%fused_computation.29 | convolution fusion | flops 1360945152 | bytes 10618368 | tf_op jit(solution)/shard_map/dot_general | solution.py:72
  330.1 40.0 %all-to-all-done.1 = bf16[2,192,24,192]{3,2,0,1:T(8,128)(2,1)} async-done(((bf16[2,192,24,192]{3,2,0,1:T(8,128)(2,1)}), bf16[2,192,24,192]{3,2,0,1:T(8,128)(2,1)}, u32[]{:S(2)}, u32[]{:S(2)}) %all-to-all-start.1) | async-done | bytes 3538976 | tf_op jit(solution)/shard_map/all_to_all | solution.py:68
  375.2 15.3 %convert_multiply_fusion.2 = (bf16[2,24,192,192]{3,2,1,0:T(8,128)(2,1)}, bf16[2,24,192,192]{3,2,1,0:T(8,128)(2,1)}, f32[2,24,192,192]{3,2,1,0:T(8,128)}) fusion(bf16[2,24,192,192]{3,2,1,0:T(8,128)(2,1)} %param.2, f32[2,24,192,192]{3,2,1,0:T(8,128)} %fusion.21, f32[192]{0:T(256)S(1)} %get-tuple-element.10, f32[192]{0:T(256)S(1)} %get-tuple-element.11, ...), kind=kOutput, calls=%fused_computation.2 | convolution fusion | flops 1369792512 | bytes 28313088 | tf_op jit(solution)/shard_map/dot_general | solution.py:72
  390.6 9.2 %fusion.9 = bf16[2,24,192,192]{3,0,2,1:T(2,128)(2,1)S(1)} fusion(bf16[2,24,192,192]{3,2,1,0:T(8,128)(2,1)} %get-tuple-element.5, s32[2]{0:T(128)S(1)} %get-tuple-element.8), kind=kOutput, calls=%fused_computation.21 | convolution fusion | flops 7077892 | bytes 7077896 | tf_op jit(solution)/shard_map/ip,ixyz->pxyz/dot_general | solution.py:75
  415.6 53.2 %collective-permute-start.3 = (bf16[2,24,192,192]{3,2,1,0:T(8,128)(2,1)}, bf16[2,24,192,192]{3,2,1,0:T(8,128)(2,1)S(1)}, u32[]{:S(2)}, u32[]{:S(2)}) collective-permute-start(bf16[2,24,192,192]{3,2,1,0:T(8,128)(2,1)} %copy.138), channel_id=1, source_target_pairs={{112,0},{120,8},{0,16},{8,24},{16,32},{24,40},{32,48},{40,56},{48,... | collective-permute-start | bytes 10616840 | tf_op jit(solution)/shard_map/ppermute | solution.py:15
  472.3 95.6 %collective-permute-done.3 = bf16[2,24,192,192]{3,2,1,0:T(8,128)(2,1)S(1)} collective-permute-done((bf16[2,24,192,192]{3,2,1,0:T(8,128)(2,1)}, bf16[2,24,192,192]{3,2,1,0:T(8,128)(2,1)S(1)}, u32[]{:S(2)}, u32[]{:S(2)}) %collective-permute-start.3) | collective-permute-done | bytes 3538976 | tf_op jit(solution)/shard_map/ppermute | solution.py:15
  567.9 53.2 %collective-permute-done.1 = bf16[2,24,192,192]{3,2,1,0:T(8,128)(2,1)S(1)} collective-permute-done((bf16[2,24,192,192]{3,2,1,0:T(8,128)(2,1)S(1)}, bf16[2,24,192,192]{3,2,1,0:T(8,128)(2,1)S(1)}, u32[]{:S(2)}, u32[]{:S(2)}) %collective-permute-start.1) | collective-permute-done | bytes 3538976 | tf_op jit(solution)/shard_map/ppermute | solution.py:15
  623.3 10.6 %fusion.4 = bf16[2,24,192,192]{3,2,1,0:T(8,128)(2,1)} fusion(f32[2,24,192,192]{3,2,1,0:T(8,128)S(1)} %bitcast.87, f32[2,24,192,192]{3,2,1,0:T(8,128)S(1)} %bitcast.85, bf16[2,24,192,192]{3,2,1,0:T(8,128)(2,1)} %copy-done.2, bf16[2,24,192,192]{3,2,1,0:T(8,128)(2,1)} %copy-done.3, bf16[2,24,192,192]{3,0,2,1:T(2,128)(2,1)} %fusion.119, ...), kind=kLoop, calls=%fused_computation.10 | loop fusion | flops 19464192 | bytes 31850496 | tf_op jit(solution)/shard_map/convert_element_type | solution.py:80
  (44 shorter events, 77.5 us)
Async XLA Ops:
  0.0 16.5 %copy-start.4 = (s32[2,2]{1,0:T(2,128)S(1)}, s32[2,2]{1,0:T(2,128)}, u32[]{:S(2)}) copy-start(s32[2,2]{1,0:T(2,128)} %param.3) | copy-start | bytes 52
  9.5 106.4 %collective-permute-start.2 = (bf16[2,24,192,192]{3,0,2,1:T(2,128)(2,1)}, bf16[2,24,192,192]{3,0,2,1:T(2,128)(2,1)S(1)}, u32[]{:S(2)}, u32[]{:S(2)}) collective-permute-start(bf16[2,24,192,192]{3,0,2,1:T(2,128)(2,1)} %copy.71), channel_id=1, source_target_pairs={{16,0},{24,8},{32,16},{40,24},{48,32},{56,40},{64,48},{72,56},{80,... | collective-permute-start | bytes 10616840 | tf_op jit(solution)/shard_map/ppermute | solution.py:15
  15.1 150.1 %collective-permute-start = (bf16[2,24,192,192]{3,0,2,1:T(2,128)(2,1)}, bf16[2,24,192,192]{3,0,2,1:T(2,128)(2,1)}, u32[]{:S(2)}, u32[]{:S(2)}) collective-permute-start(bf16[2,24,192,192]{3,0,2,1:T(2,128)(2,1)} %copy.71), channel_id=1, source_target_pairs={{8,0},{16,8},{24,16},{32,24},{40,32},{48,40},{56,48},{64,56},{72,6... | collective-permute-start | bytes 10616840 | tf_op jit(solution)/shard_map/ppermute | solution.py:15
  141.0 72.0 %all-to-all-start.2 = ((bf16[2,24,192,192]{3,1,0,2:T(8,128)(2,1)}), bf16[2,24,192,192]{3,1,0,2:T(8,128)(2,1)}, u32[]{:S(2)}, u32[]{:S(2)}) async-start(bf16[2,24,192,192]{3,1,0,2:T(8,128)(2,1)} %copy.86), calls=%async_computation.2 | async-start | bytes 9437184 | tf_op jit(solution)/shard_map/all_to_all | solution.py:58
  213.0 42.5 %all-to-all-start = ((bf16[2,24,192,192]{3,1,0,2:T(8,128)(2,1)}), bf16[2,24,192,192]{3,1,0,2:T(8,128)(2,1)}, u32[]{:S(2)}, u32[]{:S(2)}) async-start(bf16[2,24,192,192]{3,1,0,2:T(8,128)(2,1)} %copy.74), calls=%async_computation | async-start | bytes 9437184 | tf_op jit(solution)/shard_map/all_to_all | solution.py:58
  255.5 52.5 %all-to-all-start.3 = ((bf16[2,192,24,192]{3,2,0,1:T(8,128)(2,1)}), bf16[2,192,24,192]{3,2,0,1:T(8,128)(2,1)}, u32[]{:S(2)}, u32[]{:S(2)}) async-start(bf16[2,192,24,192]{3,2,0,1:T(8,128)(2,1)} %copy.90), calls=%async_computation.3 | async-start | bytes 9437184 | tf_op jit(solution)/shard_map/all_to_all | solution.py:68
  308.0 62.1 %all-to-all-start.1 = ((bf16[2,192,24,192]{3,2,0,1:T(8,128)(2,1)}), bf16[2,192,24,192]{3,2,0,1:T(8,128)(2,1)}, u32[]{:S(2)}, u32[]{:S(2)}) async-start(bf16[2,192,24,192]{3,2,0,1:T(8,128)(2,1)} %copy.78), calls=%async_computation.1 | async-start | bytes 9437184 | tf_op jit(solution)/shard_map/all_to_all | solution.py:68
  399.8 3.5 copy-start
  403.0 220.3 %slice-start = ((s8[9437184]{0:T(1024)(128)(4,1)}), s8[4194304]{0:T(1024)(128)(4,1)S(1)}, s32[]{:S(2)}) async-start(s8[9437184]{0:T(1024)(128)(4,1)} %bitcast.84), calls=%async_computation.4 | async-start | bytes 8388608
  403.0 220.3 %slice-start.3 = ((s8[9437184]{0:T(1024)(128)(4,1)}), s8[4194304]{0:T(1024)(128)(4,1)S(1)}, s32[]{:S(2)}) async-start(s8[9437184]{0:T(1024)(128)(4,1)} %bitcast.86), calls=%async_computation.7 | async-start | bytes 8388608
  403.3 220.0 %slice-start.1 = ((s8[9437184]{0:T(1024)(128)(4,1)}), s8[4194304]{0:T(1024)(128)(4,1)S(1)}, s32[]{:S(2)}) async-start(s8[9437184]{0:T(1024)(128)(4,1)} %bitcast.84), calls=%async_computation.5 | async-start | bytes 8388608
  403.3 220.0 %slice-start.2 = ((s8[9437184]{0:T(1024)(128)(4,1)}), s8[1048576]{0:T(1024)(128)(4,1)S(1)}, s32[]{:S(2)}) async-start(s8[9437184]{0:T(1024)(128)(4,1)} %bitcast.84), calls=%async_computation.6 | async-start | bytes 2097152
  403.3 220.0 %slice-start.4 = ((s8[9437184]{0:T(1024)(128)(4,1)}), s8[4194304]{0:T(1024)(128)(4,1)S(1)}, s32[]{:S(2)}) async-start(s8[9437184]{0:T(1024)(128)(4,1)} %bitcast.86), calls=%async_computation.8 | async-start | bytes 8388608
  403.3 220.0 %slice-start.5 = ((s8[9437184]{0:T(1024)(128)(4,1)}), s8[1048576]{0:T(1024)(128)(4,1)S(1)}, s32[]{:S(2)}) async-start(s8[9437184]{0:T(1024)(128)(4,1)} %bitcast.86), calls=%async_computation.9 | async-start | bytes 2097152
  410.1 58.7 %copy-start.1 = (bf16[2,24,192,192]{3,2,1,0:T(8,128)(2,1)S(1)}, bf16[2,24,192,192]{3,2,1,0:T(8,128)(2,1)}, u32[]{:S(2)}) copy-start(bf16[2,24,192,192]{3,2,1,0:T(8,128)(2,1)} %copy.139) | copy-start | bytes 10616836
  415.6 152.3 %collective-permute-start.3 = (bf16[2,24,192,192]{3,2,1,0:T(8,128)(2,1)}, bf16[2,24,192,192]{3,2,1,0:T(8,128)(2,1)S(1)}, u32[]{:S(2)}, u32[]{:S(2)}) collective-permute-start(bf16[2,24,192,192]{3,2,1,0:T(8,128)(2,1)} %copy.138), channel_id=1, source_target_pairs={{112,0},{120,8},{0,16},{8,24},{16,32},{24,40},{32,48},{40,56},{48,... | collective-permute-start | bytes 10616840 | tf_op jit(solution)/shard_map/ppermute | solution.py:15
  468.8 152.4 %collective-permute-start.1 = (bf16[2,24,192,192]{3,2,1,0:T(8,128)(2,1)S(1)}, bf16[2,24,192,192]{3,2,1,0:T(8,128)(2,1)S(1)}, u32[]{:S(2)}, u32[]{:S(2)}) collective-permute-start(bf16[2,24,192,192]{3,2,1,0:T(8,128)(2,1)S(1)} %copy-done.1), channel_id=1, source_target_pairs={{120,0},{0,8},{8,16},{16,24},{24,32},{32,40},{40,48},{48,56},{56,6... | collective-permute-start | bytes 10616840 | tf_op jit(solution)/shard_map/ppermute | solution.py:15
  567.9 53.2 %copy-start.2 = (bf16[2,24,192,192]{3,2,1,0:T(8,128)(2,1)}, bf16[2,24,192,192]{3,2,1,0:T(8,128)(2,1)S(1)}, u32[]{:S(2)}) copy-start(bf16[2,24,192,192]{3,2,1,0:T(8,128)(2,1)S(1)} %collective-permute-done.3) | copy-start | bytes 10616836
  621.2 2.1 copy-start.3
where the time goes:
time: 640 us; the launch traced here: 634 us
  waiting for transfers between devices  362 us (57%)
  matrix products  99.4 us (16%)
  starting transfers between devices  87.4 us (14%)
  local copies, waits for them, and re-layouts  71.8 us (11%)
  other arithmetic  13.4 us (2%)
    ppermute x4, waiting for transfers between devices, shifted(): return lax.ppermute(block, axis, route)  266 us
    all_to_all x2, waiting for transfers between devices, shards(): lax.all_to_all(inverse, 'grid', split_axis=1, concat_axis=2, tiled=True)  63.8 us
    ppermute x4, starting transfers between devices, shifted(): return lax.ppermute(block, axis, route)  63.7 us
    all_to_all x2, waiting for transfers between devices, shards(): lax.all_to_all(section, 'grid', split_axis=2, concat_axis=1, tiled=True)  32.1 us
    dot_general x2, matrix products, shards(): potential = jnp.dot(planes, sines, preferred_element_type=jnp.float32)  25.2 us
    dot_general x2, matrix products, shards(): jnp.einsum('pxyz,kx->pkyz', scaled, sines, preferred_element_type=jnp.flo...  20.4 us
    dot_general x2, matrix products, shards(): jnp.einsum('pxyz,ky->pxkz', section, sines, preferred_element_type=jnp.fl...  20.1 us
    dot_general x2, matrix products, shards(): jnp.einsum('ip,pxyz->ixyz', picker, partner_block, preferred_element_type...  17.8 us
  transfers between devices with their start and end apart: 8, of which 8 were waited for; matrix products, arithmetic and copies ran while one was open for 18% of the time, Pallas kernels for 0%

commit v1 on v0

v1 whole, which is shorter than its diff:
```python
import functools

import jax
import jax.numpy as jnp
from jax import lax
from jax.experimental import pallas as pl
from jax.experimental.pallas import tpu as pltpu
from jax.sharding import PartitionSpec as P

screening = 0.0005
NG = 192
SLABS = 8
ROWS = NG // SLABS
PAIRS = 4
WIDE = PAIRS * NG
PAIRED = ROWS // 2
PIECES_IN = (6, 4, 2)
PIECES_OUT = (2, 4, 4, 2)

F32 = jnp.float32
BF16 = jnp.bfloat16
VMEM_LIMIT = 16 * 1024 * 1024

SWAP_BAND, THIRD_BAND, CORE = 0, 2, 4


def params():
    return pltpu.CompilerParams(vmem_limit_bytes=VMEM_LIMIT)


def call(kernel, grid, in_specs, out_specs, out_shape, scratch=(), aliases={}, cost=0):
    return pl.pallas_call(
        kernel,
        grid_spec=pltpu.PrefetchScalarGridSpec(
            num_scalar_prefetch=1, grid=grid, in_specs=in_specs, out_specs=out_specs, scratch_shapes=scratch
        ),
        out_shape=out_shape,
        input_output_aliases=aliases,
        compiler_params=params(),
        cost_estimate=pl.CostEstimate(flops=0, bytes_accessed=cost, transcendentals=0),
    )


def sine_table():
    counts = jnp.arange(1, NG + 1, dtype=F32)
    return jnp.sin(jnp.pi * counts[:, None] * counts[None, :] / (NG + 1)).astype(BF16)


def eigen_line(modes):
    half = jnp.sin(jnp.pi * modes / (2 * (NG + 1)))
    return 4.0 * half * half


def decay(first, second):
    mu = eigen_line(first)[:, None] + eigen_line(second)[None, :] + screening
    root = 1.0 / (1.0 + 0.5 * mu + jnp.sqrt(mu + 0.25 * mu * mu))
    return jnp.concatenate([root, root], axis=1)


def twice(block):
    return jnp.concatenate([block, block], axis=1)


def unpacked(ref, band, half):
    tail = ref[band, 0, 2].astype(F32)
    return jnp.concatenate([ref[band, 0, half].astype(F32), tail[:, 64 * half : 64 * half + 64]], axis=1)


def pack_into(ref, band, low, high):
    ref[band, 0, 0] = low[:, :128].astype(BF16)
    ref[band, 0, 1] = high[:, :128].astype(BF16)
    ref[band, 0, 2] = jnp.concatenate([low[:, 128:], high[:, 128:]], axis=1).astype(BF16)


def planes(block):
    return pl.BlockSpec((2, 2, NG, NG), lambda i, table: (0, block(i), 0, 0))


def packed(block):
    return pl.BlockSpec((2, 1, 3, NG, 128), lambda i, table: (0, block(i), 0, 0, 0))


def spectra(block):
    return pl.BlockSpec((2, NG, WIDE), lambda i, table: (block(i), 0, 0))


def whole(*shape):
    return pl.BlockSpec(shape, lambda i, table: (0,) * len(shape))


ANY = pl.BlockSpec(memory_space=pl.ANY)
STATE = jax.ShapeDtypeStruct((NG, WIDE), F32)


def pack_kernel(table, x_ref, z_ref):
    for band in range(2):
        pack_into(z_ref, band, x_ref[band, 0].astype(F32), x_ref[band, 1].astype(F32))


def pack(table, x, start, count):
    return call(
        pack_kernel,
        (count,),
        [planes(lambda i: start + i)],
        packed(lambda i: i),
        jax.ShapeDtypeStruct((2, count, 3, NG, 128), BF16),
    )(table, x)


def forward_kernel(start, first, last, table, x_ref, s_ref, z_ref, sines_ref, r_ref, log_ref, *refs):
    refs = list(refs)
    if not first:
        p_in, a_in, _ = (refs.pop(0) for _ in range(3))
    out_ref = refs.pop(0)
    results = [refs.pop(0) for _ in range(1 if last else 2)]
    p_ref, a_ref, both = refs
    step = pl.program_id(0)

    @pl.when(step == 0)
    def _():
        p_ref[...] = jnp.zeros_like(p_ref) if first else p_in[...]
        a_ref[...] = jnp.zeros_like(a_ref) if first else a_in[...]

    core = table[CORE]
    sines = sines_ref[...]
    for half in range(2):
        for band in range(2):
            both[0, band] = x_ref[band, half]
            both[1, band] = unpacked(z_ref, band, half).astype(BF16)
        rows = [both[core, q] * s_ref[table[SWAP_BAND + q], half] for q in range(2)]
        rows += [both[core, q] * both[1 - core, table[THIRD_BAND + q]] for q in range(2)]
        section = jnp.dot(jnp.concatenate(rows, axis=0), sines, preferred_element_type=F32).astype(BF16)
        section = jnp.concatenate([section[q * NG : (q + 1) * NG] for q in range(PAIRS)], axis=1)
        section = jnp.dot(sines, section, preferred_element_type=F32)
        p = twice(r_ref[...]) * p_ref[...] + section
        p_ref[...] = p
        out_ref[half] = p.astype(BF16)
        depth = (2 * (start + step) + half).astype(F32)
        a_ref[...] += twice(jnp.exp2(depth * log_ref[...])) * section

    @pl.when(step == pl.num_programs(0) - 1)
    def _():
        if last:
            results[0][:, :WIDE] = a_ref[...].astype(BF16)
            results[0][:, WIDE:] = p_ref[...].astype(BF16)
        else:
            results[0][...] = p_ref[...]
            results[1][...] = a_ref[...]


def forward(table, x, s, z, sines, r, log_r, carried, start, count):
    first, last = carried is None, start + count == PAIRED
    at = lambda i: start + i
    return call(
        functools.partial(forward_kernel, start, first, last),
        (count,),
        [planes(at), planes(at), packed(lambda i: i), whole(NG, NG), whole(NG, 2 * NG), whole(NG, 2 * NG)]
        + ([] if first else [whole(NG, WIDE), whole(NG, WIDE), ANY]),
        [spectra(at)] + ([whole(NG, 2 * WIDE)] if last else [whole(NG, WIDE)] * 2),
        [jax.ShapeDtypeStruct((ROWS, NG, WIDE), BF16)]
        + ([jax.ShapeDtypeStruct((NG, 2 * WIDE), BF16)] if last else [STATE] * 2),
        scratch=[pltpu.VMEM((NG, WIDE), F32)] * 2 + [pltpu.VMEM((2, 2, NG, NG), BF16)],
        aliases={} if first else {9: 0},
    )(table, x, s, z, sines, r, log_r, *(() if first else (carried[1], carried[2], carried[0])))


def couple_kernel(table, r_ref, in_ref, out_ref):
    r = twice(r_ref[...])
    r2 = r * r
    r4 = r2 * r2
    r8 = r4 * r4
    span = r8 * r8 * r8
    gain = r / (1.0 - r2)
    part = lambda j, k: in_ref[j * ROWS : (j + 1) * ROWS, k * WIDE : (k + 1) * WIDE].astype(F32)
    reach = [jnp.ones_like(span)]
    left = [jnp.zeros_like(span)]
    for j in range(SLABS):
        reach.append(reach[-1] * span)
        left.append(span * left[-1] + part(j, 1))
    right = [jnp.zeros_like(span)]
    for j in reversed(range(SLABS)):
        right.insert(0, span * right[0] + part(j, 0))
    full = r * reach[SLABS]
    scale = r / (1.0 - full * full)
    low = scale * (full * left[SLABS] - right[0])
    high = gain * scale * (full * right[0] - left[SLABS])
    carry = [left[j] + low * reach[j] for j in range(SLABS)]
    for j in range(SLABS):
        out_ref[j * ROWS : (j + 1) * ROWS, :WIDE] = (r * carry[j]).astype(BF16)
        if j < SLABS - 1:
            beyond = gain * (r * carry[j + 1] + right[j + 1]) + high * reach[SLABS - 1 - j]
        else:
            beyond = jnp.zeros_like(span)
        out_ref[j * ROWS : (j + 1) * ROWS, WIDE:] = beyond.astype(BF16)


def couple(table, r_local, ends):
    return call(
        couple_kernel,
        (1,),
        [whole(ROWS, 2 * NG), whole(NG, 2 * WIDE)],
        whole(NG, 2 * WIDE),
        jax.ShapeDtypeStruct((NG, 2 * WIDE), BF16),
    )(table, r_local, ends)


def spread_terms(terms, places):
    on = [place.astype(F32) for place in places]
    return [
        (1.0 - on[0]) * terms[0] + (1.0 - on[1]) * terms[1],
        on[0] * terms[0] + on[1] * terms[1],
    ]


def back_kernel(start, count, first, fresh, table, x_ref, s_ref, z_ref, sines_ref, r_ref, log_ref, p_ref, e_ref, *refs):
    refs = list(refs)
    if not first:
        u_in = refs.pop(0)
    if not fresh:
        refs = refs[2:]
    xo_ref, so_ref, zo_ref = (refs.pop(0) for _ in range(3))
    if start > 0:
        u_out = refs.pop(0)
    u_ref, both = refs
    step = pl.program_id(0)

    @pl.when(step == 0)
    def _():
        u_ref[...] = e_ref[:, WIDE:].astype(F32) if first else u_in[...]

    core = table[CORE]
    low_core = core == 0
    sines = sines_ref[...]
    kept = {}
    for half in (1, 0):
        for band in range(2):
            both[0, band] = x_ref[band, half]
            both[1, band] = unpacked(z_ref, band, half).astype(BF16)
        depth = (2 * (start + count - 1 - step) + half).astype(F32)
        carried = twice(jnp.exp2(depth * log_ref[...])) * e_ref[:, :WIDE].astype(F32)
        u = twice(r_ref[...]) * (p_ref[half].astype(F32) + u_ref[...] + carried)
        u_ref[...] = u
        section = jnp.dot(sines, u.astype(BF16), preferred_element_type=F32).astype(BF16)
        section = jnp.concatenate([section[:, q * NG : (q + 1) * NG] for q in range(PAIRS)], axis=0)
        potential = jnp.dot(section, sines, preferred_element_type=F32)
        v = [potential[q * NG : (q + 1) * NG] for q in range(PAIRS)]
        f = [both[core, q].astype(F32) for q in range(2)]
        s = [s_ref[table[SWAP_BAND + q], half].astype(F32) for q in range(2)]
        t = [both[1 - core, table[THIRD_BAND + q]].astype(F32) for q in range(2)]
        own = [v[q] * s[q] + v[2 + q] * t[q] for q in range(2)]
        swap = spread_terms([v[q] * f[q] for q in range(2)], [table[SWAP_BAND + q] for q in range(2)])
        third = spread_terms([v[2 + q] * f[q] for q in range(2)], [table[THIRD_BAND + q] for q in range(2)])
        for j in range(2):
            xo_ref[j, half] = jnp.where(low_core, own[j], third[j]).astype(BF16)
            so_ref[j, half] = swap[j].astype(BF16)
            kept[j, half] = jnp.where(low_core, third[j], own[j])
    for j in range(2):
        pack_into(zo_ref, j, kept[j, 0], kept[j, 1])

    if start > 0:

        @pl.when(step == count - 1)
        def _():
            u_out[...] = u_ref[...]


def back(table, x, s, z, z_start, sines, r, log_r, p, edges, u, sums, base, size, start, count):
    first, fresh = u is None, sums is None
    at = lambda i: start + count - 1 - i
    in_sums = lambda i: at(i) - base
    outs = call(
        functools.partial(back_kernel, start, count, first, fresh),
        (count,),
        [
            planes(at),
            planes(at),
            packed(lambda i: at(i) - z_start),
            whole(NG, NG),
            whole(NG, 2 * NG),
            whole(NG, 2 * NG),
            spectra(at),
            whole(NG, 2 * WIDE),
        ]
        + ([] if first else [whole(NG, WIDE)])
        + ([] if fresh else [ANY, ANY]),
        [planes(in_sums), planes(in_sums), packed(lambda i: count - 1 - i)] + ([whole(NG, WIDE)] if start > 0 else []),
        [jax.ShapeDtypeStruct((2, 2 * size, NG, NG), BF16)] * 2
        + [jax.ShapeDtypeStruct((2, count, 3, NG, 128), BF16)]
        + ([STATE] if start > 0 else []),
        scratch=[pltpu.VMEM((NG, WIDE), F32), pltpu.VMEM((2, 2, NG, NG), BF16)],
        aliases={} if fresh else {10 - first: 0, 11 - first: 1},
        cost=0,
    )(table, x, s, z, sines, r, log_r, p, edges, *(() if first else (u,)), *(() if fresh else sums))
    return outs[:2], outs[2], outs[3] if start > 0 else None


def close_kernel(scale, table, x_ref, s_ref, z_ref, *refs):
    for half in range(2):
        for band in range(2):
            total = x_ref[band, half].astype(F32) + s_ref[band, half].astype(F32) + unpacked(z_ref, band, half)
            refs[-1][band, half] = (scale * total).astype(BF16)


def close(scale, table, xo, so, zo, out, base, start, count):
    from_sums = planes(lambda i: start - base + i)
    more = [] if out is None else [out]
    return call(
        functools.partial(close_kernel, scale),
        (count,),
        [from_sums, from_sums, packed(lambda i: i)] + [ANY] * len(more),
        planes(lambda i: start + i),
        jax.ShapeDtypeStruct((2, ROWS, NG, NG), BF16),
        aliases={4: 0} if more else {},
    )(table, xo, so, zo, *more)


def placed(pieces):
    return [(sum(pieces[:k]), pieces[k]) for k in range(len(pieces))]


def shards(orbitals, plan):
    groups = lax.axis_size("band")
    core = lax.axis_index("band") % 2
    place = lax.axis_index("grid")
    moved = lambda step: [(g, step(g) % groups) for g in range(groups)]
    out_way = moved(lambda g: g - 2 if g % 2 == 0 else g + 2)
    home_way = moved(lambda g: g + 2 if g % 2 == 0 else g - 2)
    across = moved(lambda g: g + 1 if g % 2 == 0 else g - 1)
    exchange = lambda block: lax.all_to_all(block, "grid", split_axis=0, concat_axis=0, tiled=True)

    plan_left = lax.ppermute(plan, "band", moved(lambda g: g + 2))
    swapped = lax.ppermute(orbitals, "band", across)
    table = jnp.concatenate(
        [jnp.where(core == 0, plan, plan_left).reshape(-1), core[None].astype(jnp.int32)]
    )
    arrived = [
        (start, count, lax.ppermute(pack(plan[0], orbitals, start, count), "band", out_way))
        for start, count in placed(PIECES_IN)
    ]

    sines = sine_table()
    modes = jnp.arange(1, NG + 1, dtype=F32)
    root = decay(modes, modes)
    log_root = jnp.log2(root)
    local_modes = (place * ROWS + jnp.arange(1, ROWS + 1, dtype=jnp.int32)).astype(F32)
    root_local = decay(local_modes, modes)

    carried = None
    for start, count, z in arrived:
        carried = forward(table, orbitals, swapped, z, sines, root, log_root, carried, start, count)
    held, ends = carried
    edges = exchange(couple(table, root_local, exchange(ends)))

    scale = -((2.0 / (NG + 1)) ** 2)
    u, parts = None, []
    for start, count in reversed(placed(PIECES_OUT)):
        if len(parts) == 2:
            (so, zo), u = lax.optimization_barrier((parts[0][1:3], u))
            parts[0] = (parts[0][0], so, zo, *parts[0][3:])
        z_start, z = [(at, z) for at, many, z in arrived if at <= start and start + count <= at + many][0]
        (xo, so), zo, u = back(
            table, orbitals, swapped, z, z_start, sines, root, log_root, held, edges, u, None, start, count, start, count
        )
        parts.append((xo, lax.ppermute(so, "band", across), lax.ppermute(zo, "band", home_way), start, count))
    out = None
    for xo, so, zo, start, count in parts:
        out = close(scale, table, xo, so, zo, out, start, start, count)
    return out


def solution(mesh):
    return jax.shard_map(
        shards,
        mesh=mesh,
        in_specs=(P("band", "grid", None, None), P(None, "band")),
        out_specs=P("band", "grid", None, None),
        check_vma=False,
    )
```

time: 640 us -> 157 us (0.25)
  waiting for transfers between devices: 362 us -> 43.9 us
  matrix products: 99.4 us -> 0 us
  starting transfers between devices: 87.4 us -> 21.7 us
  Pallas kernels: 0 us -> 61.7 us
  local copies, waits for them, and re-layouts: 71.8 us -> 14.5 us
  blocking collectives: 0 us -> 12.3 us
  other arithmetic: 13.4 us -> 1.41 us
    ppermute x4 -> x13, waiting for transfers between devices: 266 us -> 35.1 us  [the longest x1 27.8 us: shards(): plan_left = lax.ppermute(plan, 'band', moved(lambda g: g + 2))]
    dot_general x10 -> x0, matrix products: 99.4 us -> none  [the longest x2 25.2 us: shards(): potential = jnp.dot(planes, sines, preferred_element_type=jnp.float32)]
    all_to_all x4 -> x1, waiting for transfers between devices: 96 us -> 8.8 us  [shards(): lax.all_to_all(block, 'grid', split_axis=0, concat_axis=0, tiled=True)]
    pallas_call x0 -> x15, Pallas kernels: none -> 61.7 us  [the longest x4 25.6 us: back(): call(functools.partial(back_kernel, start, count, first, fresh), (count,)...]
    ppermute x4 -> x13, starting transfers between devices: 63.7 us -> 15.3 us  [the longest x4 8.67 us: shards(): lax.ppermute(zo, 'band', home_way)]
    convert_element_type x4 -> x0, local copies, waits for them, and re-layouts: 28.7 us -> none  [the longest x2 14.4 us: shards(): section = jnp.einsum('pxyz,ky->pxkz', section, sines, preferred_element_t...]
    all_to_all x4 -> x0, local copies, waits for them, and re-layouts: 22.5 us -> none  [the longest x2 12.3 us: shards(): lax.all_to_all(section, 'grid', split_axis=2, concat_axis=1, tiled=True)]
    all_to_all x4 -> x1, starting transfers between devices: 23.7 us -> 6.36 us  [shards(): lax.all_to_all(block, 'grid', split_axis=0, concat_axis=0, tiled=True)]
  transfers between devices with their start and end apart: 8 -> 14, of which waited for: 8 -> 4; matrix products, arithmetic and copies ran while one was open for 18% -> 1% of each run, Pallas kernels for 0% -> 32%
where the time goes in v1:
time: 157 us; the launch traced here: 156 us
  Pallas kernels  61.7 us (39%)
  waiting for transfers between devices  43.9 us (28%)
  starting transfers between devices  21.7 us (14%)
  local copies, waits for them, and re-layouts  14.5 us (9%)
  blocking collectives  12.3 us (8%)
    ppermute x1, waiting for transfers between devices, shards(): plan_left = lax.ppermute(plan, 'band', moved(lambda g: g + 2))  27.8 us
    pallas_call x4, Pallas kernels, back(): call(functools.partial(back_kernel, start, count, first, fresh), (count,)...  25.6 us
    pallas_call x3, Pallas kernels, forward(): call(functools.partial(forward_kernel, start, first, last), (count,), [pl...  18.4 us
    unnamed x22, local copies, waits for them, and re-layouts  13.7 us
    all_to_all x1, blocking collectives, shards(): lax.all_to_all(block, 'grid', split_axis=0, concat_axis=0, tiled=True)  12.3 us
    pallas_call x4, Pallas kernels, close(): call(functools.partial(close_kernel, scale), (count,), [from_sums, from_s...  9.6 us
    all_to_all x1, waiting for transfers between devices, shards(): lax.all_to_all(block, 'grid', split_axis=0, concat_axis=0, tiled=True)  8.8 us
    ppermute x4, starting transfers between devices, shards(): lax.ppermute(zo, 'band', home_way)  8.67 us
  transfers between devices with their start and end apart: 14, of which 4 were waited for; matrix products, arithmetic and copies ran while one was open for 1% of the time, Pallas kernels for 32%

profile of v1, /device:TPU:1, one launch (start us, length us, event | category | flops | bytes accessed | tf_op | source)
XLA Modules:
  0.0 155.8 jit_solution(12398733495481671403)
XLA Ops:
  2.1 2.3 %copy-done = bf16[2,24,192,192]{3,2,1,0:T(8,128)(2,1)S(1)} copy-done((bf16[2,24,192,192]{3,2,1,0:T(8,128)(2,1)S(1)}, bf16[2,24,192,192]{3,2,1,0:T(8,128)(2,1)}, u32[]{:S(2)}) %copy-start) | copy-done | bytes 3538968
  4.4 3.2 %shard_map.28 = bf16[2,6,3,192,128]{4,3,2,1,0:T(8,128)(2,1)} custom-call(s32[2]{0:T(128)S(1)} %slice_bitcast_fusion.table, bf16[2,24,192,192]{3,2,1,0:T(8,128)(2,1)S(1)} %copy-done), custom_call_target="tpu_custom_call" | custom-call | tf_op jit(solution)/shard_map/pallas_call | solution.py:101
  9.4 2.4 %shard_map.30 = bf16[2,4,3,192,128]{4,3,2,1,0:T(8,128)(2,1)} custom-call(s32[2]{0:T(128)S(1)} %slice_bitcast_fusion.table, bf16[2,24,192,192]{3,2,1,0:T(8,128)(2,1)S(1)} %copy-done), custom_call_target="tpu_custom_call" | custom-call | tf_op jit(solution)/shard_map/pallas_call | solution.py:101
  17.6 27.8 %collective-permute-done = s32[2,2]{1,0:T(2,128)S(1)} collective-permute-done((s32[2,2]{1,0:T(2,128)S(1)}, s32[2,2]{1,0:T(2,128)S(1)}, u32[]{:S(2)}, u32[]{:S(2)}) %collective-permute-start) | collective-permute-done | bytes 48 | tf_op jit(solution)/shard_map/ppermute | solution.py:331
  45.6 2.3 %copy-done.1 = bf16[2,24,192,192]{3,2,1,0:T(8,128)(2,1)S(1)} copy-done((bf16[2,24,192,192]{3,2,1,0:T(8,128)(2,1)S(1)}, bf16[2,24,192,192]{3,2,1,0:T(8,128)(2,1)}, u32[]{:S(2)}) %copy-start.1) | copy-done | bytes 3538968
  47.9 8.4 %shard_map.31 = (bf16[24,192,768]{2,1,0:T(8,128)(2,1)S(1)}, f32[192,768]{1,0:T(8,128)S(1)}, f32[192,768]{1,0:T(8,128)S(1)}) custom-call(s32[5]{0:T(128)S(1)} %pad_add_fusion.table, bf16[2,24,192,192]{3,2,1,0:T(8,128)(2,1)S(1)} %copy-done.1, bf16[2,24,192,192]{3,2,1,0:T(8,128)(2,1)} %collective-permute-done.1.s_ref, ...), custom_call_target="tpu_custom_call" | custom-call | tf_op jit(solution)/shard_map/pallas_call | solution.py:154
  56.3 6.2 %shard_map.32 = (bf16[24,192,768]{2,1,0:T(8,128)(2,1)S(1)}, f32[192,768]{1,0:T(8,128)S(1)}, f32[192,768]{1,0:T(8,128)S(1)}) custom-call(s32[5]{0:T(128)S(1)} %pad_add_fusion.table, bf16[2,24,192,192]{3,2,1,0:T(8,128)(2,1)S(1)} %copy-done.1, bf16[2,24,192,192]{3,2,1,0:T(8,128)(2,1)} %collective-permute-done.1.s_ref, ...), custom_call_target="tpu_custom_call", output_to_operand_aliasing={{0}: (9, {})} | custom-call | tf_op jit(solution)/shard_map/pallas_call | solution.py:154
  62.5 3.9 %shard_map.33 = (bf16[24,192,768]{2,1,0:T(8,128)(2,1)S(1)}, bf16[192,1536]{1,0:T(8,128)(2,1)S(1)}) custom-call(s32[5]{0:T(128)S(1)} %pad_add_fusion.table, bf16[2,24,192,192]{3,2,1,0:T(8,128)(2,1)S(1)} %copy-done.1, bf16[2,24,192,192]{3,2,1,0:T(8,128)(2,1)} %collective-permute-done.1.s_ref, ...), custom_call_target="tpu_custom_call", output_to_operand_aliasing={{0}: (9, {})} | custom-call | tf_op jit(solution)/shard_map/pallas_call | solution.py:154
  66.4 2.9 %copy-done.3 = bf16[24,192,768]{2,1,0:T(8,128)(2,1)} copy-done((bf16[24,192,768]{2,1,0:T(8,128)(2,1)}, bf16[24,192,768]{2,1,0:T(8,128)(2,1)S(1)}, u32[]{:S(2)}) %copy-start.3) | copy-done | bytes 7077912
  70.1 6.4 %all-to-all-start = ((bf16[8,24,1536]{2,1,0:T(8,128)(2,1)}), bf16[8,24,1536]{2,1,0:T(8,128)(2,1)S(1)}, u32[]{:S(2)}, u32[]{:S(2)}) async-start(bf16[8,24,1536]{2,1,0:T(8,128)(2,1)} %bitcast.15), calls=%async_computation | async-start | bytes 1179648 | tf_op jit(solution)/shard_map/all_to_all | solution.py:329
  76.7 8.8 %all-to-all-done = bf16[8,24,1536]{2,1,0:T(8,128)(2,1)S(1)} async-done(((bf16[8,24,1536]{2,1,0:T(8,128)(2,1)}), bf16[8,24,1536]{2,1,0:T(8,128)(2,1)S(1)}, u32[]{:S(2)}, u32[]{:S(2)}) %all-to-all-start) | async-done | bytes 589856 | tf_op jit(solution)/shard_map/all_to_all | solution.py:329
  86.3 12.3 %all_to_all.22 = bf16[8,24,1536]{2,1,0:T(8,128)(2,1)S(1)} all-to-all(bf16[8,24,1536]{2,1,0:T(8,128)(2,1)S(1)} %bitcast.14), channel_id=1, replica_groups=mesh['band'=16,'grid'=8] {'grid'}, dimensions={0} | all-to-all | bytes 1179648 | tf_op jit(solution)/shard_map/all_to_all | solution.py:329
  98.7 2.3 %copy-done.2 = bf16[2,24,192,192]{3,2,1,0:T(8,128)(2,1)S(1)} copy-done((bf16[2,24,192,192]{3,2,1,0:T(8,128)(2,1)S(1)}, bf16[2,24,192,192]{3,2,1,0:T(8,128)(2,1)}, u32[]{:S(2)}) %copy-start.2) | copy-done | bytes 3538968
  101.0 3.0 %copy-done.4 = bf16[24,192,768]{2,1,0:T(8,128)(2,1)S(1)} copy-done((bf16[24,192,768]{2,1,0:T(8,128)(2,1)S(1)}, bf16[24,192,768]{2,1,0:T(8,128)(2,1)}, u32[]{:S(2)}) %copy-start.4) | copy-done | bytes 7077912
  104.0 4.7 %shard_map.35 = (bf16[2,4,192,192]{3,2,1,0:T(8,128)(2,1)S(1)}, bf16[2,4,192,192]{3,2,1,0:T(8,128)(2,1)S(1)}, bf16[2,2,3,192,128]{4,3,2,1,0:T(8,128)(2,1)S(1)}, f32[192,768]{1,0:T(8,128)S(1)}) custom-call(s32[5]{0:T(128)S(1)} %pad_add_fusion.table, bf16[2,24,192,192]{3,2,1,0:T(8,128)(2,1)S(1)} %copy-done.2, ...), custom_call_target="tpu_custom_call" | custom-call | tf_op jit(solution)/shard_map/pallas_call | solution.py:271
  109.8 8.3 %shard_map.36 = (bf16[2,8,192,192]{3,2,1,0:T(8,128)(2,1)S(1)}, bf16[2,8,192,192]{3,2,1,0:T(8,128)(2,1)S(1)}, bf16[2,4,3,192,128]{4,3,2,1,0:T(8,128)(2,1)S(1)}, f32[192,768]{1,0:T(8,128)S(1)}) custom-call(s32[5]{0:T(128)S(1)} %pad_add_fusion.table, bf16[2,24,192,192]{3,2,1,0:T(8,128)(2,1)S(1)} %copy-done.2, ...), custom_call_target="tpu_custom_call" | custom-call | tf_op jit(solution)/shard_map/pallas_call | solution.py:271
  118.4 3.4 %collective-permute-start.12 = (bf16[2,4,3,192,128]{4,3,2,1,0:T(8,128)(2,1)S(1)}, bf16[2,4,3,192,128]{4,3,2,1,0:T(8,128)(2,1)S(1)}, u32[]{:S(2)}, u32[]{:S(2)}) collective-permute-start(bf16[2,4,3,192,128]{4,3,2,1,0:T(8,128)(2,1)S(1)} %get-tuple-element.53), channel_id=1, source_target_pairs={{0,16},{8,120},{16,32},{24,8},{32,48},{40,24},{48,64},{56,40},{64,... | collective-permute-start | bytes 3538952 | tf_op jit(solution)/shard_map/ppermute | solution.py:364
  121.8 7.9 %shard_map.37 = (bf16[2,8,192,192]{3,2,1,0:T(8,128)(2,1)S(1)}, bf16[2,8,192,192]{3,2,1,0:T(8,128)(2,1)S(1)}, bf16[2,4,3,192,128]{4,3,2,1,0:T(8,128)(2,1)S(1)}, f32[192,768]{1,0:T(8,128)S(1)}) custom-call(s32[5]{0:T(128)S(1)} %pad_add_fusion.table, bf16[2,24,192,192]{3,2,1,0:T(8,128)(2,1)S(1)} %copy-done.2, ...), custom_call_target="tpu_custom_call" | custom-call | tf_op jit(solution)/shard_map/pallas_call | solution.py:271
  130.8 4.7 %shard_map.38 = (bf16[2,4,192,192]{3,2,1,0:T(8,128)(2,1)S(1)}, bf16[2,4,192,192]{3,2,1,0:T(8,128)(2,1)S(1)}, bf16[2,2,3,192,128]{4,3,2,1,0:T(8,128)(2,1)S(1)}) custom-call(s32[5]{0:T(128)S(1)} %pad_add_fusion.table, bf16[2,24,192,192]{3,2,1,0:T(8,128)(2,1)S(1)} %copy-done.2, bf16[2,24,192,192]{3,2,1,0:T(8,128)(2,1)} %collective-permute-done.1.s_ref, ...), custom_call_target="tpu_custom_call" | custom-call | tf_op jit(solution)/shard_map/pallas_call | solution.py:271
  135.6 3.4 %collective-permute-start.8 = (bf16[2,2,3,192,128]{4,3,2,1,0:T(8,128)(2,1)S(1)}, bf16[2,2,3,192,128]{4,3,2,1,0:T(8,128)(2,1)S(1)}, u32[]{:S(2)}, u32[]{:S(2)}) collective-permute-start(bf16[2,2,3,192,128]{4,3,2,1,0:T(8,128)(2,1)S(1)} %get-tuple-element.47), channel_id=1, source_target_pairs={{0,16},{8,120},{16,32},{24,8},{32,48},{40,24},{48,64},{56,40},{64,... | collective-permute-start | bytes 1769480 | tf_op jit(solution)/shard_map/ppermute | solution.py:364
  140.9 2.9 %shard_map.40.refs_0_ = bf16[2,24,192,192]{3,2,1,0:T(8,128)(2,1)} custom-call(s32[5]{0:T(128)S(1)} %pad_add_fusion.table, bf16[2,8,192,192]{3,2,1,0:T(8,128)(2,1)S(1)} %get-tuple-element.51.x_ref, bf16[2,8,192,192]{3,2,1,0:T(8,128)(2,1)S(1)} %collective-permute-done.11.s_ref, ...), custom_call_target="tpu_custom_call", output_to_operand_aliasing={{}: (4, {})} | custom-call | tf_op jit(solution)/shard_map/pallas_call | solution.py:307
  143.8 3.8 %collective-permute-done.10.z_ref = bf16[2,4,3,192,128]{4,3,2,1,0:T(8,128)(2,1)S(1)} collective-permute-done((bf16[2,4,3,192,128]{4,3,2,1,0:T(8,128)(2,1)S(1)}, bf16[2,4,3,192,128]{4,3,2,1,0:T(8,128)(2,1)S(1)}, u32[]{:S(2)}, u32[]{:S(2)}) %collective-permute-start.10) | collective-permute-done | bytes 1179680 | tf_op jit(solution)/shard_map/ppermute | solution.py:364
  147.6 2.9 %shard_map.41.refs_0_ = bf16[2,24,192,192]{3,2,1,0:T(8,128)(2,1)} custom-call(s32[5]{0:T(128)S(1)} %pad_add_fusion.table, bf16[2,8,192,192]{3,2,1,0:T(8,128)(2,1)S(1)} %get-tuple-element.48.x_ref, bf16[2,8,192,192]{3,2,1,0:T(8,128)(2,1)S(1)} %collective-permute-done.9.s_ref, ...), custom_call_target="tpu_custom_call", output_to_operand_aliasing={{}: (4, {})} | custom-call | tf_op jit(solution)/shard_map/pallas_call | solution.py:307
  150.5 3.4 %collective-permute-done.8.z_ref = bf16[2,2,3,192,128]{4,3,2,1,0:T(8,128)(2,1)S(1)} collective-permute-done((bf16[2,2,3,192,128]{4,3,2,1,0:T(8,128)(2,1)S(1)}, bf16[2,2,3,192,128]{4,3,2,1,0:T(8,128)(2,1)S(1)}, u32[]{:S(2)}, u32[]{:S(2)}) %collective-permute-start.8) | collective-permute-done | bytes 589856 | tf_op jit(solution)/shard_map/ppermute | solution.py:364
  (55 shorter events, 17.8 us)
Async XLA Ops:
  0.0 45.6 %collective-permute-start.1 = (bf16[2,24,192,192]{3,2,1,0:T(8,128)(2,1)}, bf16[2,24,192,192]{3,2,1,0:T(8,128)(2,1)}, u32[]{:S(2)}, u32[]{:S(2)}) collective-permute-start(bf16[2,24,192,192]{3,2,1,0:T(8,128)(2,1)} %x_ref.19), channel_id=1, source_target_pairs={{0,8},{8,0},{16,24},{24,16},{32,40},{40,32},{48,56},{56,48},{64,72... | collective-permute-start | bytes 10616840 | tf_op jit(solution)/shard_map/ppermute | solution.py:332
  2.1 2.3 %copy-start = (bf16[2,24,192,192]{3,2,1,0:T(8,128)(2,1)S(1)}, bf16[2,24,192,192]{3,2,1,0:T(8,128)(2,1)}, u32[]{:S(2)}) copy-start(bf16[2,24,192,192]{3,2,1,0:T(8,128)(2,1)} %x_ref.19) | copy-start | bytes 10616836
  7.7 5.8 %copy-start.8 = (s32[2,2]{1,0:T(2,128)S(1)}, s32[2,2]{1,0:T(2,128)}, u32[]{:S(2)}) copy-start(s32[2,2]{1,0:T(2,128)} %param.3) | copy-start | bytes 52
  7.7 37.9 %collective-permute-start.2 = (bf16[2,6,3,192,128]{4,3,2,1,0:T(8,128)(2,1)}, bf16[2,6,3,192,128]{4,3,2,1,0:T(8,128)(2,1)S(1)}, u32[]{:S(2)}, u32[]{:S(2)}) collective-permute-start(bf16[2,6,3,192,128]{4,3,2,1,0:T(8,128)(2,1)} %shard_map.28), channel_id=1, source_target_pairs={{0,112},{8,24},{16,0},{24,40},{32,16},{40,56},{48,32},{56,72},{64,... | collective-permute-start | bytes 5308424 | tf_op jit(solution)/shard_map/ppermute | solution.py:337
  11.8 44.5 %collective-permute-start.4 = (bf16[2,4,3,192,128]{4,3,2,1,0:T(8,128)(2,1)}, bf16[2,4,3,192,128]{4,3,2,1,0:T(8,128)(2,1)}, u32[]{:S(2)}, u32[]{:S(2)}) collective-permute-start(bf16[2,4,3,192,128]{4,3,2,1,0:T(8,128)(2,1)} %shard_map.30), channel_id=1, source_target_pairs={{0,112},{8,24},{16,0},{24,40},{32,16},{40,56},{48,32},{56,72},{64,... | collective-permute-start | bytes 3538952 | tf_op jit(solution)/shard_map/ppermute | solution.py:337
  13.5 31.9 %collective-permute-start = (s32[2,2]{1,0:T(2,128)S(1)}, s32[2,2]{1,0:T(2,128)S(1)}, u32[]{:S(2)}, u32[]{:S(2)}) collective-permute-start(s32[2,2]{1,0:T(2,128)S(1)} %copy-done.8), channel_id=1, source_target_pairs={{0,16},{8,24},{16,32},{24,40},{32,48},{40,56},{48,64},{56,72},{64,... | collective-permute-start | bytes 56 | tf_op jit(solution)/shard_map/ppermute | solution.py:331
  16.4 46.1 %collective-permute-start.3 = (bf16[2,2,3,192,128]{4,3,2,1,0:T(8,128)(2,1)}, bf16[2,2,3,192,128]{4,3,2,1,0:T(8,128)(2,1)S(1)}, u32[]{:S(2)}, u32[]{:S(2)}) collective-permute-start(bf16[2,2,3,192,128]{4,3,2,1,0:T(8,128)(2,1)} %shard_map.29), channel_id=1, source_target_pairs={{0,112},{8,24},{16,0},{24,40},{32,16},{40,56},{48,32},{56,72},{64,... | collective-permute-start | bytes 1769480 | tf_op jit(solution)/shard_map/ppermute | solution.py:337
  45.6 2.3 %copy-start.1 = (bf16[2,24,192,192]{3,2,1,0:T(8,128)(2,1)S(1)}, bf16[2,24,192,192]{3,2,1,0:T(8,128)(2,1)}, u32[]{:S(2)}) copy-start(bf16[2,24,192,192]{3,2,1,0:T(8,128)(2,1)} %x_ref.19) | copy-start | bytes 10616836
  62.5 3.9 %copy-start.5 = (bf16[2,2,3,192,128]{4,3,2,1,0:T(8,128)(2,1)}, bf16[2,2,3,192,128]{4,3,2,1,0:T(8,128)(2,1)S(1)}, u32[]{:S(2)}) copy-start(bf16[2,2,3,192,128]{4,3,2,1,0:T(8,128)(2,1)S(1)} %collective-permute-done.3.z_ref) | copy-start | bytes 1769476
  66.4 2.9 %copy-start.3 = (bf16[24,192,768]{2,1,0:T(8,128)(2,1)}, bf16[24,192,768]{2,1,0:T(8,128)(2,1)S(1)}, u32[]{:S(2)}) copy-start(bf16[24,192,768]{2,1,0:T(8,128)(2,1)S(1)} %get-tuple-element.37.p_ref) | copy-start | bytes 21233668
  70.1 15.4 %all-to-all-start = ((bf16[8,24,1536]{2,1,0:T(8,128)(2,1)}), bf16[8,24,1536]{2,1,0:T(8,128)(2,1)S(1)}, u32[]{:S(2)}, u32[]{:S(2)}) async-start(bf16[8,24,1536]{2,1,0:T(8,128)(2,1)} %bitcast.15), calls=%async_computation | async-start | bytes 1179648 | tf_op jit(solution)/shard_map/all_to_all | solution.py:329
  85.5 13.2 %copy-start.6 = (bf16[2,2,3,192,128]{4,3,2,1,0:T(8,128)(2,1)S(1)}, bf16[2,2,3,192,128]{4,3,2,1,0:T(8,128)(2,1)}, u32[]{:S(2)}) copy-start(bf16[2,2,3,192,128]{4,3,2,1,0:T(8,128)(2,1)} %copy-done.5) | copy-start | bytes 1769476
  98.7 2.3 %copy-start.2 = (bf16[2,24,192,192]{3,2,1,0:T(8,128)(2,1)S(1)}, bf16[2,24,192,192]{3,2,1,0:T(8,128)(2,1)}, u32[]{:S(2)}) copy-start(bf16[2,24,192,192]{3,2,1,0:T(8,128)(2,1)} %x_ref.19) | copy-start | bytes 10616836
  101.0 3.0 %copy-start.4 = (bf16[24,192,768]{2,1,0:T(8,128)(2,1)S(1)}, bf16[24,192,768]{2,1,0:T(8,128)(2,1)}, u32[]{:S(2)}) copy-start(bf16[24,192,768]{2,1,0:T(8,128)(2,1)} %copy-done.3) | copy-start | bytes 21233668
  108.8 13.0 %collective-permute-start.5 = (bf16[2,4,192,192]{3,2,1,0:T(8,128)(2,1)S(1)}, bf16[2,4,192,192]{3,2,1,0:T(8,128)(2,1)S(1)}, u32[]{:S(2)}, u32[]{:S(2)}) collective-permute-start(bf16[2,4,192,192]{3,2,1,0:T(8,128)(2,1)S(1)} %get-tuple-element.39), channel_id=1, source_target_pairs={{0,8},{8,0},{16,24},{24,16},{32,40},{40,32},{48,56},{56,48},{64,72... | collective-permute-start | bytes 1769480 | tf_op jit(solution)/shard_map/ppermute | solution.py:364
  108.9 12.9 %collective-permute-start.6 = (bf16[2,2,3,192,128]{4,3,2,1,0:T(8,128)(2,1)S(1)}, bf16[2,2,3,192,128]{4,3,2,1,0:T(8,128)(2,1)S(1)}, u32[]{:S(2)}, u32[]{:S(2)}) collective-permute-start(bf16[2,2,3,192,128]{4,3,2,1,0:T(8,128)(2,1)S(1)} %get-tuple-element.40), channel_id=1, source_target_pairs={{0,16},{8,120},{16,32},{24,8},{32,48},{40,24},{48,64},{56,40},{64,... | collective-permute-start | bytes 1769480 | tf_op jit(solution)/shard_map/ppermute | solution.py:364
  109.8 12.0 %slice-start = ((s8[7077888]{0:T(1024)(128)(4,1)}), s8[4194304]{0:T(1024)(128)(4,1)S(1)}, s32[]{:S(2)}) async-start(s8[7077888]{0:T(1024)(128)(4,1)} %bitcast.7), calls=%async_computation.2 | async-start | bytes 8388608
  109.8 12.0 %slice-start.1 = ((s8[7077888]{0:T(1024)(128)(4,1)}), s8[2883584]{0:T(1024)(128)(4,1)S(1)}, s32[]{:S(2)}) async-start(s8[7077888]{0:T(1024)(128)(4,1)} %bitcast.7), calls=%async_computation.3 | async-start | bytes 5767168
  118.1 17.5 %collective-permute-start.11 = (bf16[2,8,192,192]{3,2,1,0:T(8,128)(2,1)S(1)}, bf16[2,8,192,192]{3,2,1,0:T(8,128)(2,1)S(1)}, u32[]{:S(2)}, u32[]{:S(2)}) collective-permute-start(bf16[2,8,192,192]{3,2,1,0:T(8,128)(2,1)S(1)} %get-tuple-element.52), channel_id=1, source_target_pairs={{0,8},{8,0},{16,24},{24,16},{32,40},{40,32},{48,56},{56,48},{64,72... | collective-permute-start | bytes 3538952 | tf_op jit(solution)/shard_map/ppermute | solution.py:364
  118.4 22.5 %collective-permute-start.12 = (bf16[2,4,3,192,128]{4,3,2,1,0:T(8,128)(2,1)S(1)}, bf16[2,4,3,192,128]{4,3,2,1,0:T(8,128)(2,1)S(1)}, u32[]{:S(2)}, u32[]{:S(2)}) collective-permute-start(bf16[2,4,3,192,128]{4,3,2,1,0:T(8,128)(2,1)S(1)} %get-tuple-element.53), channel_id=1, source_target_pairs={{0,16},{8,120},{16,32},{24,8},{32,48},{40,24},{48,64},{56,40},{64,... | collective-permute-start | bytes 3538952 | tf_op jit(solution)/shard_map/ppermute | solution.py:364
  129.8 14.0 %collective-permute-start.9 = (bf16[2,8,192,192]{3,2,1,0:T(8,128)(2,1)S(1)}, bf16[2,8,192,192]{3,2,1,0:T(8,128)(2,1)S(1)}, u32[]{:S(2)}, u32[]{:S(2)}) collective-permute-start(bf16[2,8,192,192]{3,2,1,0:T(8,128)(2,1)S(1)} %get-tuple-element.49), channel_id=1, source_target_pairs={{0,8},{8,0},{16,24},{24,16},{32,40},{40,32},{48,56},{56,48},{64,72... | collective-permute-start | bytes 3538952 | tf_op jit(solution)/shard_map/ppermute | solution.py:364
  129.8 17.7 %collective-permute-start.10 = (bf16[2,4,3,192,128]{4,3,2,1,0:T(8,128)(2,1)S(1)}, bf16[2,4,3,192,128]{4,3,2,1,0:T(8,128)(2,1)S(1)}, u32[]{:S(2)}, u32[]{:S(2)}) collective-permute-start(bf16[2,4,3,192,128]{4,3,2,1,0:T(8,128)(2,1)S(1)} %get-tuple-element.50), channel_id=1, source_target_pairs={{0,16},{8,120},{16,32},{24,8},{32,48},{40,24},{48,64},{56,40},{64,... | collective-permute-start | bytes 3538952 | tf_op jit(solution)/shard_map/ppermute | solution.py:364
  135.5 15.0 %collective-permute-start.7 = (bf16[2,4,192,192]{3,2,1,0:T(8,128)(2,1)S(1)}, bf16[2,4,192,192]{3,2,1,0:T(8,128)(2,1)S(1)}, u32[]{:S(2)}, u32[]{:S(2)}) collective-permute-start(bf16[2,4,192,192]{3,2,1,0:T(8,128)(2,1)S(1)} %get-tuple-element.46), channel_id=1, source_target_pairs={{0,8},{8,0},{16,24},{24,16},{32,40},{40,32},{48,56},{56,48},{64,72... | collective-permute-start | bytes 1769480 | tf_op jit(solution)/shard_map/ppermute | solution.py:364
  135.6 18.3 %collective-permute-start.8 = (bf16[2,2,3,192,128]{4,3,2,1,0:T(8,128)(2,1)S(1)}, bf16[2,2,3,192,128]{4,3,2,1,0:T(8,128)(2,1)S(1)}, u32[]{:S(2)}, u32[]{:S(2)}) collective-permute-start(bf16[2,2,3,192,128]{4,3,2,1,0:T(8,128)(2,1)S(1)} %get-tuple-element.47), channel_id=1, source_target_pairs={{0,16},{8,120},{16,32},{24,8},{32,48},{40,24},{48,64},{56,40},{64,... | collective-permute-start | bytes 1769480 | tf_op jit(solution)/shard_map/ppermute | solution.py:364
  (1 other events, 0.8 us)

commit v2 on v1

--- a/solution.py
+++ b/solution.py
@@ -15,7 +15,8 @@
 WIDE = PAIRS * NG
 PAIRED = ROWS // 2
 PIECES_IN = (6, 4, 2)
-PIECES_OUT = (2, 4, 4, 2)
+PIECES_OUT = (1, 3, 5, 3)
+PACKED = 2
 
 F32 = jnp.float32
 BF16 = jnp.bfloat16
@@ -92,19 +93,28 @@
 STATE = jax.ShapeDtypeStruct((NG, WIDE), F32)
 
 
+def in_hbm(block):
+    return pltpu.with_memory_space_constraint(block, pltpu.HBM)
+
+
 def pack_kernel(table, x_ref, z_ref):
     for band in range(2):
-        pack_into(z_ref, band, x_ref[band, 0].astype(F32), x_ref[band, 1].astype(F32))
+        for pair in range(PACKED):
+            low, high = 2 * pair, 2 * pair + 1
+            z_ref[band, pair, 0] = x_ref[band, low, :, :128]
+            z_ref[band, pair, 1] = x_ref[band, high, :, :128]
+            tails = [x_ref[band, plane, :, 128:].astype(F32) for plane in (low, high)]
+            z_ref[band, pair, 2] = jnp.concatenate(tails, axis=1).astype(BF16)
 
 
 def pack(table, x, start, count):
     return call(
         pack_kernel,
-        (count,),
-        [planes(lambda i: start + i)],
-        packed(lambda i: i),
+        (count // PACKED,),
+        [pl.BlockSpec((2, 2 * PACKED, NG, NG), lambda i, table: (0, start // PACKED + i, 0, 0))],
+        pl.BlockSpec((2, PACKED, 3, NG, 128), lambda i, table: (0, i, 0, 0, 0)),
         jax.ShapeDtypeStruct((2, count, 3, NG, 128), BF16),
-    )(table, x)
+    )(table, in_hbm(x))
 
 
 def forward_kernel(start, first, last, table, x_ref, s_ref, z_ref, sines_ref, r_ref, log_ref, *refs):
@@ -157,8 +167,7 @@
         [planes(at), planes(at), packed(lambda i: i), whole(NG, NG), whole(NG, 2 * NG), whole(NG, 2 * NG)]
         + ([] if first else [whole(NG, WIDE), whole(NG, WIDE), ANY]),
         [spectra(at)] + ([whole(NG, 2 * WIDE)] if last else [whole(NG, WIDE)] * 2),
-        [jax.ShapeDtypeStruct((ROWS, NG, WIDE), BF16)]
-        + ([jax.ShapeDtypeStruct((NG, 2 * WIDE), BF16)] if last else [STATE] * 2),
+        [pltpu.HBM((ROWS, NG, WIDE), BF16)] + ([jax.ShapeDtypeStruct((NG, 2 * WIDE), BF16)] if last else [STATE] * 2),
         scratch=[pltpu.VMEM((NG, WIDE), F32)] * 2 + [pltpu.VMEM((2, 2, NG, NG), BF16)],
         aliases={} if first else {9: 0},
     )(table, x, s, z, sines, r, log_r, *(() if first else (carried[1], carried[2], carried[0])))
@@ -205,11 +214,9 @@
 
 
 def spread_terms(terms, places):
-    on = [place.astype(F32) for place in places]
-    return [
-        (1.0 - on[0]) * terms[0] + (1.0 - on[1]) * terms[1],
-        on[0] * terms[0] + on[1] * terms[1],
-    ]
+    apart = jnp.where(places[0] == places[1], 0.0, 1.0)
+    other = apart * terms[1]
+    return [terms[0] + (terms[1] - other), other]
 
 
 def back_kernel(start, count, first, fresh, table, x_ref, s_ref, z_ref, sines_ref, r_ref, log_ref, p_ref, e_ref, *refs):
@@ -250,12 +257,14 @@
         own = [v[q] * s[q] + v[2 + q] * t[q] for q in range(2)]
         swap = spread_terms([v[q] * f[q] for q in range(2)], [table[SWAP_BAND + q] for q in range(2)])
         third = spread_terms([v[2 + q] * f[q] for q in range(2)], [table[THIRD_BAND + q] for q in range(2)])
+        swap_at, third_at = table[SWAP_BAND], table[THIRD_BAND]
+        own_at, sent_at = jnp.where(low_core, 0, third_at), jnp.where(low_core, third_at, 0)
         for j in range(2):
-            xo_ref[j, half] = jnp.where(low_core, own[j], third[j]).astype(BF16)
-            so_ref[j, half] = swap[j].astype(BF16)
+            xo_ref[jnp.abs(own_at - j), half] = jnp.where(low_core, own[j], third[j]).astype(BF16)
+            so_ref[jnp.abs(swap_at - j), half] = swap[j].astype(BF16)
             kept[j, half] = jnp.where(low_core, third[j], own[j])
     for j in range(2):
-        pack_into(zo_ref, j, kept[j, 0], kept[j, 1])
+        pack_into(zo_ref, jnp.abs(sent_at - j), kept[j, 0], kept[j, 1])
 
     if start > 0:
 
@@ -290,7 +299,7 @@
         scratch=[pltpu.VMEM((NG, WIDE), F32), pltpu.VMEM((2, 2, NG, NG), BF16)],
         aliases={} if fresh else {10 - first: 0, 11 - first: 1},
         cost=0,
-    )(table, x, s, z, sines, r, log_r, p, edges, *(() if first else (u,)), *(() if fresh else sums))
+    )(table, *(in_hbm(block) for block in (x, s, z, sines, r, log_r, p, edges)), *(() if first else (u,)), *(() if fresh else sums))
     return outs[:2], outs[2], outs[3] if start > 0 else None
 
 
@@ -328,15 +337,15 @@
     across = moved(lambda g: g + 1 if g % 2 == 0 else g - 1)
     exchange = lambda block: lax.all_to_all(block, "grid", split_axis=0, concat_axis=0, tiled=True)
 
-    plan_left = lax.ppermute(plan, "band", moved(lambda g: g + 2))
     swapped = lax.ppermute(orbitals, "band", across)
+    plan_left = lax.ppermute(lax.ppermute(plan, "band", across), "band", moved(lambda g: g + 3 if g % 2 == 0 else g - 3))
     table = jnp.concatenate(
         [jnp.where(core == 0, plan, plan_left).reshape(-1), core[None].astype(jnp.int32)]
     )
-    arrived = [
-        (start, count, lax.ppermute(pack(plan[0], orbitals, start, count), "band", out_way))
-        for start, count in placed(PIECES_IN)
-    ]
+    arrived = []
+    for start, count in placed(PIECES_IN):
+        piece = pack(plan[0], orbitals, start, count)
+        arrived.append((start, count, lax.ppermute(piece, "band", out_way)))
 
     sines = sine_table()
     modes = jnp.arange(1, NG + 1, dtype=F32)
@@ -352,14 +361,15 @@
     edges = exchange(couple(table, root_local, exchange(ends)))
 
     scale = -((2.0 / (NG + 1)) ** 2)
+    joined = jnp.concatenate([z for _, _, z in arrived], axis=1)
     u, parts = None, []
     for start, count in reversed(placed(PIECES_OUT)):
         if len(parts) == 2:
-            (so, zo), u = lax.optimization_barrier((parts[0][1:3], u))
-            parts[0] = (parts[0][0], so, zo, *parts[0][3:])
-        z_start, z = [(at, z) for at, many, z in arrived if at <= start and start + count <= at + many][0]
+            xo, so, zo, *where = parts[-2]
+            so, zo, u = lax.optimization_barrier((so, zo, u))
+            parts[-2] = (xo, so, zo, *where)
         (xo, so), zo, u = back(
-            table, orbitals, swapped, z, z_start, sines, root, log_root, held, edges, u, None, start, count, start, count
+            table, orbitals, swapped, joined, 0, sines, root, log_root, held, edges, u, None, start, count, start, count
         )
         parts.append((xo, lax.ppermute(so, "band", across), lax.ppermute(zo, "band", home_way), start, count))
     out = None

time: 157 us -> 145 us (0.924)
  waiting for transfers between devices: 43.9 us -> 31.4 us
  blocking collectives: 12.3 us -> 0 us
  starting transfers between devices: 21.7 us -> 31.2 us
  Pallas kernels: 61.7 us -> 70.1 us
  local copies, waits for them, and re-layouts: 14.5 us -> 9.74 us
    ppermute x4 -> x5, waiting for transfers between devices: 27.8 us -> 12.1 us  [the longest x3 7.02 us: shards(): arrived.append((start, count, lax.ppermute(piece, 'band', out_way)))]
    all_to_all x1 -> x0, blocking collectives: 12.3 us -> none  [shards(): lax.all_to_all(block, 'grid', split_axis=0, concat_axis=0, tiled=True)]
    all_to_all x1 -> x2, waiting for transfers between devices: 8.8 us -> 16.8 us  [shards(): lax.all_to_all(block, 'grid', split_axis=0, concat_axis=0, tiled=True)]
    unnamed x22 -> x16, local copies, waits for them, and re-layouts: 13.7 us -> 8.06 us
    ppermute x4, waiting for transfers between devices: 7.2 us -> 2.51 us  [shards(): lax.ppermute(zo, 'band', home_way)]
    ppermute x4, starting transfers between devices: 0.52 us -> 4.88 us  [shards(): lax.ppermute(so, 'band', across)]
    all_to_all x1 -> x2, starting transfers between devices: 6.36 us -> 9.89 us  [shards(): lax.all_to_all(block, 'grid', split_axis=0, concat_axis=0, tiled=True)]
    pallas_call x3, Pallas kernels: 7.22 us -> 10 us  [pack(): call(pack_kernel, (count // PACKED,), [pl.BlockSpec((2, 2 * PACKED, NG, N...]
  transfers between devices with their start and end apart: 14 -> 16, of which waited for: 4 -> 8; matrix products, arithmetic and copies ran while one was open for 1% -> 5% of each run, Pallas kernels for 32% -> 39%
where the time goes in v2:
time: 145 us; the launch traced here: 144 us
  Pallas kernels  70.1 us (48%)
  waiting for transfers between devices  31.4 us (22%)
  starting transfers between devices  31.2 us (22%)
  local copies, waits for them, and re-layouts  9.74 us (7%)
    pallas_call x4, Pallas kernels, back(): call(functools.partial(back_kernel, start, count, first, fresh), (count,)...  26.9 us
    pallas_call x3, Pallas kernels, forward(): call(functools.partial(forward_kernel, start, first, last), (count,), [pl...  21.2 us
    all_to_all x2, waiting for transfers between devices, shards(): lax.all_to_all(block, 'grid', split_axis=0, concat_axis=0, tiled=True)  16.8 us
    pallas_call x4, Pallas kernels, close(): call(functools.partial(close_kernel, scale), (count,), [from_sums, from_s...  10.3 us
    pallas_call x3, Pallas kernels, pack(): call(pack_kernel, (count // PACKED,), [pl.BlockSpec((2, 2 * PACKED, NG, N...  10 us
    all_to_all x2, starting transfers between devices, shards(): lax.all_to_all(block, 'grid', split_axis=0, concat_axis=0, tiled=True)  9.89 us
    unnamed x16, local copies, waits for them, and re-layouts  8.06 us
    ppermute x4, starting transfers between devices, shards(): lax.ppermute(zo, 'band', home_way)  7.91 us
  transfers between devices with their start and end apart: 16, of which 8 were waited for; matrix products, arithmetic and copies ran while one was open for 5% of the time, Pallas kernels for 39%

profile of v2, /device:TPU:1, one launch (start us, length us, event | category | flops | bytes accessed | tf_op | source)
XLA Modules:
  0.0 144.0 jit_solution(8763535516800086822)
XLA Ops:
  2.1 4.5 %shard_map.28 = bf16[2,6,3,192,128]{4,3,2,1,0:T(8,128)(2,1)} custom-call(s32[2]{0:T(128)S(1)} %slice_bitcast_fusion.table, bf16[2,24,192,192]{3,2,1,0:T(8,128)(2,1)} %x_ref.19), custom_call_target="tpu_custom_call" | custom-call | tf_op jit(solution)/shard_map/pallas_call | solution.py:111
  8.3 2.9 %shard_map.29 = bf16[2,4,3,192,128]{4,3,2,1,0:T(8,128)(2,1)} custom-call(s32[2]{0:T(128)S(1)} %slice_bitcast_fusion.table, bf16[2,24,192,192]{3,2,1,0:T(8,128)(2,1)} %x_ref.19), custom_call_target="tpu_custom_call" | custom-call | tf_op jit(solution)/shard_map/pallas_call | solution.py:111
  12.9 2.2 %collective-permute-start = (s32[2,2]{1,0:T(2,128)S(1)}, s32[2,2]{1,0:T(2,128)S(1)}, u32[]{:S(2)}, u32[]{:S(2)}) collective-permute-start(s32[2,2]{1,0:T(2,128)S(1)} %copy-done.6), channel_id=1, source_target_pairs={{0,8},{8,0},{16,24},{24,16},{32,40},{40,32},{48,56},{56,48},{64,72... | collective-permute-start | bytes 56 | tf_op jit(solution)/shard_map/ppermute | solution.py:341
  15.0 2.6 %shard_map.30 = bf16[2,2,3,192,128]{4,3,2,1,0:T(8,128)(2,1)} custom-call(s32[2]{0:T(128)S(1)} %slice_bitcast_fusion.table, bf16[2,24,192,192]{3,2,1,0:T(8,128)(2,1)} %x_ref.19), custom_call_target="tpu_custom_call" | custom-call | tf_op jit(solution)/shard_map/pallas_call | solution.py:111
  20.4 5.0 %collective-permute-done.1 = s32[2,2]{1,0:T(2,128)S(1)} collective-permute-done((s32[2,2]{1,0:T(2,128)S(1)}, s32[2,2]{1,0:T(2,128)S(1)}, u32[]{:S(2)}, u32[]{:S(2)}) %collective-permute-start.1) | collective-permute-done | bytes 48 | tf_op jit(solution)/shard_map/ppermute | solution.py:341
  25.6 5.9 %collective-permute-done.3.z_ref = bf16[2,6,3,192,128]{4,3,2,1,0:T(8,128)(2,1)S(1)} collective-permute-done((bf16[2,6,3,192,128]{4,3,2,1,0:T(8,128)(2,1)}, bf16[2,6,3,192,128]{4,3,2,1,0:T(8,128)(2,1)S(1)}, u32[]{:S(2)}, u32[]{:S(2)}) %collective-permute-start.3) | collective-permute-done | bytes 1769504 | tf_op jit(solution)/shard_map/ppermute | solution.py:348
  31.6 2.3 %copy-done = bf16[2,24,192,192]{3,2,1,0:T(8,128)(2,1)S(1)} copy-done((bf16[2,24,192,192]{3,2,1,0:T(8,128)(2,1)S(1)}, bf16[2,24,192,192]{3,2,1,0:T(8,128)(2,1)}, u32[]{:S(2)}) %copy-start) | copy-done | bytes 3538968
  33.9 9.3 %shard_map.31 = (bf16[24,192,768]{2,1,0:T(8,128)(2,1)}, f32[192,768]{1,0:T(8,128)S(1)}, f32[192,768]{1,0:T(8,128)S(1)}) custom-call(s32[5]{0:T(128)S(1)} %pad_add_fusion.table, bf16[2,24,192,192]{3,2,1,0:T(8,128)(2,1)S(1)} %copy-done, bf16[2,24,192,192]{3,2,1,0:T(8,128)(2,1)} %collective-permute-done.2.s_ref, ...), custom_call_target="tpu_custom_call" | custom-call | tf_op jit(solution)/shard_map/pallas_call | solution.py:164
  44.3 7.2 %shard_map.32 = (bf16[24,192,768]{2,1,0:T(8,128)(2,1)}, f32[192,768]{1,0:T(8,128)S(1)}, f32[192,768]{1,0:T(8,128)S(1)}) custom-call(s32[5]{0:T(128)S(1)} %pad_add_fusion.table, bf16[2,24,192,192]{3,2,1,0:T(8,128)(2,1)S(1)} %copy-done, bf16[2,24,192,192]{3,2,1,0:T(8,128)(2,1)} %collective-permute-done.2.s_ref, ...), custom_call_target="tpu_custom_call", output_to_operand_aliasing={{0}: (9, {})} | custom-call | tf_op jit(solution)/shard_map/pallas_call | solution.py:164
  51.5 4.7 %shard_map.33 = (bf16[24,192,768]{2,1,0:T(8,128)(2,1)}, bf16[192,1536]{1,0:T(8,128)(2,1)S(1)}) custom-call(s32[5]{0:T(128)S(1)} %pad_add_fusion.table, bf16[2,24,192,192]{3,2,1,0:T(8,128)(2,1)S(1)} %copy-done, bf16[2,24,192,192]{3,2,1,0:T(8,128)(2,1)} %collective-permute-done.2.s_ref, ...), custom_call_target="tpu_custom_call", output_to_operand_aliasing={{0}: (9, {})} | custom-call | tf_op jit(solution)/shard_map/pallas_call | solution.py:164
  57.0 6.4 %all-to-all-start = ((bf16[8,24,1536]{2,1,0:T(8,128)(2,1)}), bf16[8,24,1536]{2,1,0:T(8,128)(2,1)S(1)}, u32[]{:S(2)}, u32[]{:S(2)}) async-start(bf16[8,24,1536]{2,1,0:T(8,128)(2,1)} %bitcast.8), calls=%async_computation | async-start | bytes 1179648 | tf_op jit(solution)/shard_map/all_to_all | solution.py:338
  63.6 11.1 %all-to-all-done = bf16[8,24,1536]{2,1,0:T(8,128)(2,1)S(1)} async-done(((bf16[8,24,1536]{2,1,0:T(8,128)(2,1)}), bf16[8,24,1536]{2,1,0:T(8,128)(2,1)S(1)}, u32[]{:S(2)}, u32[]{:S(2)}) %all-to-all-start) | async-done | bytes 589856 | tf_op jit(solution)/shard_map/all_to_all | solution.py:338
  76.3 3.5 %all-to-all-start.1 = ((bf16[8,24,1536]{2,1,0:T(8,128)(2,1)}), bf16[8,24,1536]{2,1,0:T(8,128)(2,1)S(1)}, u32[]{:S(2)}, u32[]{:S(2)}) async-start(bf16[8,24,1536]{2,1,0:T(8,128)(2,1)} %bitcast.4), calls=%async_computation.1 | async-start | bytes 1179648 | tf_op jit(solution)/shard_map/all_to_all | solution.py:338
  81.4 2.5 %constant_dynamic-update-slice_fusion.1 = bf16[2,12,3,192,128]{4,3,2,1,0:T(8,128)(2,1)} fusion(bf16[2,12,3,192,128]{4,3,2,1,0:T(8,128)(2,1)} %constant_dynamic-update-slice_fusion.2, bf16[2,4,3,192,128]{4,3,2,1,0:T(8,128)(2,1)} %collective-permute-done.4.z_ref), kind=kLoop, calls=%fused_computation.13 | loop fusion | bytes 2359296
  84.9 5.7 %all-to-all-done.1 = bf16[8,24,1536]{2,1,0:T(8,128)(2,1)S(1)} async-done(((bf16[8,24,1536]{2,1,0:T(8,128)(2,1)}), bf16[8,24,1536]{2,1,0:T(8,128)(2,1)S(1)}, u32[]{:S(2)}, u32[]{:S(2)}) %all-to-all-start.1) | async-done | bytes 589856 | tf_op jit(solution)/shard_map/all_to_all | solution.py:338
  91.4 6.8 %shard_map.35 = (bf16[2,6,192,192]{3,2,1,0:T(8,128)(2,1)S(1)}, bf16[2,6,192,192]{3,2,1,0:T(8,128)(2,1)S(1)}, bf16[2,3,3,192,128]{4,3,2,1,0:T(8,128)(2,1)S(1)}, f32[192,768]{1,0:T(8,128)S(1)}) custom-call(s32[5]{0:T(128)S(1)} %pad_add_fusion.table, bf16[2,24,192,192]{3,2,1,0:T(8,128)(2,1)} %x_ref.19, bf16[2,24,192,192]{3,2,1,0:T(8,128)(2,1)} %collective-permute-done.2.s_ref, ...), custom_call_target="tpu_custom_call" | custom-call | tf_op jit(solution)/shard_map/pallas_call | solution.py:280
  100.2 9.7 %shard_map.36 = (bf16[2,10,192,192]{3,2,1,0:T(8,128)(2,1)S(1)}, bf16[2,10,192,192]{3,2,1,0:T(8,128)(2,1)S(1)}, bf16[2,5,3,192,128]{4,3,2,1,0:T(8,128)(2,1)S(1)}, f32[192,768]{1,0:T(8,128)S(1)}) custom-call(s32[5]{0:T(128)S(1)} %pad_add_fusion.table, bf16[2,24,192,192]{3,2,1,0:T(8,128)(2,1)} %x_ref.19, ...), custom_call_target="tpu_custom_call" | custom-call | tf_op jit(solution)/shard_map/pallas_call | solution.py:280
  109.9 3.6 %collective-permute-start.13 = (bf16[2,5,3,192,128]{4,3,2,1,0:T(8,128)(2,1)S(1)}, bf16[2,5,3,192,128]{4,3,2,1,0:T(8,128)(2,1)S(1)}, u32[]{:S(2)}, u32[]{:S(2)}) collective-permute-start(bf16[2,5,3,192,128]{4,3,2,1,0:T(8,128)(2,1)S(1)} %get-tuple-element.53), channel_id=1, source_target_pairs={{0,16},{8,120},{16,32},{24,8},{32,48},{40,24},{48,64},{56,40},{64,... | collective-permute-start | bytes 4423688 | tf_op jit(solution)/shard_map/ppermute | solution.py:374
  113.6 6.8 %shard_map.37 = (bf16[2,6,192,192]{3,2,1,0:T(8,128)(2,1)S(1)}, bf16[2,6,192,192]{3,2,1,0:T(8,128)(2,1)S(1)}, bf16[2,3,3,192,128]{4,3,2,1,0:T(8,128)(2,1)S(1)}, f32[192,768]{1,0:T(8,128)S(1)}) custom-call(s32[5]{0:T(128)S(1)} %pad_add_fusion.table, bf16[2,24,192,192]{3,2,1,0:T(8,128)(2,1)} %x_ref.19, bf16[2,24,192,192]{3,2,1,0:T(8,128)(2,1)} %collective-permute-done.2.s_ref, ...), custom_call_target="tpu_custom_call" | custom-call | tf_op jit(solution)/shard_map/pallas_call | solution.py:280
  122.1 3.7 %shard_map.38 = (bf16[2,2,192,192]{3,2,1,0:T(8,128)(2,1)S(1)}, bf16[2,2,192,192]{3,2,1,0:T(8,128)(2,1)S(1)}, bf16[2,1,3,192,128]{4,3,2,1,0:T(8,128)(2,1)S(1)}) custom-call(s32[5]{0:T(128)S(1)} %pad_add_fusion.table, bf16[2,24,192,192]{3,2,1,0:T(8,128)(2,1)} %x_ref.19, bf16[2,24,192,192]{3,2,1,0:T(8,128)(2,1)} %collective-permute-done.2.s_ref, ...), custom_call_target="tpu_custom_call" | custom-call | tf_op jit(solution)/shard_map/pallas_call | solution.py:280
  125.7 3.8 %collective-permute-start.9 = (bf16[2,1,3,192,128]{4,3,2,1,0:T(8,128)(2,1)S(1)}, bf16[2,1,3,192,128]{4,3,2,1,0:T(8,128)(2,1)S(1)}, u32[]{:S(2)}, u32[]{:S(2)}) collective-permute-start(bf16[2,1,3,192,128]{4,3,2,1,0:T(8,128)(2,1)S(1)} %get-tuple-element.47), channel_id=1, source_target_pairs={{0,16},{8,120},{16,32},{24,8},{32,48},{40,24},{48,64},{56,40},{64,... | collective-permute-start | bytes 884744 | tf_op jit(solution)/shard_map/ppermute | solution.py:374
  131.5 2.6 %shard_map.39.refs_0_ = bf16[2,24,192,192]{3,2,1,0:T(8,128)(2,1)} custom-call(s32[5]{0:T(128)S(1)} %pad_add_fusion.table, bf16[2,6,192,192]{3,2,1,0:T(8,128)(2,1)S(1)} %get-tuple-element.54.x_ref, bf16[2,6,192,192]{3,2,1,0:T(8,128)(2,1)S(1)} %collective-permute-done.6.s_ref, bf16[2,3,3,192,128]{4,3,2,1,0:T(8,128)(2,1)S(1)} %collective-permute-done.7.z_ref), custom_call_target="tpu_custom_call" | custom-call | tf_op jit(solution)/shard_map/pallas_call | solution.py:316
  134.1 3.6 %shard_map.40.refs_0_ = bf16[2,24,192,192]{3,2,1,0:T(8,128)(2,1)} custom-call(s32[5]{0:T(128)S(1)} %pad_add_fusion.table, bf16[2,10,192,192]{3,2,1,0:T(8,128)(2,1)S(1)} %get-tuple-element.51.x_ref, bf16[2,10,192,192]{3,2,1,0:T(8,128)(2,1)S(1)} %collective-permute-done.12.s_ref, ...), custom_call_target="tpu_custom_call", output_to_operand_aliasing={{}: (4, {})} | custom-call | tf_op jit(solution)/shard_map/pallas_call | solution.py:316
  139.4 2.6 %shard_map.41.refs_0_ = bf16[2,24,192,192]{3,2,1,0:T(8,128)(2,1)} custom-call(s32[5]{0:T(128)S(1)} %pad_add_fusion.table, bf16[2,6,192,192]{3,2,1,0:T(8,128)(2,1)S(1)} %get-tuple-element.48.x_ref, bf16[2,6,192,192]{3,2,1,0:T(8,128)(2,1)S(1)} %collective-permute-done.10.s_ref, ...), custom_call_target="tpu_custom_call", output_to_operand_aliasing={{}: (4, {})} | custom-call | tf_op jit(solution)/shard_map/pallas_call | solution.py:316
  (52 shorter events, 24.7 us)
Async XLA Ops:
  0.0 31.6 %collective-permute-start.2 = (bf16[2,24,192,192]{3,2,1,0:T(8,128)(2,1)}, bf16[2,24,192,192]{3,2,1,0:T(8,128)(2,1)}, u32[]{:S(2)}, u32[]{:S(2)}) collective-permute-start(bf16[2,24,192,192]{3,2,1,0:T(8,128)(2,1)} %x_ref.19), channel_id=1, source_target_pairs={{0,8},{8,0},{16,24},{24,16},{32,40},{40,32},{48,56},{56,48},{64,72... | collective-permute-start | bytes 10616840 | tf_op jit(solution)/shard_map/ppermute | solution.py:340
  6.6 6.3 %copy-start.6 = (s32[2,2]{1,0:T(2,128)S(1)}, s32[2,2]{1,0:T(2,128)}, u32[]{:S(2)}) copy-start(s32[2,2]{1,0:T(2,128)} %param.3) | copy-start | bytes 52
  6.6 25.0 %collective-permute-start.3 = (bf16[2,6,3,192,128]{4,3,2,1,0:T(8,128)(2,1)}, bf16[2,6,3,192,128]{4,3,2,1,0:T(8,128)(2,1)S(1)}, u32[]{:S(2)}, u32[]{:S(2)}) collective-permute-start(bf16[2,6,3,192,128]{4,3,2,1,0:T(8,128)(2,1)} %shard_map.28), channel_id=1, source_target_pairs={{0,112},{8,24},{16,0},{24,40},{32,16},{40,56},{48,32},{56,72},{64,... | collective-permute-start | bytes 5308424 | tf_op jit(solution)/shard_map/ppermute | solution.py:348
  11.2 33.1 %collective-permute-start.4 = (bf16[2,4,3,192,128]{4,3,2,1,0:T(8,128)(2,1)}, bf16[2,4,3,192,128]{4,3,2,1,0:T(8,128)(2,1)}, u32[]{:S(2)}, u32[]{:S(2)}) collective-permute-start(bf16[2,4,3,192,128]{4,3,2,1,0:T(8,128)(2,1)} %shard_map.29), channel_id=1, source_target_pairs={{0,112},{8,24},{16,0},{24,40},{32,16},{40,56},{48,32},{56,72},{64,... | collective-permute-start | bytes 3538952 | tf_op jit(solution)/shard_map/ppermute | solution.py:348
  12.9 7.4 %collective-permute-start = (s32[2,2]{1,0:T(2,128)S(1)}, s32[2,2]{1,0:T(2,128)S(1)}, u32[]{:S(2)}, u32[]{:S(2)}) collective-permute-start(s32[2,2]{1,0:T(2,128)S(1)} %copy-done.6), channel_id=1, source_target_pairs={{0,8},{8,0},{16,24},{24,16},{32,40},{40,32},{48,56},{56,48},{64,72... | collective-permute-start | bytes 56 | tf_op jit(solution)/shard_map/ppermute | solution.py:341
  17.7 33.8 %collective-permute-start.5 = (bf16[2,2,3,192,128]{4,3,2,1,0:T(8,128)(2,1)}, bf16[2,2,3,192,128]{4,3,2,1,0:T(8,128)(2,1)S(1)}, u32[]{:S(2)}, u32[]{:S(2)}) collective-permute-start(bf16[2,2,3,192,128]{4,3,2,1,0:T(8,128)(2,1)} %shard_map.30), channel_id=1, source_target_pairs={{0,112},{8,24},{16,0},{24,40},{32,16},{40,56},{48,32},{56,72},{64,... | collective-permute-start | bytes 1769480 | tf_op jit(solution)/shard_map/ppermute | solution.py:348
  19.4 32.1 %copy-start.1 = (f32[192,384]{1,0:T(8,128)}, f32[192,384]{1,0:T(8,128)S(1)}, u32[]{:S(2)}) copy-start(f32[192,384]{1,0:T(8,128)S(1)} %get-tuple-element.57.log_ref) | copy-start | bytes 884740
  19.4 32.1 %copy-start.2 = (f32[192,384]{1,0:T(8,128)}, f32[192,384]{1,0:T(8,128)S(1)}, u32[]{:S(2)}) copy-start(f32[192,384]{1,0:T(8,128)S(1)} %get-tuple-element.58.r_ref) | copy-start | bytes 884740
  20.2 31.3 %copy-start.3 = (bf16[192,192]{1,0:T(8,128)(2,1)}, bf16[192,192]{1,0:T(8,128)(2,1)S(1)}, u32[]{:S(2)}) copy-start(bf16[192,192]{1,0:T(8,128)(2,1)S(1)} %sine_convert_fusion.sines_ref) | copy-start | bytes 221188
  20.2 5.3 %collective-permute-start.1 = (s32[2,2]{1,0:T(2,128)S(1)}, s32[2,2]{1,0:T(2,128)S(1)}, u32[]{:S(2)}, u32[]{:S(2)}) collective-permute-start(s32[2,2]{1,0:T(2,128)S(1)} %collective-permute-done), channel_id=1, source_target_pairs={{0,24},{8,112},{16,40},{24,0},{32,56},{40,16},{48,72},{56,32},{64,... | collective-permute-start | bytes 56 | tf_op jit(solution)/shard_map/ppermute | solution.py:341
  31.6 2.3 %copy-start = (bf16[2,24,192,192]{3,2,1,0:T(8,128)(2,1)S(1)}, bf16[2,24,192,192]{3,2,1,0:T(8,128)(2,1)}, u32[]{:S(2)}) copy-start(bf16[2,24,192,192]{3,2,1,0:T(8,128)(2,1)} %x_ref.19) | copy-start | bytes 10616836
  56.2 0.8 copy-start.4
  57.0 17.7 %all-to-all-start = ((bf16[8,24,1536]{2,1,0:T(8,128)(2,1)}), bf16[8,24,1536]{2,1,0:T(8,128)(2,1)S(1)}, u32[]{:S(2)}, u32[]{:S(2)}) async-start(bf16[8,24,1536]{2,1,0:T(8,128)(2,1)} %bitcast.8), calls=%async_computation | async-start | bytes 1179648 | tf_op jit(solution)/shard_map/all_to_all | solution.py:338
  76.3 14.2 %all-to-all-start.1 = ((bf16[8,24,1536]{2,1,0:T(8,128)(2,1)}), bf16[8,24,1536]{2,1,0:T(8,128)(2,1)S(1)}, u32[]{:S(2)}, u32[]{:S(2)}) async-start(bf16[8,24,1536]{2,1,0:T(8,128)(2,1)} %bitcast.4), calls=%async_computation.1 | async-start | bytes 1179648 | tf_op jit(solution)/shard_map/all_to_all | solution.py:338
  90.6 0.8 copy-start.5
  98.2 15.4 %collective-permute-start.7 = (bf16[2,3,3,192,128]{4,3,2,1,0:T(8,128)(2,1)S(1)}, bf16[2,3,3,192,128]{4,3,2,1,0:T(8,128)(2,1)S(1)}, u32[]{:S(2)}, u32[]{:S(2)}) collective-permute-start(bf16[2,3,3,192,128]{4,3,2,1,0:T(8,128)(2,1)S(1)} %get-tuple-element.40), channel_id=1, source_target_pairs={{0,16},{8,120},{16,32},{24,8},{32,48},{40,24},{48,64},{56,40},{64,... | collective-permute-start | bytes 2654216 | tf_op jit(solution)/shard_map/ppermute | solution.py:374
  98.3 15.3 %collective-permute-start.6 = (bf16[2,6,192,192]{3,2,1,0:T(8,128)(2,1)S(1)}, bf16[2,6,192,192]{3,2,1,0:T(8,128)(2,1)S(1)}, u32[]{:S(2)}, u32[]{:S(2)}) collective-permute-start(bf16[2,6,192,192]{3,2,1,0:T(8,128)(2,1)S(1)} %get-tuple-element.39), channel_id=1, source_target_pairs={{0,8},{8,0},{16,24},{24,16},{32,40},{40,32},{48,56},{56,48},{64,72... | collective-permute-start | bytes 2654216 | tf_op jit(solution)/shard_map/ppermute | solution.py:374
  109.9 20.0 %collective-permute-start.13 = (bf16[2,5,3,192,128]{4,3,2,1,0:T(8,128)(2,1)S(1)}, bf16[2,5,3,192,128]{4,3,2,1,0:T(8,128)(2,1)S(1)}, u32[]{:S(2)}, u32[]{:S(2)}) collective-permute-start(bf16[2,5,3,192,128]{4,3,2,1,0:T(8,128)(2,1)S(1)} %get-tuple-element.53), channel_id=1, source_target_pairs={{0,16},{8,120},{16,32},{24,8},{32,48},{40,24},{48,64},{56,40},{64,... | collective-permute-start | bytes 4423688 | tf_op jit(solution)/shard_map/ppermute | solution.py:374
  113.6 20.5 %collective-permute-start.12 = (bf16[2,10,192,192]{3,2,1,0:T(8,128)(2,1)S(1)}, bf16[2,10,192,192]{3,2,1,0:T(8,128)(2,1)S(1)}, u32[]{:S(2)}, u32[]{:S(2)}) collective-permute-start(bf16[2,10,192,192]{3,2,1,0:T(8,128)(2,1)S(1)} %get-tuple-element.52), channel_id=1, source_target_pairs={{0,8},{8,0},{16,24},{24,16},{32,40},{40,32},{48,56},{56,48},{64,72... | collective-permute-start | bytes 4423688 | tf_op jit(solution)/shard_map/ppermute | solution.py:374
  120.4 19.0 %collective-permute-start.11 = (bf16[2,3,3,192,128]{4,3,2,1,0:T(8,128)(2,1)S(1)}, bf16[2,3,3,192,128]{4,3,2,1,0:T(8,128)(2,1)S(1)}, u32[]{:S(2)}, u32[]{:S(2)}) collective-permute-start(bf16[2,3,3,192,128]{4,3,2,1,0:T(8,128)(2,1)S(1)} %get-tuple-element.50), channel_id=1, source_target_pairs={{0,16},{8,120},{16,32},{24,8},{32,48},{40,24},{48,64},{56,40},{64,... | collective-permute-start | bytes 2654216 | tf_op jit(solution)/shard_map/ppermute | solution.py:374
  120.7 18.6 %collective-permute-start.10 = (bf16[2,6,192,192]{3,2,1,0:T(8,128)(2,1)S(1)}, bf16[2,6,192,192]{3,2,1,0:T(8,128)(2,1)S(1)}, u32[]{:S(2)}, u32[]{:S(2)}) collective-permute-start(bf16[2,6,192,192]{3,2,1,0:T(8,128)(2,1)S(1)} %get-tuple-element.49), channel_id=1, source_target_pairs={{0,8},{8,0},{16,24},{24,16},{32,40},{40,32},{48,56},{56,48},{64,72... | collective-permute-start | bytes 2654216 | tf_op jit(solution)/shard_map/ppermute | solution.py:374
  125.7 16.8 %collective-permute-start.9 = (bf16[2,1,3,192,128]{4,3,2,1,0:T(8,128)(2,1)S(1)}, bf16[2,1,3,192,128]{4,3,2,1,0:T(8,128)(2,1)S(1)}, u32[]{:S(2)}, u32[]{:S(2)}) collective-permute-start(bf16[2,1,3,192,128]{4,3,2,1,0:T(8,128)(2,1)S(1)} %get-tuple-element.47), channel_id=1, source_target_pairs={{0,16},{8,120},{16,32},{24,8},{32,48},{40,24},{48,64},{56,40},{64,... | collective-permute-start | bytes 884744 | tf_op jit(solution)/shard_map/ppermute | solution.py:374
  129.9 12.6 %collective-permute-start.8 = (bf16[2,2,192,192]{3,2,1,0:T(8,128)(2,1)S(1)}, bf16[2,2,192,192]{3,2,1,0:T(8,128)(2,1)S(1)}, u32[]{:S(2)}, u32[]{:S(2)}) collective-permute-start(bf16[2,2,192,192]{3,2,1,0:T(8,128)(2,1)S(1)} %get-tuple-element.46), channel_id=1, source_target_pairs={{0,8},{8,0},{16,24},{24,16},{32,40},{40,32},{48,56},{56,48},{64,72... | collective-permute-start | bytes 884744 | tf_op jit(solution)/shard_map/ppermute | solution.py:374

commit v3 on v2

--- a/solution.py
+++ b/solution.py
@@ -16,7 +16,7 @@
 PAIRED = ROWS // 2
 PIECES_IN = (6, 4, 2)
 PIECES_OUT = (1, 3, 5, 3)
-PACKED = 2
+WAITS = (2,)
 
 F32 = jnp.float32
 BF16 = jnp.bfloat16
@@ -97,24 +97,42 @@
     return pltpu.with_memory_space_constraint(block, pltpu.HBM)
 
 
-def pack_kernel(table, x_ref, z_ref):
-    for band in range(2):
-        for pair in range(PACKED):
-            low, high = 2 * pair, 2 * pair + 1
-            z_ref[band, pair, 0] = x_ref[band, low, :, :128]
-            z_ref[band, pair, 1] = x_ref[band, high, :, :128]
-            tails = [x_ref[band, plane, :, 128:].astype(F32) for plane in (low, high)]
-            z_ref[band, pair, 2] = jnp.concatenate(tails, axis=1).astype(BF16)
-
-
-def pack(table, x, start, count):
-    return call(
-        pack_kernel,
-        (count // PACKED,),
-        [pl.BlockSpec((2, 2 * PACKED, NG, NG), lambda i, table: (0, start // PACKED + i, 0, 0))],
-        pl.BlockSpec((2, PACKED, 3, NG, 128), lambda i, table: (0, i, 0, 0, 0)),
-        jax.ShapeDtypeStruct((2, count, 3, NG, 128), BF16),
-    )(table, in_hbm(x))
+def pack_kernel(start, count, x_ref, z_ref, planes_in, packed_out, sems_in, sems_out):
+    def fetch(i):
+        return pltpu.make_async_copy(x_ref.at[:, pl.ds(2 * (start + i), 2)], planes_in.at[i], sems_in.at[i])
+
+    def store(i):
+        return pltpu.make_async_copy(packed_out.at[i], z_ref.at[:, i], sems_out.at[i])
+
+    for i in range(count):
+        fetch(i).start()
+    for i in range(count):
+        fetch(i).wait()
+        for band in range(2):
+            for half in range(2):
+                packed_out[i, band, half] = planes_in[i, band, half, :, :128]
+            tails = [planes_in[i, band, half, :, 128:].astype(F32) for half in range(2)]
+            packed_out[i, band, 2] = jnp.concatenate(tails, axis=1).astype(BF16)
+        store(i).start()
+    for i in range(count):
+        store(i).wait()
+
+
+def pack(x, start, count):
+    return pl.pallas_call(
+        functools.partial(pack_kernel, start, count),
+        in_specs=[ANY],
+        out_specs=ANY,
+        out_shape=jax.ShapeDtypeStruct((2, count, 3, NG, 128), BF16),
+        scratch_shapes=[
+            pltpu.VMEM((count, 2, 2, NG, NG), BF16),
+            pltpu.VMEM((count, 2, 3, NG, 128), BF16),
+            pltpu.SemaphoreType.DMA((count,)),
+            pltpu.SemaphoreType.DMA((count,)),
+        ],
+        compiler_params=params(),
+        cost_estimate=pl.CostEstimate(flops=0, bytes_accessed=0, transcendentals=0),
+    )(in_hbm(x))
 
 
 def forward_kernel(start, first, last, table, x_ref, s_ref, z_ref, sines_ref, r_ref, log_ref, *refs):
@@ -167,7 +185,7 @@
         [planes(at), planes(at), packed(lambda i: i), whole(NG, NG), whole(NG, 2 * NG), whole(NG, 2 * NG)]
         + ([] if first else [whole(NG, WIDE), whole(NG, WIDE), ANY]),
         [spectra(at)] + ([whole(NG, 2 * WIDE)] if last else [whole(NG, WIDE)] * 2),
-        [pltpu.HBM((ROWS, NG, WIDE), BF16)] + ([jax.ShapeDtypeStruct((NG, 2 * WIDE), BF16)] if last else [STATE] * 2),
+        [pltpu.HBM((ROWS, NG, WIDE), BF16)] + ([pltpu.HBM((NG, 2 * WIDE), BF16)] if last else [STATE] * 2),
         scratch=[pltpu.VMEM((NG, WIDE), F32)] * 2 + [pltpu.VMEM((2, 2, NG, NG), BF16)],
         aliases={} if first else {9: 0},
     )(table, x, s, z, sines, r, log_r, *(() if first else (carried[1], carried[2], carried[0])))
@@ -219,12 +237,10 @@
     return [terms[0] + (terms[1] - other), other]
 
 
-def back_kernel(start, count, first, fresh, table, x_ref, s_ref, z_ref, sines_ref, r_ref, log_ref, p_ref, e_ref, *refs):
+def back_kernel(start, count, first, table, x_ref, s_ref, z_ref, sines_ref, r_ref, log_ref, p_ref, e_ref, *refs):
     refs = list(refs)
     if not first:
         u_in = refs.pop(0)
-    if not fresh:
-        refs = refs[2:]
     xo_ref, so_ref, zo_ref = (refs.pop(0) for _ in range(3))
     if start > 0:
         u_out = refs.pop(0)
@@ -238,7 +254,7 @@
     core = table[CORE]
     low_core = core == 0
     sines = sines_ref[...]
-    kept = {}
+    kept, given = {}, {}
     for half in (1, 0):
         for band in range(2):
             both[0, band] = x_ref[band, half]
@@ -261,9 +277,10 @@
         own_at, sent_at = jnp.where(low_core, 0, third_at), jnp.where(low_core, third_at, 0)
         for j in range(2):
             xo_ref[jnp.abs(own_at - j), half] = jnp.where(low_core, own[j], third[j]).astype(BF16)
-            so_ref[jnp.abs(swap_at - j), half] = swap[j].astype(BF16)
+            given[j, half] = swap[j]
             kept[j, half] = jnp.where(low_core, third[j], own[j])
     for j in range(2):
+        pack_into(so_ref, jnp.abs(swap_at - j), given[j, 0], given[j, 1])
         pack_into(zo_ref, jnp.abs(sent_at - j), kept[j, 0], kept[j, 1])
 
     if start > 0:
@@ -273,50 +290,47 @@
             u_out[...] = u_ref[...]
 
 
-def back(table, x, s, z, z_start, sines, r, log_r, p, edges, u, sums, base, size, start, count):
-    first, fresh = u is None, sums is None
+def back(table, x, s, z, sines, r, log_r, p, edges, u, start, count):
+    first = u is None
     at = lambda i: start + count - 1 - i
-    in_sums = lambda i: at(i) - base
+    local = lambda i: count - 1 - i
     outs = call(
-        functools.partial(back_kernel, start, count, first, fresh),
+        functools.partial(back_kernel, start, count, first),
         (count,),
         [
             planes(at),
             planes(at),
-            packed(lambda i: at(i) - z_start),
+            packed(at),
             whole(NG, NG),
             whole(NG, 2 * NG),
             whole(NG, 2 * NG),
             spectra(at),
             whole(NG, 2 * WIDE),
         ]
-        + ([] if first else [whole(NG, WIDE)])
-        + ([] if fresh else [ANY, ANY]),
-        [planes(in_sums), planes(in_sums), packed(lambda i: count - 1 - i)] + ([whole(NG, WIDE)] if start > 0 else []),
-        [jax.ShapeDtypeStruct((2, 2 * size, NG, NG), BF16)] * 2
-        + [jax.ShapeDtypeStruct((2, count, 3, NG, 128), BF16)]
+        + ([] if first else [whole(NG, WIDE)]),
+        [planes(local), packed(local), packed(local)] + ([whole(NG, WIDE)] if start > 0 else []),
+        [jax.ShapeDtypeStruct((2, 2 * count, NG, NG), BF16)]
+        + [jax.ShapeDtypeStruct((2, count, 3, NG, 128), BF16)] * 2
         + ([STATE] if start > 0 else []),
         scratch=[pltpu.VMEM((NG, WIDE), F32), pltpu.VMEM((2, 2, NG, NG), BF16)],
-        aliases={} if fresh else {10 - first: 0, 11 - first: 1},
-        cost=0,
-    )(table, *(in_hbm(block) for block in (x, s, z, sines, r, log_r, p, edges)), *(() if first else (u,)), *(() if fresh else sums))
-    return outs[:2], outs[2], outs[3] if start > 0 else None
+    )(table, *(in_hbm(block) for block in (x, s, z, sines, r, log_r, p, edges)), *(() if first else (u,)))
+    return outs[:3], outs[3] if start > 0 else None
 
 
 def close_kernel(scale, table, x_ref, s_ref, z_ref, *refs):
     for half in range(2):
         for band in range(2):
-            total = x_ref[band, half].astype(F32) + s_ref[band, half].astype(F32) + unpacked(z_ref, band, half)
+            total = x_ref[band, half].astype(F32) + unpacked(s_ref, band, half) + unpacked(z_ref, band, half)
             refs[-1][band, half] = (scale * total).astype(BF16)
 
 
-def close(scale, table, xo, so, zo, out, base, start, count):
-    from_sums = planes(lambda i: start - base + i)
+def close(scale, table, xo, so, zo, out, start, count):
+    same = lambda i: i
     more = [] if out is None else [out]
     return call(
         functools.partial(close_kernel, scale),
         (count,),
-        [from_sums, from_sums, packed(lambda i: i)] + [ANY] * len(more),
+        [planes(same), packed(same), packed(same)] + [ANY] * len(more),
         planes(lambda i: start + i),
         jax.ShapeDtypeStruct((2, ROWS, NG, NG), BF16),
         aliases={4: 0} if more else {},
@@ -344,7 +358,7 @@
     )
     arrived = []
     for start, count in placed(PIECES_IN):
-        piece = pack(plan[0], orbitals, start, count)
+        piece = pack(orbitals, start, count)
         arrived.append((start, count, lax.ppermute(piece, "band", out_way)))
 
     sines = sine_table()
@@ -364,17 +378,16 @@
     joined = jnp.concatenate([z for _, _, z in arrived], axis=1)
     u, parts = None, []
     for start, count in reversed(placed(PIECES_OUT)):
-        if len(parts) == 2:
+        if len(parts) in WAITS:
             xo, so, zo, *where = parts[-2]
             so, zo, u = lax.optimization_barrier((so, zo, u))
             parts[-2] = (xo, so, zo, *where)
-        (xo, so), zo, u = back(
-            table, orbitals, swapped, joined, 0, sines, root, log_root, held, edges, u, None, start, count, start, count
-        )
+        (xo, so, zo), u = back(table, orbitals, swapped, joined, sines, root, log_root, held, edges, u, start, count)
         parts.append((xo, lax.ppermute(so, "band", across), lax.ppermute(zo, "band", home_way), start, count))
     out = None
-    for xo, so, zo, start, count in parts:
-        out = close(scale, table, xo, so, zo, out, start, start, count)
+    for part in parts:
+        xo, so, zo, start, count = part
+        out = close(scale, table, xo, so, zo, out, start, count)
     return out
 
 

time: 145 us -> 143 us (0.986)
  Pallas kernels: 70.1 us -> 67.5 us
  waiting for transfers between devices: 31.4 us -> 33.8 us
  local copies, waits for them, and re-layouts: 9.74 us -> 8.2 us
    pallas_call x11, Pallas kernels: 47.3 us -> 43.9 us  [the longest x4 26.8 us: back(): call(functools.partial(back_kernel, start, count, first), (count,), [plan...]
    ppermute x4, waiting for transfers between devices: 2.51 us -> 3.97 us  [shards(): lax.ppermute(zo, 'band', home_way)]
    unnamed x16 -> x14, local copies, waits for them, and re-layouts: 8.06 us -> 7.2 us
  transfers between devices with their start and end apart: 16 -> 16, of which waited for: 8 -> 7; matrix products, arithmetic and copies ran while one was open for 5% -> 5% of each run, Pallas kernels for 39% -> 37%
where the time goes in v3:
time: 143 us; the launch traced here: 141 us
  Pallas kernels  67.5 us (47%)
  waiting for transfers between devices  33.8 us (24%)
  starting transfers between devices  30.3 us (21%)
  local copies, waits for them, and re-layouts  8.2 us (6%)
    pallas_call x4, Pallas kernels, back(): call(functools.partial(back_kernel, start, count, first), (count,), [plan...  26.8 us
    pallas_call x3, Pallas kernels, forward(): call(functools.partial(forward_kernel, start, first, last), (count,), [pl...  21.9 us
    all_to_all x2, waiting for transfers between devices, shards(): lax.all_to_all(block, 'grid', split_axis=0, concat_axis=0, tiled=True)  16.9 us
    pallas_call x4, Pallas kernels, close(): call(functools.partial(close_kernel, scale), (count,), [planes(same), pac...  10.4 us
    all_to_all x2, starting transfers between devices, shards(): lax.all_to_all(block, 'grid', split_axis=0, concat_axis=0, tiled=True)  9.89 us
    ppermute x3, waiting for transfers between devices, shards(): arrived.append((start, count, lax.ppermute(piece, 'band', out_way)))  8 us
    ppermute x4, starting transfers between devices, shards(): lax.ppermute(zo, 'band', home_way)  7.94 us
    unnamed x14, local copies, waits for them, and re-layouts  7.2 us
  transfers between devices with their start and end apart: 16, of which 7 were waited for; matrix products, arithmetic and copies ran while one was open for 5% of the time, Pallas kernels for 37%

profile of v3, /device:TPU:1, one launch (start us, length us, event | category | flops | bytes accessed | tf_op | source)
XLA Modules:
  0.0 141.4 jit_solution(5502196393643329529)
XLA Ops:
  1.4 2.5 %shard_map.28 = bf16[2,6,3,192,128]{4,3,2,1,0:T(8,128)(2,1)} custom-call(bf16[2,24,192,192]{3,2,1,0:T(8,128)(2,1)} %x_ref.19), custom_call_target="tpu_custom_call" | custom-call | tf_op jit(solution)/shard_map/pallas_call | solution.py:122
  5.7 2.2 %shard_map.29 = bf16[2,4,3,192,128]{4,3,2,1,0:T(8,128)(2,1)} custom-call(bf16[2,24,192,192]{3,2,1,0:T(8,128)(2,1)} %x_ref.19), custom_call_target="tpu_custom_call" | custom-call | tf_op jit(solution)/shard_map/pallas_call | solution.py:122
  9.7 2.2 %collective-permute-start = (s32[2,2]{1,0:T(2,128)S(1)}, s32[2,2]{1,0:T(2,128)S(1)}, u32[]{:S(2)}, u32[]{:S(2)}) collective-permute-start(s32[2,2]{1,0:T(2,128)S(1)} %copy-done.5), channel_id=1, source_target_pairs={{0,8},{8,0},{16,24},{24,16},{32,40},{40,32},{48,56},{56,48},{64,72... | collective-permute-start | bytes 56 | tf_op jit(solution)/shard_map/ppermute | solution.py:355
  16.7 5.0 %collective-permute-done.1 = s32[2,2]{1,0:T(2,128)S(1)} collective-permute-done((s32[2,2]{1,0:T(2,128)S(1)}, s32[2,2]{1,0:T(2,128)S(1)}, u32[]{:S(2)}, u32[]{:S(2)}) %collective-permute-start.1) | collective-permute-done | bytes 48 | tf_op jit(solution)/shard_map/ppermute | solution.py:355
  21.8 7.2 %collective-permute-done.3.z_ref = bf16[2,6,3,192,128]{4,3,2,1,0:T(8,128)(2,1)S(1)} collective-permute-done((bf16[2,6,3,192,128]{4,3,2,1,0:T(8,128)(2,1)}, bf16[2,6,3,192,128]{4,3,2,1,0:T(8,128)(2,1)S(1)}, u32[]{:S(2)}, u32[]{:S(2)}) %collective-permute-start.3) | collective-permute-done | bytes 1769504 | tf_op jit(solution)/shard_map/ppermute | solution.py:362
  29.0 2.3 %copy-done = bf16[2,24,192,192]{3,2,1,0:T(8,128)(2,1)S(1)} copy-done((bf16[2,24,192,192]{3,2,1,0:T(8,128)(2,1)S(1)}, bf16[2,24,192,192]{3,2,1,0:T(8,128)(2,1)}, u32[]{:S(2)}) %copy-start) | copy-done | bytes 3538968
  31.3 9.6 %shard_map.31 = (bf16[24,192,768]{2,1,0:T(8,128)(2,1)}, f32[192,768]{1,0:T(8,128)S(1)}, f32[192,768]{1,0:T(8,128)S(1)}) custom-call(s32[5]{0:T(128)S(1)} %pad_add_fusion.table, bf16[2,24,192,192]{3,2,1,0:T(8,128)(2,1)S(1)} %copy-done, bf16[2,24,192,192]{3,2,1,0:T(8,128)(2,1)} %collective-permute-done.2.s_ref, ...), custom_call_target="tpu_custom_call" | custom-call | tf_op jit(solution)/shard_map/pallas_call | solution.py:182
  41.7 7.4 %shard_map.32 = (bf16[24,192,768]{2,1,0:T(8,128)(2,1)}, f32[192,768]{1,0:T(8,128)S(1)}, f32[192,768]{1,0:T(8,128)S(1)}) custom-call(s32[5]{0:T(128)S(1)} %pad_add_fusion.table, bf16[2,24,192,192]{3,2,1,0:T(8,128)(2,1)S(1)} %copy-done, bf16[2,24,192,192]{3,2,1,0:T(8,128)(2,1)} %collective-permute-done.2.s_ref, ...), custom_call_target="tpu_custom_call", output_to_operand_aliasing={{0}: (9, {})} | custom-call | tf_op jit(solution)/shard_map/pallas_call | solution.py:182
  49.1 5.0 %shard_map.33 = (bf16[24,192,768]{2,1,0:T(8,128)(2,1)}, bf16[192,1536]{1,0:T(8,128)(2,1)}) custom-call(s32[5]{0:T(128)S(1)} %pad_add_fusion.table, bf16[2,24,192,192]{3,2,1,0:T(8,128)(2,1)S(1)} %copy-done, bf16[2,24,192,192]{3,2,1,0:T(8,128)(2,1)} %collective-permute-done.2.s_ref, ...), custom_call_target="tpu_custom_call", output_to_operand_aliasing={{0}: (9, {})} | custom-call | tf_op jit(solution)/shard_map/pallas_call | solution.py:182
  54.1 6.4 %all-to-all-start = ((bf16[8,24,1536]{2,1,0:T(8,128)(2,1)}), bf16[8,24,1536]{2,1,0:T(8,128)(2,1)S(1)}, u32[]{:S(2)}, u32[]{:S(2)}) async-start(bf16[8,24,1536]{2,1,0:T(8,128)(2,1)} %bitcast.10), calls=%async_computation | async-start | bytes 1179648 | tf_op jit(solution)/shard_map/all_to_all | solution.py:352
  60.7 11.1 %all-to-all-done = bf16[8,24,1536]{2,1,0:T(8,128)(2,1)S(1)} async-done(((bf16[8,24,1536]{2,1,0:T(8,128)(2,1)}), bf16[8,24,1536]{2,1,0:T(8,128)(2,1)S(1)}, u32[]{:S(2)}, u32[]{:S(2)}) %all-to-all-start) | async-done | bytes 589856 | tf_op jit(solution)/shard_map/all_to_all | solution.py:352
  73.5 3.5 %all-to-all-start.1 = ((bf16[8,24,1536]{2,1,0:T(8,128)(2,1)}), bf16[8,24,1536]{2,1,0:T(8,128)(2,1)S(1)}, u32[]{:S(2)}, u32[]{:S(2)}) async-start(bf16[8,24,1536]{2,1,0:T(8,128)(2,1)} %bitcast.3), calls=%async_computation.1 | async-start | bytes 1179648 | tf_op jit(solution)/shard_map/all_to_all | solution.py:352
  78.5 2.5 %constant_dynamic-update-slice_fusion.1 = bf16[2,12,3,192,128]{4,3,2,1,0:T(8,128)(2,1)} fusion(bf16[2,12,3,192,128]{4,3,2,1,0:T(8,128)(2,1)} %constant_dynamic-update-slice_fusion.2, bf16[2,4,3,192,128]{4,3,2,1,0:T(8,128)(2,1)} %collective-permute-done.4.z_ref), kind=kLoop, calls=%fused_computation.13 | loop fusion | bytes 2359296
  81.9 5.8 %all-to-all-done.1 = bf16[8,24,1536]{2,1,0:T(8,128)(2,1)S(1)} async-done(((bf16[8,24,1536]{2,1,0:T(8,128)(2,1)}), bf16[8,24,1536]{2,1,0:T(8,128)(2,1)S(1)}, u32[]{:S(2)}, u32[]{:S(2)}) %all-to-all-start.1) | async-done | bytes 589856 | tf_op jit(solution)/shard_map/all_to_all | solution.py:352
  88.5 6.7 %shard_map.35 = (bf16[2,6,192,192]{3,2,1,0:T(8,128)(2,1)S(1)}, bf16[2,3,3,192,128]{4,3,2,1,0:T(8,128)(2,1)S(1)}, bf16[2,3,3,192,128]{4,3,2,1,0:T(8,128)(2,1)S(1)}, f32[192,768]{1,0:T(8,128)S(1)}) custom-call(s32[5]{0:T(128)S(1)} %pad_add_fusion.table, bf16[2,24,192,192]{3,2,1,0:T(8,128)(2,1)} %x_ref.19, ...), custom_call_target="tpu_custom_call" | custom-call | tf_op jit(solution)/shard_map/pallas_call | solution.py:297
  97.9 9.7 %shard_map.36 = (bf16[2,10,192,192]{3,2,1,0:T(8,128)(2,1)S(1)}, bf16[2,5,3,192,128]{4,3,2,1,0:T(8,128)(2,1)S(1)}, bf16[2,5,3,192,128]{4,3,2,1,0:T(8,128)(2,1)S(1)}, f32[192,768]{1,0:T(8,128)S(1)}) custom-call(s32[5]{0:T(128)S(1)} %pad_add_fusion.table, bf16[2,24,192,192]{3,2,1,0:T(8,128)(2,1)} %x_ref.19, ...), custom_call_target="tpu_custom_call" | custom-call | tf_op jit(solution)/shard_map/pallas_call | solution.py:297
  107.7 3.3 %collective-permute-start.13 = (bf16[2,5,3,192,128]{4,3,2,1,0:T(8,128)(2,1)S(1)}, bf16[2,5,3,192,128]{4,3,2,1,0:T(8,128)(2,1)S(1)}, u32[]{:S(2)}, u32[]{:S(2)}) collective-permute-start(bf16[2,5,3,192,128]{4,3,2,1,0:T(8,128)(2,1)S(1)} %get-tuple-element.53), channel_id=1, source_target_pairs={{0,16},{8,120},{16,32},{24,8},{32,48},{40,24},{48,64},{56,40},{64,... | collective-permute-start | bytes 4423688 | tf_op jit(solution)/shard_map/ppermute | solution.py:386
  111.0 6.8 %shard_map.37 = (bf16[2,6,192,192]{3,2,1,0:T(8,128)(2,1)S(1)}, bf16[2,3,3,192,128]{4,3,2,1,0:T(8,128)(2,1)S(1)}, bf16[2,3,3,192,128]{4,3,2,1,0:T(8,128)(2,1)S(1)}, f32[192,768]{1,0:T(8,128)S(1)}) custom-call(s32[5]{0:T(128)S(1)} %pad_add_fusion.table, bf16[2,24,192,192]{3,2,1,0:T(8,128)(2,1)} %x_ref.19, ...), custom_call_target="tpu_custom_call" | custom-call | tf_op jit(solution)/shard_map/pallas_call | solution.py:297
  119.3 3.7 %shard_map.38 = (bf16[2,2,192,192]{3,2,1,0:T(8,128)(2,1)S(1)}, bf16[2,1,3,192,128]{4,3,2,1,0:T(8,128)(2,1)S(1)}, bf16[2,1,3,192,128]{4,3,2,1,0:T(8,128)(2,1)S(1)}) custom-call(s32[5]{0:T(128)S(1)} %pad_add_fusion.table, bf16[2,24,192,192]{3,2,1,0:T(8,128)(2,1)} %x_ref.19, bf16[2,24,192,192]{3,2,1,0:T(8,128)(2,1)} %collective-permute-done.2.s_ref, ...), custom_call_target="tpu_custom_call" | custom-call | tf_op jit(solution)/shard_map/pallas_call | solution.py:297
  123.2 3.8 %collective-permute-start.9 = (bf16[2,1,3,192,128]{4,3,2,1,0:T(8,128)(2,1)S(1)}, bf16[2,1,3,192,128]{4,3,2,1,0:T(8,128)(2,1)S(1)}, u32[]{:S(2)}, u32[]{:S(2)}) collective-permute-start(bf16[2,1,3,192,128]{4,3,2,1,0:T(8,128)(2,1)S(1)} %get-tuple-element.47), channel_id=1, source_target_pairs={{0,16},{8,120},{16,32},{24,8},{32,48},{40,24},{48,64},{56,40},{64,... | collective-permute-start | bytes 884744 | tf_op jit(solution)/shard_map/ppermute | solution.py:386
  127.0 2.6 %shard_map.39.refs_0_ = bf16[2,24,192,192]{3,2,1,0:T(8,128)(2,1)} custom-call(s32[5]{0:T(128)S(1)} %pad_add_fusion.table, bf16[2,6,192,192]{3,2,1,0:T(8,128)(2,1)S(1)} %get-tuple-element.54.x_ref, bf16[2,3,3,192,128]{4,3,2,1,0:T(8,128)(2,1)S(1)} %collective-permute-done.6.s_ref, bf16[2,3,3,192,128]{4,3,2,1,0:T(8,128)(2,1)S(1)} %collective-permute-done.7.z_ref), custom_call_target="tpu_custom_call" | custom-call | tf_op jit(solution)/shard_map/pallas_call | solution.py:330
  129.6 3.7 %shard_map.40.refs_0_ = bf16[2,24,192,192]{3,2,1,0:T(8,128)(2,1)} custom-call(s32[5]{0:T(128)S(1)} %pad_add_fusion.table, bf16[2,10,192,192]{3,2,1,0:T(8,128)(2,1)S(1)} %get-tuple-element.51.x_ref, bf16[2,5,3,192,128]{4,3,2,1,0:T(8,128)(2,1)S(1)} %collective-permute-done.12.s_ref, ...), custom_call_target="tpu_custom_call", output_to_operand_aliasing={{}: (4, {})} | custom-call | tf_op jit(solution)/shard_map/pallas_call | solution.py:330
  133.3 3.4 %collective-permute-done.11.z_ref = bf16[2,3,3,192,128]{4,3,2,1,0:T(8,128)(2,1)S(1)} collective-permute-done((bf16[2,3,3,192,128]{4,3,2,1,0:T(8,128)(2,1)S(1)}, bf16[2,3,3,192,128]{4,3,2,1,0:T(8,128)(2,1)S(1)}, u32[]{:S(2)}, u32[]{:S(2)}) %collective-permute-start.11) | collective-permute-done | bytes 884768 | tf_op jit(solution)/shard_map/ppermute | solution.py:386
  136.7 2.6 %shard_map.41.refs_0_ = bf16[2,24,192,192]{3,2,1,0:T(8,128)(2,1)} custom-call(s32[5]{0:T(128)S(1)} %pad_add_fusion.table, bf16[2,6,192,192]{3,2,1,0:T(8,128)(2,1)S(1)} %get-tuple-element.48.x_ref, bf16[2,3,3,192,128]{4,3,2,1,0:T(8,128)(2,1)S(1)} %collective-permute-done.10.s_ref, ...), custom_call_target="tpu_custom_call", output_to_operand_aliasing={{}: (4, {})} | custom-call | tf_op jit(solution)/shard_map/pallas_call | solution.py:330
  (49 shorter events, 22.4 us)
Async XLA Ops:
  0.0 29.0 %collective-permute-start.2 = (bf16[2,24,192,192]{3,2,1,0:T(8,128)(2,1)}, bf16[2,24,192,192]{3,2,1,0:T(8,128)(2,1)}, u32[]{:S(2)}, u32[]{:S(2)}) collective-permute-start(bf16[2,24,192,192]{3,2,1,0:T(8,128)(2,1)} %x_ref.19), channel_id=1, source_target_pairs={{0,8},{8,0},{16,24},{24,16},{32,40},{40,32},{48,56},{56,48},{64,72... | collective-permute-start | bytes 10616840 | tf_op jit(solution)/shard_map/ppermute | solution.py:354
  3.9 5.7 %copy-start.5 = (s32[2,2]{1,0:T(2,128)S(1)}, s32[2,2]{1,0:T(2,128)}, u32[]{:S(2)}) copy-start(s32[2,2]{1,0:T(2,128)} %param.3) | copy-start | bytes 52
  3.9 25.1 %collective-permute-start.3 = (bf16[2,6,3,192,128]{4,3,2,1,0:T(8,128)(2,1)}, bf16[2,6,3,192,128]{4,3,2,1,0:T(8,128)(2,1)S(1)}, u32[]{:S(2)}, u32[]{:S(2)}) collective-permute-start(bf16[2,6,3,192,128]{4,3,2,1,0:T(8,128)(2,1)} %shard_map.28), channel_id=1, source_target_pairs={{0,112},{8,24},{16,0},{24,40},{32,16},{40,56},{48,32},{56,72},{64,... | collective-permute-start | bytes 5308424 | tf_op jit(solution)/shard_map/ppermute | solution.py:362
  8.0 33.8 %collective-permute-start.4 = (bf16[2,4,3,192,128]{4,3,2,1,0:T(8,128)(2,1)}, bf16[2,4,3,192,128]{4,3,2,1,0:T(8,128)(2,1)}, u32[]{:S(2)}, u32[]{:S(2)}) collective-permute-start(bf16[2,4,3,192,128]{4,3,2,1,0:T(8,128)(2,1)} %shard_map.29), channel_id=1, source_target_pairs={{0,112},{8,24},{16,0},{24,40},{32,16},{40,56},{48,32},{56,72},{64,... | collective-permute-start | bytes 3538952 | tf_op jit(solution)/shard_map/ppermute | solution.py:362
  9.7 6.8 %collective-permute-start = (s32[2,2]{1,0:T(2,128)S(1)}, s32[2,2]{1,0:T(2,128)S(1)}, u32[]{:S(2)}, u32[]{:S(2)}) collective-permute-start(s32[2,2]{1,0:T(2,128)S(1)} %copy-done.5), channel_id=1, source_target_pairs={{0,8},{8,0},{16,24},{24,16},{32,40},{40,32},{48,56},{56,48},{64,72... | collective-permute-start | bytes 56 | tf_op jit(solution)/shard_map/ppermute | solution.py:355
  13.8 35.3 %collective-permute-start.5 = (bf16[2,2,3,192,128]{4,3,2,1,0:T(8,128)(2,1)}, bf16[2,2,3,192,128]{4,3,2,1,0:T(8,128)(2,1)S(1)}, u32[]{:S(2)}, u32[]{:S(2)}) collective-permute-start(bf16[2,2,3,192,128]{4,3,2,1,0:T(8,128)(2,1)} %shard_map.30), channel_id=1, source_target_pairs={{0,112},{8,24},{16,0},{24,40},{32,16},{40,56},{48,32},{56,72},{64,... | collective-permute-start | bytes 1769480 | tf_op jit(solution)/shard_map/ppermute | solution.py:362
  15.6 33.5 %copy-start.1 = (f32[192,384]{1,0:T(8,128)}, f32[192,384]{1,0:T(8,128)S(1)}, u32[]{:S(2)}) copy-start(f32[192,384]{1,0:T(8,128)S(1)} %get-tuple-element.57.log_ref) | copy-start | bytes 884740
  15.6 33.5 %copy-start.2 = (f32[192,384]{1,0:T(8,128)}, f32[192,384]{1,0:T(8,128)S(1)}, u32[]{:S(2)}) copy-start(f32[192,384]{1,0:T(8,128)S(1)} %get-tuple-element.58.r_ref) | copy-start | bytes 884740
  16.4 32.7 %copy-start.3 = (bf16[192,192]{1,0:T(8,128)(2,1)}, bf16[192,192]{1,0:T(8,128)(2,1)S(1)}, u32[]{:S(2)}) copy-start(bf16[192,192]{1,0:T(8,128)(2,1)S(1)} %sine_convert_fusion.sines_ref) | copy-start | bytes 221188
  16.4 5.3 %collective-permute-start.1 = (s32[2,2]{1,0:T(2,128)S(1)}, s32[2,2]{1,0:T(2,128)S(1)}, u32[]{:S(2)}, u32[]{:S(2)}) collective-permute-start(s32[2,2]{1,0:T(2,128)S(1)} %collective-permute-done), channel_id=1, source_target_pairs={{0,24},{8,112},{16,40},{24,0},{32,56},{40,16},{48,72},{56,32},{64,... | collective-permute-start | bytes 56 | tf_op jit(solution)/shard_map/ppermute | solution.py:355
  29.0 2.3 %copy-start = (bf16[2,24,192,192]{3,2,1,0:T(8,128)(2,1)S(1)}, bf16[2,24,192,192]{3,2,1,0:T(8,128)(2,1)}, u32[]{:S(2)}) copy-start(bf16[2,24,192,192]{3,2,1,0:T(8,128)(2,1)} %x_ref.19) | copy-start | bytes 10616836
  54.1 17.7 %all-to-all-start = ((bf16[8,24,1536]{2,1,0:T(8,128)(2,1)}), bf16[8,24,1536]{2,1,0:T(8,128)(2,1)S(1)}, u32[]{:S(2)}, u32[]{:S(2)}) async-start(bf16[8,24,1536]{2,1,0:T(8,128)(2,1)} %bitcast.10), calls=%async_computation | async-start | bytes 1179648 | tf_op jit(solution)/shard_map/all_to_all | solution.py:352
  73.5 14.2 %all-to-all-start.1 = ((bf16[8,24,1536]{2,1,0:T(8,128)(2,1)}), bf16[8,24,1536]{2,1,0:T(8,128)(2,1)S(1)}, u32[]{:S(2)}, u32[]{:S(2)}) async-start(bf16[8,24,1536]{2,1,0:T(8,128)(2,1)} %bitcast.3), calls=%async_computation.1 | async-start | bytes 1179648 | tf_op jit(solution)/shard_map/all_to_all | solution.py:352
  87.7 0.8 copy-start.4
  95.3 15.7 %collective-permute-start.6 = (bf16[2,3,3,192,128]{4,3,2,1,0:T(8,128)(2,1)S(1)}, bf16[2,3,3,192,128]{4,3,2,1,0:T(8,128)(2,1)S(1)}, u32[]{:S(2)}, u32[]{:S(2)}) collective-permute-start(bf16[2,3,3,192,128]{4,3,2,1,0:T(8,128)(2,1)S(1)} %get-tuple-element.39), channel_id=1, source_target_pairs={{0,8},{8,0},{16,24},{24,16},{32,40},{40,32},{48,56},{56,48},{64,72... | collective-permute-start | bytes 2654216 | tf_op jit(solution)/shard_map/ppermute | solution.py:386
  97.1 13.9 %collective-permute-start.7 = (bf16[2,3,3,192,128]{4,3,2,1,0:T(8,128)(2,1)S(1)}, bf16[2,3,3,192,128]{4,3,2,1,0:T(8,128)(2,1)S(1)}, u32[]{:S(2)}, u32[]{:S(2)}) collective-permute-start(bf16[2,3,3,192,128]{4,3,2,1,0:T(8,128)(2,1)S(1)} %get-tuple-element.40), channel_id=1, source_target_pairs={{0,16},{8,120},{16,32},{24,8},{32,48},{40,24},{48,64},{56,40},{64,... | collective-permute-start | bytes 2654216 | tf_op jit(solution)/shard_map/ppermute | solution.py:386
  107.6 15.6 %collective-permute-start.12 = (bf16[2,5,3,192,128]{4,3,2,1,0:T(8,128)(2,1)S(1)}, bf16[2,5,3,192,128]{4,3,2,1,0:T(8,128)(2,1)S(1)}, u32[]{:S(2)}, u32[]{:S(2)}) collective-permute-start(bf16[2,5,3,192,128]{4,3,2,1,0:T(8,128)(2,1)S(1)} %get-tuple-element.52), channel_id=1, source_target_pairs={{0,8},{8,0},{16,24},{24,16},{32,40},{40,32},{48,56},{56,48},{64,72... | collective-permute-start | bytes 4423688 | tf_op jit(solution)/shard_map/ppermute | solution.py:386
  107.7 22.0 %collective-permute-start.13 = (bf16[2,5,3,192,128]{4,3,2,1,0:T(8,128)(2,1)S(1)}, bf16[2,5,3,192,128]{4,3,2,1,0:T(8,128)(2,1)S(1)}, u32[]{:S(2)}, u32[]{:S(2)}) collective-permute-start(bf16[2,5,3,192,128]{4,3,2,1,0:T(8,128)(2,1)S(1)} %get-tuple-element.53), channel_id=1, source_target_pairs={{0,16},{8,120},{16,32},{24,8},{32,48},{40,24},{48,64},{56,40},{64,... | collective-permute-start | bytes 4423688 | tf_op jit(solution)/shard_map/ppermute | solution.py:386
  117.7 15.6 %collective-permute-start.10 = (bf16[2,3,3,192,128]{4,3,2,1,0:T(8,128)(2,1)S(1)}, bf16[2,3,3,192,128]{4,3,2,1,0:T(8,128)(2,1)S(1)}, u32[]{:S(2)}, u32[]{:S(2)}) collective-permute-start(bf16[2,3,3,192,128]{4,3,2,1,0:T(8,128)(2,1)S(1)} %get-tuple-element.49), channel_id=1, source_target_pairs={{0,8},{8,0},{16,24},{24,16},{32,40},{40,32},{48,56},{56,48},{64,72... | collective-permute-start | bytes 2654216 | tf_op jit(solution)/shard_map/ppermute | solution.py:386
  119.3 17.4 %collective-permute-start.11 = (bf16[2,3,3,192,128]{4,3,2,1,0:T(8,128)(2,1)S(1)}, bf16[2,3,3,192,128]{4,3,2,1,0:T(8,128)(2,1)S(1)}, u32[]{:S(2)}, u32[]{:S(2)}) collective-permute-start(bf16[2,3,3,192,128]{4,3,2,1,0:T(8,128)(2,1)S(1)} %get-tuple-element.50), channel_id=1, source_target_pairs={{0,16},{8,120},{16,32},{24,8},{32,48},{40,24},{48,64},{56,40},{64,... | collective-permute-start | bytes 2654216 | tf_op jit(solution)/shard_map/ppermute | solution.py:386
  123.0 16.4 %collective-permute-start.8 = (bf16[2,1,3,192,128]{4,3,2,1,0:T(8,128)(2,1)S(1)}, bf16[2,1,3,192,128]{4,3,2,1,0:T(8,128)(2,1)S(1)}, u32[]{:S(2)}, u32[]{:S(2)}) collective-permute-start(bf16[2,1,3,192,128]{4,3,2,1,0:T(8,128)(2,1)S(1)} %get-tuple-element.46), channel_id=1, source_target_pairs={{0,8},{8,0},{16,24},{24,16},{32,40},{40,32},{48,56},{56,48},{64,72... | collective-permute-start | bytes 884744 | tf_op jit(solution)/shard_map/ppermute | solution.py:386
  123.2 16.7 %collective-permute-start.9 = (bf16[2,1,3,192,128]{4,3,2,1,0:T(8,128)(2,1)S(1)}, bf16[2,1,3,192,128]{4,3,2,1,0:T(8,128)(2,1)S(1)}, u32[]{:S(2)}, u32[]{:S(2)}) collective-permute-start(bf16[2,1,3,192,128]{4,3,2,1,0:T(8,128)(2,1)S(1)} %get-tuple-element.47), channel_id=1, source_target_pairs={{0,16},{8,120},{16,32},{24,8},{32,48},{40,24},{48,64},{56,40},{64,... | collective-permute-start | bytes 884744 | tf_op jit(solution)/shard_map/ppermute | solution.py:386

commit v4 on v3

--- a/solution.py
+++ b/solution.py
@@ -15,7 +15,7 @@
 WIDE = PAIRS * NG
 PAIRED = ROWS // 2
 PIECES_IN = (6, 4, 2)
-PIECES_OUT = (1, 3, 5, 3)
+PIECES_OUT = (1, 3, 3, 3, 2)
 WAITS = (2,)
 
 F32 = jnp.float32

time: 143 us -> 143 us (level)
  waiting for transfers between devices: 33.8 us -> 29.8 us
  Pallas kernels: 67.5 us -> 71 us
    ppermute x4 -> x5, waiting for transfers between devices: 3.97 us -> 0.01 us  [shards(): lax.ppermute(zo, 'band', home_way)]
    pallas_call x4 -> x5, Pallas kernels: 26.8 us -> 29.4 us  [back(): call(functools.partial(back_kernel, start, count, first), (count,), [plan...]
    pallas_call x4 -> x5, Pallas kernels: 10.4 us -> 11.3 us  [close(): call(functools.partial(close_kernel, scale), (count,), [planes(same), pac...]
    ppermute x4 -> x5, starting transfers between devices: 7.94 us -> 8.35 us  [shards(): lax.ppermute(zo, 'band', home_way)]
    ppermute x4 -> x5, starting transfers between devices: 3.66 us -> 3.44 us  [shards(): lax.ppermute(so, 'band', across)]
  transfers between devices with their start and end apart: 16 -> 18, of which waited for: 7 -> 5; matrix products, arithmetic and copies ran while one was open for 5% -> 5% of each run, Pallas kernels for 37% -> 41%
where the time goes in v4:
time: 143 us; the launch traced here: 141 us
  Pallas kernels  71 us (50%)
  starting transfers between devices  30.5 us (21%)
  waiting for transfers between devices  29.8 us (21%)
  local copies, waits for them, and re-layouts  8.21 us (6%)
    pallas_call x5, Pallas kernels, back(): call(functools.partial(back_kernel, start, count, first), (count,), [plan...  29.4 us
    pallas_call x3, Pallas kernels, forward(): call(functools.partial(forward_kernel, start, first, last), (count,), [pl...  21.9 us
    all_to_all x2, waiting for transfers between devices, shards(): lax.all_to_all(block, 'grid', split_axis=0, concat_axis=0, tiled=True)  16.9 us
    pallas_call x5, Pallas kernels, close(): call(functools.partial(close_kernel, scale), (count,), [planes(same), pac...  11.3 us
    all_to_all x2, starting transfers between devices, shards(): lax.all_to_all(block, 'grid', split_axis=0, concat_axis=0, tiled=True)  9.9 us
    ppermute x5, starting transfers between devices, shards(): lax.ppermute(zo, 'band', home_way)  8.35 us
    ppermute x3, waiting for transfers between devices, shards(): arrived.append((start, count, lax.ppermute(piece, 'band', out_way)))  7.98 us
    unnamed x14, local copies, waits for them, and re-layouts  7.21 us
  transfers between devices with their start and end apart: 18, of which 5 were waited for; matrix products, arithmetic and copies ran while one was open for 5% of the time, Pallas kernels for 41%

profile of v4, /device:TPU:1, one launch (start us, length us, event | category | flops | bytes accessed | tf_op | source)
XLA Modules:
  0.0 141.2 jit_solution(17515328780967987903)
XLA Ops:
  1.4 2.5 %shard_map.28 = bf16[2,6,3,192,128]{4,3,2,1,0:T(8,128)(2,1)} custom-call(bf16[2,24,192,192]{3,2,1,0:T(8,128)(2,1)} %x_ref.21), custom_call_target="tpu_custom_call" | custom-call | tf_op jit(solution)/shard_map/pallas_call | solution.py:122
  5.7 2.2 %shard_map.29 = bf16[2,4,3,192,128]{4,3,2,1,0:T(8,128)(2,1)} custom-call(bf16[2,24,192,192]{3,2,1,0:T(8,128)(2,1)} %x_ref.21), custom_call_target="tpu_custom_call" | custom-call | tf_op jit(solution)/shard_map/pallas_call | solution.py:122
  9.7 2.2 %collective-permute-start = (s32[2,2]{1,0:T(2,128)S(1)}, s32[2,2]{1,0:T(2,128)S(1)}, u32[]{:S(2)}, u32[]{:S(2)}) collective-permute-start(s32[2,2]{1,0:T(2,128)S(1)} %copy-done.5), channel_id=1, source_target_pairs={{0,8},{8,0},{16,24},{24,16},{32,40},{40,32},{48,56},{56,48},{64,72... | collective-permute-start | bytes 56 | tf_op jit(solution)/shard_map/ppermute | solution.py:355
  16.7 5.0 %collective-permute-done.1 = s32[2,2]{1,0:T(2,128)S(1)} collective-permute-done((s32[2,2]{1,0:T(2,128)S(1)}, s32[2,2]{1,0:T(2,128)S(1)}, u32[]{:S(2)}, u32[]{:S(2)}) %collective-permute-start.1) | collective-permute-done | bytes 48 | tf_op jit(solution)/shard_map/ppermute | solution.py:355
  21.9 7.1 %collective-permute-done.3.z_ref = bf16[2,6,3,192,128]{4,3,2,1,0:T(8,128)(2,1)S(1)} collective-permute-done((bf16[2,6,3,192,128]{4,3,2,1,0:T(8,128)(2,1)}, bf16[2,6,3,192,128]{4,3,2,1,0:T(8,128)(2,1)S(1)}, u32[]{:S(2)}, u32[]{:S(2)}) %collective-permute-start.3) | collective-permute-done | bytes 1769504 | tf_op jit(solution)/shard_map/ppermute | solution.py:362
  29.0 2.3 %copy-done = bf16[2,24,192,192]{3,2,1,0:T(8,128)(2,1)S(1)} copy-done((bf16[2,24,192,192]{3,2,1,0:T(8,128)(2,1)S(1)}, bf16[2,24,192,192]{3,2,1,0:T(8,128)(2,1)}, u32[]{:S(2)}) %copy-start) | copy-done | bytes 3538968
  31.3 9.6 %shard_map.31 = (bf16[24,192,768]{2,1,0:T(8,128)(2,1)}, f32[192,768]{1,0:T(8,128)S(1)}, f32[192,768]{1,0:T(8,128)S(1)}) custom-call(s32[5]{0:T(128)S(1)} %pad_add_fusion.table, bf16[2,24,192,192]{3,2,1,0:T(8,128)(2,1)S(1)} %copy-done, bf16[2,24,192,192]{3,2,1,0:T(8,128)(2,1)} %collective-permute-done.2.s_ref, ...), custom_call_target="tpu_custom_call" | custom-call | tf_op jit(solution)/shard_map/pallas_call | solution.py:182
  41.7 7.4 %shard_map.32 = (bf16[24,192,768]{2,1,0:T(8,128)(2,1)}, f32[192,768]{1,0:T(8,128)S(1)}, f32[192,768]{1,0:T(8,128)S(1)}) custom-call(s32[5]{0:T(128)S(1)} %pad_add_fusion.table, bf16[2,24,192,192]{3,2,1,0:T(8,128)(2,1)S(1)} %copy-done, bf16[2,24,192,192]{3,2,1,0:T(8,128)(2,1)} %collective-permute-done.2.s_ref, ...), custom_call_target="tpu_custom_call", output_to_operand_aliasing={{0}: (9, {})} | custom-call | tf_op jit(solution)/shard_map/pallas_call | solution.py:182
  49.1 5.0 %shard_map.33 = (bf16[24,192,768]{2,1,0:T(8,128)(2,1)}, bf16[192,1536]{1,0:T(8,128)(2,1)}) custom-call(s32[5]{0:T(128)S(1)} %pad_add_fusion.table, bf16[2,24,192,192]{3,2,1,0:T(8,128)(2,1)S(1)} %copy-done, bf16[2,24,192,192]{3,2,1,0:T(8,128)(2,1)} %collective-permute-done.2.s_ref, ...), custom_call_target="tpu_custom_call", output_to_operand_aliasing={{0}: (9, {})} | custom-call | tf_op jit(solution)/shard_map/pallas_call | solution.py:182
  54.1 6.4 %all-to-all-start = ((bf16[8,24,1536]{2,1,0:T(8,128)(2,1)}), bf16[8,24,1536]{2,1,0:T(8,128)(2,1)S(1)}, u32[]{:S(2)}, u32[]{:S(2)}) async-start(bf16[8,24,1536]{2,1,0:T(8,128)(2,1)} %bitcast.11), calls=%async_computation | async-start | bytes 1179648 | tf_op jit(solution)/shard_map/all_to_all | solution.py:352
  60.7 11.1 %all-to-all-done = bf16[8,24,1536]{2,1,0:T(8,128)(2,1)S(1)} async-done(((bf16[8,24,1536]{2,1,0:T(8,128)(2,1)}), bf16[8,24,1536]{2,1,0:T(8,128)(2,1)S(1)}, u32[]{:S(2)}, u32[]{:S(2)}) %all-to-all-start) | async-done | bytes 589856 | tf_op jit(solution)/shard_map/all_to_all | solution.py:352
  73.5 3.5 %all-to-all-start.1 = ((bf16[8,24,1536]{2,1,0:T(8,128)(2,1)}), bf16[8,24,1536]{2,1,0:T(8,128)(2,1)S(1)}, u32[]{:S(2)}, u32[]{:S(2)}) async-start(bf16[8,24,1536]{2,1,0:T(8,128)(2,1)} %bitcast.3), calls=%async_computation.1 | async-start | bytes 1179648 | tf_op jit(solution)/shard_map/all_to_all | solution.py:352
  78.5 2.5 %constant_dynamic-update-slice_fusion.1 = bf16[2,12,3,192,128]{4,3,2,1,0:T(8,128)(2,1)} fusion(bf16[2,12,3,192,128]{4,3,2,1,0:T(8,128)(2,1)} %constant_dynamic-update-slice_fusion.2, bf16[2,4,3,192,128]{4,3,2,1,0:T(8,128)(2,1)} %collective-permute-done.4.z_ref), kind=kLoop, calls=%fused_computation.13 | loop fusion | bytes 2359296
  81.9 5.8 %all-to-all-done.1 = bf16[8,24,1536]{2,1,0:T(8,128)(2,1)S(1)} async-done(((bf16[8,24,1536]{2,1,0:T(8,128)(2,1)}), bf16[8,24,1536]{2,1,0:T(8,128)(2,1)S(1)}, u32[]{:S(2)}, u32[]{:S(2)}) %all-to-all-start.1) | async-done | bytes 589856 | tf_op jit(solution)/shard_map/all_to_all | solution.py:352
  88.6 5.3 %shard_map.35 = (bf16[2,4,192,192]{3,2,1,0:T(8,128)(2,1)S(1)}, bf16[2,2,3,192,128]{4,3,2,1,0:T(8,128)(2,1)S(1)}, bf16[2,2,3,192,128]{4,3,2,1,0:T(8,128)(2,1)S(1)}, f32[192,768]{1,0:T(8,128)S(1)}) custom-call(s32[5]{0:T(128)S(1)} %pad_add_fusion.table, bf16[2,24,192,192]{3,2,1,0:T(8,128)(2,1)} %x_ref.21, ...), custom_call_target="tpu_custom_call" | custom-call | tf_op jit(solution)/shard_map/pallas_call | solution.py:297
  96.5 6.8 %shard_map.36 = (bf16[2,6,192,192]{3,2,1,0:T(8,128)(2,1)S(1)}, bf16[2,3,3,192,128]{4,3,2,1,0:T(8,128)(2,1)S(1)}, bf16[2,3,3,192,128]{4,3,2,1,0:T(8,128)(2,1)S(1)}, f32[192,768]{1,0:T(8,128)S(1)}) custom-call(s32[5]{0:T(128)S(1)} %pad_add_fusion.table, bf16[2,24,192,192]{3,2,1,0:T(8,128)(2,1)} %x_ref.21, ...), custom_call_target="tpu_custom_call" | custom-call | tf_op jit(solution)/shard_map/pallas_call | solution.py:297
  103.4 3.3 %collective-permute-start.15 = (bf16[2,3,3,192,128]{4,3,2,1,0:T(8,128)(2,1)S(1)}, bf16[2,3,3,192,128]{4,3,2,1,0:T(8,128)(2,1)S(1)}, u32[]{:S(2)}, u32[]{:S(2)}) collective-permute-start(bf16[2,3,3,192,128]{4,3,2,1,0:T(8,128)(2,1)S(1)} %get-tuple-element.61), channel_id=1, source_target_pairs={{0,16},{8,120},{16,32},{24,8},{32,48},{40,24},{48,64},{56,40},{64,... | collective-permute-start | bytes 2654216 | tf_op jit(solution)/shard_map/ppermute | solution.py:386
  106.7 6.8 %shard_map.37 = (bf16[2,6,192,192]{3,2,1,0:T(8,128)(2,1)S(1)}, bf16[2,3,3,192,128]{4,3,2,1,0:T(8,128)(2,1)S(1)}, bf16[2,3,3,192,128]{4,3,2,1,0:T(8,128)(2,1)S(1)}, f32[192,768]{1,0:T(8,128)S(1)}) custom-call(s32[5]{0:T(128)S(1)} %pad_add_fusion.table, bf16[2,24,192,192]{3,2,1,0:T(8,128)(2,1)} %x_ref.21, ...), custom_call_target="tpu_custom_call" | custom-call | tf_op jit(solution)/shard_map/pallas_call | solution.py:297
  114.8 6.8 %shard_map.38 = (bf16[2,6,192,192]{3,2,1,0:T(8,128)(2,1)S(1)}, bf16[2,3,3,192,128]{4,3,2,1,0:T(8,128)(2,1)S(1)}, bf16[2,3,3,192,128]{4,3,2,1,0:T(8,128)(2,1)S(1)}, f32[192,768]{1,0:T(8,128)S(1)}) custom-call(s32[5]{0:T(128)S(1)} %pad_add_fusion.table, bf16[2,24,192,192]{3,2,1,0:T(8,128)(2,1)} %x_ref.21, ...), custom_call_target="tpu_custom_call" | custom-call | tf_op jit(solution)/shard_map/pallas_call | solution.py:297
  121.8 3.8 %collective-permute-start.11 = (bf16[2,3,3,192,128]{4,3,2,1,0:T(8,128)(2,1)S(1)}, bf16[2,3,3,192,128]{4,3,2,1,0:T(8,128)(2,1)S(1)}, u32[]{:S(2)}, u32[]{:S(2)}) collective-permute-start(bf16[2,3,3,192,128]{4,3,2,1,0:T(8,128)(2,1)S(1)} %get-tuple-element.55), channel_id=1, source_target_pairs={{0,16},{8,120},{16,32},{24,8},{32,48},{40,24},{48,64},{56,40},{64,... | collective-permute-start | bytes 2654216 | tf_op jit(solution)/shard_map/ppermute | solution.py:386
  125.7 3.7 %shard_map.39 = (bf16[2,2,192,192]{3,2,1,0:T(8,128)(2,1)S(1)}, bf16[2,1,3,192,128]{4,3,2,1,0:T(8,128)(2,1)S(1)}, bf16[2,1,3,192,128]{4,3,2,1,0:T(8,128)(2,1)S(1)}) custom-call(s32[5]{0:T(128)S(1)} %pad_add_fusion.table, bf16[2,24,192,192]{3,2,1,0:T(8,128)(2,1)} %x_ref.21, bf16[2,24,192,192]{3,2,1,0:T(8,128)(2,1)} %collective-permute-done.2.s_ref, ...), custom_call_target="tpu_custom_call" | custom-call | tf_op jit(solution)/shard_map/pallas_call | solution.py:297
  131.8 2.6 %shard_map.41.refs_0_ = bf16[2,24,192,192]{3,2,1,0:T(8,128)(2,1)} custom-call(s32[5]{0:T(128)S(1)} %pad_add_fusion.table, bf16[2,6,192,192]{3,2,1,0:T(8,128)(2,1)S(1)} %get-tuple-element.59.x_ref, bf16[2,3,3,192,128]{4,3,2,1,0:T(8,128)(2,1)S(1)} %collective-permute-done.14.s_ref, ...), custom_call_target="tpu_custom_call", output_to_operand_aliasing={{}: (4, {})} | custom-call | tf_op jit(solution)/shard_map/pallas_call | solution.py:330
  134.4 2.6 %shard_map.42.refs_0_ = bf16[2,24,192,192]{3,2,1,0:T(8,128)(2,1)} custom-call(s32[5]{0:T(128)S(1)} %pad_add_fusion.table, bf16[2,6,192,192]{3,2,1,0:T(8,128)(2,1)S(1)} %get-tuple-element.56.x_ref, bf16[2,3,3,192,128]{4,3,2,1,0:T(8,128)(2,1)S(1)} %collective-permute-done.12.s_ref, ...), custom_call_target="tpu_custom_call", output_to_operand_aliasing={{}: (4, {})} | custom-call | tf_op jit(solution)/shard_map/pallas_call | solution.py:330
  137.1 2.6 %shard_map.43.refs_0_ = bf16[2,24,192,192]{3,2,1,0:T(8,128)(2,1)} custom-call(s32[5]{0:T(128)S(1)} %pad_add_fusion.table, bf16[2,6,192,192]{3,2,1,0:T(8,128)(2,1)S(1)} %get-tuple-element.53.x_ref, bf16[2,3,3,192,128]{4,3,2,1,0:T(8,128)(2,1)S(1)} %collective-permute-done.10.s_ref, ...), custom_call_target="tpu_custom_call", output_to_operand_aliasing={{}: (4, {})} | custom-call | tf_op jit(solution)/shard_map/pallas_call | solution.py:330
  (55 shorter events, 24.0 us)
Async XLA Ops:
  0.0 29.0 %collective-permute-start.2 = (bf16[2,24,192,192]{3,2,1,0:T(8,128)(2,1)}, bf16[2,24,192,192]{3,2,1,0:T(8,128)(2,1)}, u32[]{:S(2)}, u32[]{:S(2)}) collective-permute-start(bf16[2,24,192,192]{3,2,1,0:T(8,128)(2,1)} %x_ref.21), channel_id=1, source_target_pairs={{0,8},{8,0},{16,24},{24,16},{32,40},{40,32},{48,56},{56,48},{64,72... | collective-permute-start | bytes 10616840 | tf_op jit(solution)/shard_map/ppermute | solution.py:354
  3.9 5.7 %copy-start.5 = (s32[2,2]{1,0:T(2,128)S(1)}, s32[2,2]{1,0:T(2,128)}, u32[]{:S(2)}) copy-start(s32[2,2]{1,0:T(2,128)} %param.3) | copy-start | bytes 52
  3.9 25.1 %collective-permute-start.3 = (bf16[2,6,3,192,128]{4,3,2,1,0:T(8,128)(2,1)}, bf16[2,6,3,192,128]{4,3,2,1,0:T(8,128)(2,1)S(1)}, u32[]{:S(2)}, u32[]{:S(2)}) collective-permute-start(bf16[2,6,3,192,128]{4,3,2,1,0:T(8,128)(2,1)} %shard_map.28), channel_id=1, source_target_pairs={{0,112},{8,24},{16,0},{24,40},{32,16},{40,56},{48,32},{56,72},{64,... | collective-permute-start | bytes 5308424 | tf_op jit(solution)/shard_map/ppermute | solution.py:362
  8.0 33.8 %collective-permute-start.4 = (bf16[2,4,3,192,128]{4,3,2,1,0:T(8,128)(2,1)}, bf16[2,4,3,192,128]{4,3,2,1,0:T(8,128)(2,1)}, u32[]{:S(2)}, u32[]{:S(2)}) collective-permute-start(bf16[2,4,3,192,128]{4,3,2,1,0:T(8,128)(2,1)} %shard_map.29), channel_id=1, source_target_pairs={{0,112},{8,24},{16,0},{24,40},{32,16},{40,56},{48,32},{56,72},{64,... | collective-permute-start | bytes 3538952 | tf_op jit(solution)/shard_map/ppermute | solution.py:362
  9.7 6.8 %collective-permute-start = (s32[2,2]{1,0:T(2,128)S(1)}, s32[2,2]{1,0:T(2,128)S(1)}, u32[]{:S(2)}, u32[]{:S(2)}) collective-permute-start(s32[2,2]{1,0:T(2,128)S(1)} %copy-done.5), channel_id=1, source_target_pairs={{0,8},{8,0},{16,24},{24,16},{32,40},{40,32},{48,56},{56,48},{64,72... | collective-permute-start | bytes 56 | tf_op jit(solution)/shard_map/ppermute | solution.py:355
  13.8 35.3 %collective-permute-start.5 = (bf16[2,2,3,192,128]{4,3,2,1,0:T(8,128)(2,1)}, bf16[2,2,3,192,128]{4,3,2,1,0:T(8,128)(2,1)S(1)}, u32[]{:S(2)}, u32[]{:S(2)}) collective-permute-start(bf16[2,2,3,192,128]{4,3,2,1,0:T(8,128)(2,1)} %shard_map.30), channel_id=1, source_target_pairs={{0,112},{8,24},{16,0},{24,40},{32,16},{40,56},{48,32},{56,72},{64,... | collective-permute-start | bytes 1769480 | tf_op jit(solution)/shard_map/ppermute | solution.py:362
  15.6 33.5 %copy-start.1 = (f32[192,384]{1,0:T(8,128)}, f32[192,384]{1,0:T(8,128)S(1)}, u32[]{:S(2)}) copy-start(f32[192,384]{1,0:T(8,128)S(1)} %get-tuple-element.65.log_ref) | copy-start | bytes 884740
  15.6 33.5 %copy-start.2 = (f32[192,384]{1,0:T(8,128)}, f32[192,384]{1,0:T(8,128)S(1)}, u32[]{:S(2)}) copy-start(f32[192,384]{1,0:T(8,128)S(1)} %get-tuple-element.66.r_ref) | copy-start | bytes 884740
  16.4 32.7 %copy-start.3 = (bf16[192,192]{1,0:T(8,128)(2,1)}, bf16[192,192]{1,0:T(8,128)(2,1)S(1)}, u32[]{:S(2)}) copy-start(bf16[192,192]{1,0:T(8,128)(2,1)S(1)} %sine_convert_fusion.sines_ref) | copy-start | bytes 221188
  16.4 5.3 %collective-permute-start.1 = (s32[2,2]{1,0:T(2,128)S(1)}, s32[2,2]{1,0:T(2,128)S(1)}, u32[]{:S(2)}, u32[]{:S(2)}) collective-permute-start(s32[2,2]{1,0:T(2,128)S(1)} %collective-permute-done), channel_id=1, source_target_pairs={{0,24},{8,112},{16,40},{24,0},{32,56},{40,16},{48,72},{56,32},{64,... | collective-permute-start | bytes 56 | tf_op jit(solution)/shard_map/ppermute | solution.py:355
  29.0 2.3 %copy-start = (bf16[2,24,192,192]{3,2,1,0:T(8,128)(2,1)S(1)}, bf16[2,24,192,192]{3,2,1,0:T(8,128)(2,1)}, u32[]{:S(2)}) copy-start(bf16[2,24,192,192]{3,2,1,0:T(8,128)(2,1)} %x_ref.21) | copy-start | bytes 10616836
  54.1 17.7 %all-to-all-start = ((bf16[8,24,1536]{2,1,0:T(8,128)(2,1)}), bf16[8,24,1536]{2,1,0:T(8,128)(2,1)S(1)}, u32[]{:S(2)}, u32[]{:S(2)}) async-start(bf16[8,24,1536]{2,1,0:T(8,128)(2,1)} %bitcast.11), calls=%async_computation | async-start | bytes 1179648 | tf_op jit(solution)/shard_map/all_to_all | solution.py:352
  73.5 14.2 %all-to-all-start.1 = ((bf16[8,24,1536]{2,1,0:T(8,128)(2,1)}), bf16[8,24,1536]{2,1,0:T(8,128)(2,1)S(1)}, u32[]{:S(2)}, u32[]{:S(2)}) async-start(bf16[8,24,1536]{2,1,0:T(8,128)(2,1)} %bitcast.3), calls=%async_computation.1 | async-start | bytes 1179648 | tf_op jit(solution)/shard_map/all_to_all | solution.py:352
  87.7 0.8 copy-start.4
  93.9 12.8 %collective-permute-start.6 = (bf16[2,2,3,192,128]{4,3,2,1,0:T(8,128)(2,1)S(1)}, bf16[2,2,3,192,128]{4,3,2,1,0:T(8,128)(2,1)S(1)}, u32[]{:S(2)}, u32[]{:S(2)}) collective-permute-start(bf16[2,2,3,192,128]{4,3,2,1,0:T(8,128)(2,1)S(1)} %get-tuple-element.43), channel_id=1, source_target_pairs={{0,8},{8,0},{16,24},{24,16},{32,40},{40,32},{48,56},{56,48},{64,72... | collective-permute-start | bytes 1769480 | tf_op jit(solution)/shard_map/ppermute | solution.py:386
  95.7 11.0 %collective-permute-start.7 = (bf16[2,2,3,192,128]{4,3,2,1,0:T(8,128)(2,1)S(1)}, bf16[2,2,3,192,128]{4,3,2,1,0:T(8,128)(2,1)S(1)}, u32[]{:S(2)}, u32[]{:S(2)}) collective-permute-start(bf16[2,2,3,192,128]{4,3,2,1,0:T(8,128)(2,1)S(1)} %get-tuple-element.44), channel_id=1, source_target_pairs={{0,16},{8,120},{16,32},{24,8},{32,48},{40,24},{48,64},{56,40},{64,... | collective-permute-start | bytes 1769480 | tf_op jit(solution)/shard_map/ppermute | solution.py:386
  103.3 18.5 %collective-permute-start.14 = (bf16[2,3,3,192,128]{4,3,2,1,0:T(8,128)(2,1)S(1)}, bf16[2,3,3,192,128]{4,3,2,1,0:T(8,128)(2,1)S(1)}, u32[]{:S(2)}, u32[]{:S(2)}) collective-permute-start(bf16[2,3,3,192,128]{4,3,2,1,0:T(8,128)(2,1)S(1)} %get-tuple-element.60), channel_id=1, source_target_pairs={{0,8},{8,0},{16,24},{24,16},{32,40},{40,32},{48,56},{56,48},{64,72... | collective-permute-start | bytes 2654216 | tf_op jit(solution)/shard_map/ppermute | solution.py:386
  103.4 26.0 %collective-permute-start.15 = (bf16[2,3,3,192,128]{4,3,2,1,0:T(8,128)(2,1)S(1)}, bf16[2,3,3,192,128]{4,3,2,1,0:T(8,128)(2,1)S(1)}, u32[]{:S(2)}, u32[]{:S(2)}) collective-permute-start(bf16[2,3,3,192,128]{4,3,2,1,0:T(8,128)(2,1)S(1)} %get-tuple-element.61), channel_id=1, source_target_pairs={{0,16},{8,120},{16,32},{24,8},{32,48},{40,24},{48,64},{56,40},{64,... | collective-permute-start | bytes 2654216 | tf_op jit(solution)/shard_map/ppermute | solution.py:386
  113.5 16.0 %collective-permute-start.12 = (bf16[2,3,3,192,128]{4,3,2,1,0:T(8,128)(2,1)S(1)}, bf16[2,3,3,192,128]{4,3,2,1,0:T(8,128)(2,1)S(1)}, u32[]{:S(2)}, u32[]{:S(2)}) collective-permute-start(bf16[2,3,3,192,128]{4,3,2,1,0:T(8,128)(2,1)S(1)} %get-tuple-element.57), channel_id=1, source_target_pairs={{0,8},{8,0},{16,24},{24,16},{32,40},{40,32},{48,56},{56,48},{64,72... | collective-permute-start | bytes 2654216 | tf_op jit(solution)/shard_map/ppermute | solution.py:386
  114.8 19.6 %collective-permute-start.13 = (bf16[2,3,3,192,128]{4,3,2,1,0:T(8,128)(2,1)S(1)}, bf16[2,3,3,192,128]{4,3,2,1,0:T(8,128)(2,1)S(1)}, u32[]{:S(2)}, u32[]{:S(2)}) collective-permute-start(bf16[2,3,3,192,128]{4,3,2,1,0:T(8,128)(2,1)S(1)} %get-tuple-element.58), channel_id=1, source_target_pairs={{0,16},{8,120},{16,32},{24,8},{32,48},{40,24},{48,64},{56,40},{64,... | collective-permute-start | bytes 2654216 | tf_op jit(solution)/shard_map/ppermute | solution.py:386
  121.6 15.4 %collective-permute-start.10 = (bf16[2,3,3,192,128]{4,3,2,1,0:T(8,128)(2,1)S(1)}, bf16[2,3,3,192,128]{4,3,2,1,0:T(8,128)(2,1)S(1)}, u32[]{:S(2)}, u32[]{:S(2)}) collective-permute-start(bf16[2,3,3,192,128]{4,3,2,1,0:T(8,128)(2,1)S(1)} %get-tuple-element.54), channel_id=1, source_target_pairs={{0,8},{8,0},{16,24},{24,16},{32,40},{40,32},{48,56},{56,48},{64,72... | collective-permute-start | bytes 2654216 | tf_op jit(solution)/shard_map/ppermute | solution.py:386
  121.8 15.2 %collective-permute-start.11 = (bf16[2,3,3,192,128]{4,3,2,1,0:T(8,128)(2,1)S(1)}, bf16[2,3,3,192,128]{4,3,2,1,0:T(8,128)(2,1)S(1)}, u32[]{:S(2)}, u32[]{:S(2)}) collective-permute-start(bf16[2,3,3,192,128]{4,3,2,1,0:T(8,128)(2,1)S(1)} %get-tuple-element.55), channel_id=1, source_target_pairs={{0,16},{8,120},{16,32},{24,8},{32,48},{40,24},{48,64},{56,40},{64,... | collective-permute-start | bytes 2654216 | tf_op jit(solution)/shard_map/ppermute | solution.py:386
  129.4 10.3 %collective-permute-start.8 = (bf16[2,1,3,192,128]{4,3,2,1,0:T(8,128)(2,1)S(1)}, bf16[2,1,3,192,128]{4,3,2,1,0:T(8,128)(2,1)S(1)}, u32[]{:S(2)}, u32[]{:S(2)}) collective-permute-start(bf16[2,1,3,192,128]{4,3,2,1,0:T(8,128)(2,1)S(1)} %get-tuple-element.51), channel_id=1, source_target_pairs={{0,8},{8,0},{16,24},{24,16},{32,40},{40,32},{48,56},{56,48},{64,72... | collective-permute-start | bytes 884744 | tf_op jit(solution)/shard_map/ppermute | solution.py:386
  129.5 10.2 %collective-permute-start.9 = (bf16[2,1,3,192,128]{4,3,2,1,0:T(8,128)(2,1)S(1)}, bf16[2,1,3,192,128]{4,3,2,1,0:T(8,128)(2,1)S(1)}, u32[]{:S(2)}, u32[]{:S(2)}) collective-permute-start(bf16[2,1,3,192,128]{4,3,2,1,0:T(8,128)(2,1)S(1)} %get-tuple-element.52), channel_id=1, source_target_pairs={{0,16},{8,120},{16,32},{24,8},{32,48},{40,24},{48,64},{56,40},{64,... | collective-permute-start | bytes 884744 | tf_op jit(solution)/shard_map/ppermute | solution.py:386

commit v5 on v4

--- a/solution.py
+++ b/solution.py
@@ -15,7 +15,7 @@
 WIDE = PAIRS * NG
 PAIRED = ROWS // 2
 PIECES_IN = (6, 4, 2)
-PIECES_OUT = (1, 3, 3, 3, 2)
+PIECES_OUT = (1, 1, 4, 4, 2)
 WAITS = (2,)
 
 F32 = jnp.float32

time: 143 us -> 143 us (level)
  transfers between devices with their start and end apart: 18 -> 18, of which waited for: 5 -> 6; matrix products, arithmetic and copies ran while one was open for 5% -> 5% of each run, Pallas kernels for 41% -> 40%
where the time goes in v5:
time: 143 us; the launch traced here: 142 us
  Pallas kernels  70.4 us (49%)
  waiting for transfers between devices  31.2 us (22%)
  starting transfers between devices  30.3 us (21%)
  local copies, waits for them, and re-layouts  8.21 us (6%)
    pallas_call x5, Pallas kernels, back(): call(functools.partial(back_kernel, start, count, first), (count,), [plan...  29.3 us
    pallas_call x3, Pallas kernels, forward(): call(functools.partial(forward_kernel, start, first, last), (count,), [pl...  21.9 us
    all_to_all x2, waiting for transfers between devices, shards(): lax.all_to_all(block, 'grid', split_axis=0, concat_axis=0, tiled=True)  16.9 us
    pallas_call x5, Pallas kernels, close(): call(functools.partial(close_kernel, scale), (count,), [planes(same), pac...  10.8 us
    all_to_all x2, starting transfers between devices, shards(): lax.all_to_all(block, 'grid', split_axis=0, concat_axis=0, tiled=True)  9.9 us
    ppermute x5, starting transfers between devices, shards(): lax.ppermute(zo, 'band', home_way)  9.57 us
    ppermute x3, waiting for transfers between devices, shards(): arrived.append((start, count, lax.ppermute(piece, 'band', out_way)))  7.98 us
    unnamed x14, local copies, waits for them, and re-layouts  7.21 us
  transfers between devices with their start and end apart: 18, of which 6 were waited for; matrix products, arithmetic and copies ran while one was open for 5% of the time, Pallas kernels for 40%

profile of v5, /device:TPU:1, one launch (start us, length us, event | category | flops | bytes accessed | tf_op | source)
XLA Modules:
  0.0 141.8 jit_solution(4788401067991452060)
XLA Ops:
  1.4 2.5 %shard_map.28 = bf16[2,6,3,192,128]{4,3,2,1,0:T(8,128)(2,1)} custom-call(bf16[2,24,192,192]{3,2,1,0:T(8,128)(2,1)} %x_ref.21), custom_call_target="tpu_custom_call" | custom-call | tf_op jit(solution)/shard_map/pallas_call | solution.py:122
  5.7 2.2 %shard_map.29 = bf16[2,4,3,192,128]{4,3,2,1,0:T(8,128)(2,1)} custom-call(bf16[2,24,192,192]{3,2,1,0:T(8,128)(2,1)} %x_ref.21), custom_call_target="tpu_custom_call" | custom-call | tf_op jit(solution)/shard_map/pallas_call | solution.py:122
  9.7 2.2 %collective-permute-start = (s32[2,2]{1,0:T(2,128)S(1)}, s32[2,2]{1,0:T(2,128)S(1)}, u32[]{:S(2)}, u32[]{:S(2)}) collective-permute-start(s32[2,2]{1,0:T(2,128)S(1)} %copy-done.5), channel_id=1, source_target_pairs={{0,8},{8,0},{16,24},{24,16},{32,40},{40,32},{48,56},{56,48},{64,72... | collective-permute-start | bytes 56 | tf_op jit(solution)/shard_map/ppermute | solution.py:355
  11.8 2.0 %shard_map.30 = bf16[2,2,3,192,128]{4,3,2,1,0:T(8,128)(2,1)} custom-call(bf16[2,24,192,192]{3,2,1,0:T(8,128)(2,1)} %x_ref.21), custom_call_target="tpu_custom_call" | custom-call | tf_op jit(solution)/shard_map/pallas_call | solution.py:122
  16.7 5.0 %collective-permute-done.1 = s32[2,2]{1,0:T(2,128)S(1)} collective-permute-done((s32[2,2]{1,0:T(2,128)S(1)}, s32[2,2]{1,0:T(2,128)S(1)}, u32[]{:S(2)}, u32[]{:S(2)}) %collective-permute-start.1) | collective-permute-done | bytes 48 | tf_op jit(solution)/shard_map/ppermute | solution.py:355
  21.9 7.1 %collective-permute-done.3.z_ref = bf16[2,6,3,192,128]{4,3,2,1,0:T(8,128)(2,1)S(1)} collective-permute-done((bf16[2,6,3,192,128]{4,3,2,1,0:T(8,128)(2,1)}, bf16[2,6,3,192,128]{4,3,2,1,0:T(8,128)(2,1)S(1)}, u32[]{:S(2)}, u32[]{:S(2)}) %collective-permute-start.3) | collective-permute-done | bytes 1769504 | tf_op jit(solution)/shard_map/ppermute | solution.py:362
  29.0 2.3 %copy-done = bf16[2,24,192,192]{3,2,1,0:T(8,128)(2,1)S(1)} copy-done((bf16[2,24,192,192]{3,2,1,0:T(8,128)(2,1)S(1)}, bf16[2,24,192,192]{3,2,1,0:T(8,128)(2,1)}, u32[]{:S(2)}) %copy-start) | copy-done | bytes 3538968
  31.3 9.6 %shard_map.31 = (bf16[24,192,768]{2,1,0:T(8,128)(2,1)}, f32[192,768]{1,0:T(8,128)S(1)}, f32[192,768]{1,0:T(8,128)S(1)}) custom-call(s32[5]{0:T(128)S(1)} %pad_add_fusion.table, bf16[2,24,192,192]{3,2,1,0:T(8,128)(2,1)S(1)} %copy-done, bf16[2,24,192,192]{3,2,1,0:T(8,128)(2,1)} %collective-permute-done.2.s_ref, ...), custom_call_target="tpu_custom_call" | custom-call | tf_op jit(solution)/shard_map/pallas_call | solution.py:182
  41.7 7.4 %shard_map.32 = (bf16[24,192,768]{2,1,0:T(8,128)(2,1)}, f32[192,768]{1,0:T(8,128)S(1)}, f32[192,768]{1,0:T(8,128)S(1)}) custom-call(s32[5]{0:T(128)S(1)} %pad_add_fusion.table, bf16[2,24,192,192]{3,2,1,0:T(8,128)(2,1)S(1)} %copy-done, bf16[2,24,192,192]{3,2,1,0:T(8,128)(2,1)} %collective-permute-done.2.s_ref, ...), custom_call_target="tpu_custom_call", output_to_operand_aliasing={{0}: (9, {})} | custom-call | tf_op jit(solution)/shard_map/pallas_call | solution.py:182
  49.1 5.0 %shard_map.33 = (bf16[24,192,768]{2,1,0:T(8,128)(2,1)}, bf16[192,1536]{1,0:T(8,128)(2,1)}) custom-call(s32[5]{0:T(128)S(1)} %pad_add_fusion.table, bf16[2,24,192,192]{3,2,1,0:T(8,128)(2,1)S(1)} %copy-done, bf16[2,24,192,192]{3,2,1,0:T(8,128)(2,1)} %collective-permute-done.2.s_ref, ...), custom_call_target="tpu_custom_call", output_to_operand_aliasing={{0}: (9, {})} | custom-call | tf_op jit(solution)/shard_map/pallas_call | solution.py:182
  54.1 6.4 %all-to-all-start = ((bf16[8,24,1536]{2,1,0:T(8,128)(2,1)}), bf16[8,24,1536]{2,1,0:T(8,128)(2,1)S(1)}, u32[]{:S(2)}, u32[]{:S(2)}) async-start(bf16[8,24,1536]{2,1,0:T(8,128)(2,1)} %bitcast.11), calls=%async_computation | async-start | bytes 1179648 | tf_op jit(solution)/shard_map/all_to_all | solution.py:352
  60.7 11.1 %all-to-all-done = bf16[8,24,1536]{2,1,0:T(8,128)(2,1)S(1)} async-done(((bf16[8,24,1536]{2,1,0:T(8,128)(2,1)}), bf16[8,24,1536]{2,1,0:T(8,128)(2,1)S(1)}, u32[]{:S(2)}, u32[]{:S(2)}) %all-to-all-start) | async-done | bytes 589856 | tf_op jit(solution)/shard_map/all_to_all | solution.py:352
  73.5 3.5 %all-to-all-start.1 = ((bf16[8,24,1536]{2,1,0:T(8,128)(2,1)}), bf16[8,24,1536]{2,1,0:T(8,128)(2,1)S(1)}, u32[]{:S(2)}, u32[]{:S(2)}) async-start(bf16[8,24,1536]{2,1,0:T(8,128)(2,1)} %bitcast.3), calls=%async_computation.1 | async-start | bytes 1179648 | tf_op jit(solution)/shard_map/all_to_all | solution.py:352
  78.5 2.5 %constant_dynamic-update-slice_fusion.1 = bf16[2,12,3,192,128]{4,3,2,1,0:T(8,128)(2,1)} fusion(bf16[2,12,3,192,128]{4,3,2,1,0:T(8,128)(2,1)} %constant_dynamic-update-slice_fusion.2, bf16[2,4,3,192,128]{4,3,2,1,0:T(8,128)(2,1)} %collective-permute-done.4.z_ref), kind=kLoop, calls=%fused_computation.13 | loop fusion | bytes 2359296
  81.9 5.8 %all-to-all-done.1 = bf16[8,24,1536]{2,1,0:T(8,128)(2,1)S(1)} async-done(((bf16[8,24,1536]{2,1,0:T(8,128)(2,1)}), bf16[8,24,1536]{2,1,0:T(8,128)(2,1)S(1)}, u32[]{:S(2)}, u32[]{:S(2)}) %all-to-all-start.1) | async-done | bytes 589856 | tf_op jit(solution)/shard_map/all_to_all | solution.py:352
  88.6 5.3 %shard_map.35 = (bf16[2,4,192,192]{3,2,1,0:T(8,128)(2,1)S(1)}, bf16[2,2,3,192,128]{4,3,2,1,0:T(8,128)(2,1)S(1)}, bf16[2,2,3,192,128]{4,3,2,1,0:T(8,128)(2,1)S(1)}, f32[192,768]{1,0:T(8,128)S(1)}) custom-call(s32[5]{0:T(128)S(1)} %pad_add_fusion.table, bf16[2,24,192,192]{3,2,1,0:T(8,128)(2,1)} %x_ref.21, ...), custom_call_target="tpu_custom_call" | custom-call | tf_op jit(solution)/shard_map/pallas_call | solution.py:297
  96.5 8.3 %shard_map.36 = (bf16[2,8,192,192]{3,2,1,0:T(8,128)(2,1)S(1)}, bf16[2,4,3,192,128]{4,3,2,1,0:T(8,128)(2,1)S(1)}, bf16[2,4,3,192,128]{4,3,2,1,0:T(8,128)(2,1)S(1)}, f32[192,768]{1,0:T(8,128)S(1)}) custom-call(s32[5]{0:T(128)S(1)} %pad_add_fusion.table, bf16[2,24,192,192]{3,2,1,0:T(8,128)(2,1)} %x_ref.21, ...), custom_call_target="tpu_custom_call" | custom-call | tf_op jit(solution)/shard_map/pallas_call | solution.py:297
  104.9 3.3 %collective-permute-start.15 = (bf16[2,4,3,192,128]{4,3,2,1,0:T(8,128)(2,1)S(1)}, bf16[2,4,3,192,128]{4,3,2,1,0:T(8,128)(2,1)S(1)}, u32[]{:S(2)}, u32[]{:S(2)}) collective-permute-start(bf16[2,4,3,192,128]{4,3,2,1,0:T(8,128)(2,1)S(1)} %get-tuple-element.61), channel_id=1, source_target_pairs={{0,16},{8,120},{16,32},{24,8},{32,48},{40,24},{48,64},{56,40},{64,... | collective-permute-start | bytes 3538952 | tf_op jit(solution)/shard_map/ppermute | solution.py:386
  108.2 8.3 %shard_map.37 = (bf16[2,8,192,192]{3,2,1,0:T(8,128)(2,1)S(1)}, bf16[2,4,3,192,128]{4,3,2,1,0:T(8,128)(2,1)S(1)}, bf16[2,4,3,192,128]{4,3,2,1,0:T(8,128)(2,1)S(1)}, f32[192,768]{1,0:T(8,128)S(1)}) custom-call(s32[5]{0:T(128)S(1)} %pad_add_fusion.table, bf16[2,24,192,192]{3,2,1,0:T(8,128)(2,1)} %x_ref.21, ...), custom_call_target="tpu_custom_call" | custom-call | tf_op jit(solution)/shard_map/pallas_call | solution.py:297
  117.6 3.7 %shard_map.38 = (bf16[2,2,192,192]{3,2,1,0:T(8,128)(2,1)S(1)}, bf16[2,1,3,192,128]{4,3,2,1,0:T(8,128)(2,1)S(1)}, bf16[2,1,3,192,128]{4,3,2,1,0:T(8,128)(2,1)S(1)}, f32[192,768]{1,0:T(8,128)S(1)}) custom-call(s32[5]{0:T(128)S(1)} %pad_add_fusion.table, bf16[2,24,192,192]{3,2,1,0:T(8,128)(2,1)} %x_ref.21, ...), custom_call_target="tpu_custom_call" | custom-call | tf_op jit(solution)/shard_map/pallas_call | solution.py:297
  121.4 3.7 %shard_map.39 = (bf16[2,2,192,192]{3,2,1,0:T(8,128)(2,1)S(1)}, bf16[2,1,3,192,128]{4,3,2,1,0:T(8,128)(2,1)S(1)}, bf16[2,1,3,192,128]{4,3,2,1,0:T(8,128)(2,1)S(1)}) custom-call(s32[5]{0:T(128)S(1)} %pad_add_fusion.table, bf16[2,24,192,192]{3,2,1,0:T(8,128)(2,1)} %x_ref.21, bf16[2,24,192,192]{3,2,1,0:T(8,128)(2,1)} %collective-permute-done.2.s_ref, ...), custom_call_target="tpu_custom_call" | custom-call | tf_op jit(solution)/shard_map/pallas_call | solution.py:297
  125.2 3.3 %collective-permute-start.11 = (bf16[2,1,3,192,128]{4,3,2,1,0:T(8,128)(2,1)S(1)}, bf16[2,1,3,192,128]{4,3,2,1,0:T(8,128)(2,1)S(1)}, u32[]{:S(2)}, u32[]{:S(2)}) collective-permute-start(bf16[2,1,3,192,128]{4,3,2,1,0:T(8,128)(2,1)S(1)} %get-tuple-element.55), channel_id=1, source_target_pairs={{0,16},{8,120},{16,32},{24,8},{32,48},{40,24},{48,64},{56,40},{64,... | collective-permute-start | bytes 884744 | tf_op jit(solution)/shard_map/ppermute | solution.py:386
  131.5 2.9 %shard_map.41.refs_0_ = bf16[2,24,192,192]{3,2,1,0:T(8,128)(2,1)} custom-call(s32[5]{0:T(128)S(1)} %pad_add_fusion.table, bf16[2,8,192,192]{3,2,1,0:T(8,128)(2,1)S(1)} %get-tuple-element.59.x_ref, bf16[2,4,3,192,128]{4,3,2,1,0:T(8,128)(2,1)S(1)} %collective-permute-done.14.s_ref, ...), custom_call_target="tpu_custom_call", output_to_operand_aliasing={{}: (4, {})} | custom-call | tf_op jit(solution)/shard_map/pallas_call | solution.py:330
  134.4 2.9 %shard_map.42.refs_0_ = bf16[2,24,192,192]{3,2,1,0:T(8,128)(2,1)} custom-call(s32[5]{0:T(128)S(1)} %pad_add_fusion.table, bf16[2,8,192,192]{3,2,1,0:T(8,128)(2,1)S(1)} %get-tuple-element.56.x_ref, bf16[2,4,3,192,128]{4,3,2,1,0:T(8,128)(2,1)S(1)} %collective-permute-done.12.s_ref, ...), custom_call_target="tpu_custom_call", output_to_operand_aliasing={{}: (4, {})} | custom-call | tf_op jit(solution)/shard_map/pallas_call | solution.py:330
  (55 shorter events, 25.2 us)
Async XLA Ops:
  0.0 29.0 %collective-permute-start.2 = (bf16[2,24,192,192]{3,2,1,0:T(8,128)(2,1)}, bf16[2,24,192,192]{3,2,1,0:T(8,128)(2,1)}, u32[]{:S(2)}, u32[]{:S(2)}) collective-permute-start(bf16[2,24,192,192]{3,2,1,0:T(8,128)(2,1)} %x_ref.21), channel_id=1, source_target_pairs={{0,8},{8,0},{16,24},{24,16},{32,40},{40,32},{48,56},{56,48},{64,72... | collective-permute-start | bytes 10616840 | tf_op jit(solution)/shard_map/ppermute | solution.py:354
  3.9 5.7 %copy-start.5 = (s32[2,2]{1,0:T(2,128)S(1)}, s32[2,2]{1,0:T(2,128)}, u32[]{:S(2)}) copy-start(s32[2,2]{1,0:T(2,128)} %param.3) | copy-start | bytes 52
  3.9 25.1 %collective-permute-start.3 = (bf16[2,6,3,192,128]{4,3,2,1,0:T(8,128)(2,1)}, bf16[2,6,3,192,128]{4,3,2,1,0:T(8,128)(2,1)S(1)}, u32[]{:S(2)}, u32[]{:S(2)}) collective-permute-start(bf16[2,6,3,192,128]{4,3,2,1,0:T(8,128)(2,1)} %shard_map.28), channel_id=1, source_target_pairs={{0,112},{8,24},{16,0},{24,40},{32,16},{40,56},{48,32},{56,72},{64,... | collective-permute-start | bytes 5308424 | tf_op jit(solution)/shard_map/ppermute | solution.py:362
  8.0 33.8 %collective-permute-start.4 = (bf16[2,4,3,192,128]{4,3,2,1,0:T(8,128)(2,1)}, bf16[2,4,3,192,128]{4,3,2,1,0:T(8,128)(2,1)}, u32[]{:S(2)}, u32[]{:S(2)}) collective-permute-start(bf16[2,4,3,192,128]{4,3,2,1,0:T(8,128)(2,1)} %shard_map.29), channel_id=1, source_target_pairs={{0,112},{8,24},{16,0},{24,40},{32,16},{40,56},{48,32},{56,72},{64,... | collective-permute-start | bytes 3538952 | tf_op jit(solution)/shard_map/ppermute | solution.py:362
  9.7 6.8 %collective-permute-start = (s32[2,2]{1,0:T(2,128)S(1)}, s32[2,2]{1,0:T(2,128)S(1)}, u32[]{:S(2)}, u32[]{:S(2)}) collective-permute-start(s32[2,2]{1,0:T(2,128)S(1)} %copy-done.5), channel_id=1, source_target_pairs={{0,8},{8,0},{16,24},{24,16},{32,40},{40,32},{48,56},{56,48},{64,72... | collective-permute-start | bytes 56 | tf_op jit(solution)/shard_map/ppermute | solution.py:355
  13.8 35.3 %collective-permute-start.5 = (bf16[2,2,3,192,128]{4,3,2,1,0:T(8,128)(2,1)}, bf16[2,2,3,192,128]{4,3,2,1,0:T(8,128)(2,1)S(1)}, u32[]{:S(2)}, u32[]{:S(2)}) collective-permute-start(bf16[2,2,3,192,128]{4,3,2,1,0:T(8,128)(2,1)} %shard_map.30), channel_id=1, source_target_pairs={{0,112},{8,24},{16,0},{24,40},{32,16},{40,56},{48,32},{56,72},{64,... | collective-permute-start | bytes 1769480 | tf_op jit(solution)/shard_map/ppermute | solution.py:362
  15.6 33.5 %copy-start.1 = (f32[192,384]{1,0:T(8,128)}, f32[192,384]{1,0:T(8,128)S(1)}, u32[]{:S(2)}) copy-start(f32[192,384]{1,0:T(8,128)S(1)} %get-tuple-element.65.log_ref) | copy-start | bytes 884740
  15.6 33.5 %copy-start.2 = (f32[192,384]{1,0:T(8,128)}, f32[192,384]{1,0:T(8,128)S(1)}, u32[]{:S(2)}) copy-start(f32[192,384]{1,0:T(8,128)S(1)} %get-tuple-element.66.r_ref) | copy-start | bytes 884740
  16.4 32.7 %copy-start.3 = (bf16[192,192]{1,0:T(8,128)(2,1)}, bf16[192,192]{1,0:T(8,128)(2,1)S(1)}, u32[]{:S(2)}) copy-start(bf16[192,192]{1,0:T(8,128)(2,1)S(1)} %sine_convert_fusion.sines_ref) | copy-start | bytes 221188
  16.4 5.3 %collective-permute-start.1 = (s32[2,2]{1,0:T(2,128)S(1)}, s32[2,2]{1,0:T(2,128)S(1)}, u32[]{:S(2)}, u32[]{:S(2)}) collective-permute-start(s32[2,2]{1,0:T(2,128)S(1)} %collective-permute-done), channel_id=1, source_target_pairs={{0,24},{8,112},{16,40},{24,0},{32,56},{40,16},{48,72},{56,32},{64,... | collective-permute-start | bytes 56 | tf_op jit(solution)/shard_map/ppermute | solution.py:355
  29.0 2.3 %copy-start = (bf16[2,24,192,192]{3,2,1,0:T(8,128)(2,1)S(1)}, bf16[2,24,192,192]{3,2,1,0:T(8,128)(2,1)}, u32[]{:S(2)}) copy-start(bf16[2,24,192,192]{3,2,1,0:T(8,128)(2,1)} %x_ref.21) | copy-start | bytes 10616836
  54.1 17.7 %all-to-all-start = ((bf16[8,24,1536]{2,1,0:T(8,128)(2,1)}), bf16[8,24,1536]{2,1,0:T(8,128)(2,1)S(1)}, u32[]{:S(2)}, u32[]{:S(2)}) async-start(bf16[8,24,1536]{2,1,0:T(8,128)(2,1)} %bitcast.11), calls=%async_computation | async-start | bytes 1179648 | tf_op jit(solution)/shard_map/all_to_all | solution.py:352
  73.5 14.2 %all-to-all-start.1 = ((bf16[8,24,1536]{2,1,0:T(8,128)(2,1)}), bf16[8,24,1536]{2,1,0:T(8,128)(2,1)S(1)}, u32[]{:S(2)}, u32[]{:S(2)}) async-start(bf16[8,24,1536]{2,1,0:T(8,128)(2,1)} %bitcast.3), calls=%async_computation.1 | async-start | bytes 1179648 | tf_op jit(solution)/shard_map/all_to_all | solution.py:352
  87.7 0.8 copy-start.4
  93.9 14.3 %collective-permute-start.6 = (bf16[2,2,3,192,128]{4,3,2,1,0:T(8,128)(2,1)S(1)}, bf16[2,2,3,192,128]{4,3,2,1,0:T(8,128)(2,1)S(1)}, u32[]{:S(2)}, u32[]{:S(2)}) collective-permute-start(bf16[2,2,3,192,128]{4,3,2,1,0:T(8,128)(2,1)S(1)} %get-tuple-element.43), channel_id=1, source_target_pairs={{0,8},{8,0},{16,24},{24,16},{32,40},{40,32},{48,56},{56,48},{64,72... | collective-permute-start | bytes 1769480 | tf_op jit(solution)/shard_map/ppermute | solution.py:386
  95.7 12.5 %collective-permute-start.7 = (bf16[2,2,3,192,128]{4,3,2,1,0:T(8,128)(2,1)S(1)}, bf16[2,2,3,192,128]{4,3,2,1,0:T(8,128)(2,1)S(1)}, u32[]{:S(2)}, u32[]{:S(2)}) collective-permute-start(bf16[2,2,3,192,128]{4,3,2,1,0:T(8,128)(2,1)S(1)} %get-tuple-element.44), channel_id=1, source_target_pairs={{0,16},{8,120},{16,32},{24,8},{32,48},{40,24},{48,64},{56,40},{64,... | collective-permute-start | bytes 1769480 | tf_op jit(solution)/shard_map/ppermute | solution.py:386
  104.8 20.4 %collective-permute-start.14 = (bf16[2,4,3,192,128]{4,3,2,1,0:T(8,128)(2,1)S(1)}, bf16[2,4,3,192,128]{4,3,2,1,0:T(8,128)(2,1)S(1)}, u32[]{:S(2)}, u32[]{:S(2)}) collective-permute-start(bf16[2,4,3,192,128]{4,3,2,1,0:T(8,128)(2,1)S(1)} %get-tuple-element.60), channel_id=1, source_target_pairs={{0,8},{8,0},{16,24},{24,16},{32,40},{40,32},{48,56},{56,48},{64,72... | collective-permute-start | bytes 3538952 | tf_op jit(solution)/shard_map/ppermute | solution.py:386
  104.9 23.6 %collective-permute-start.15 = (bf16[2,4,3,192,128]{4,3,2,1,0:T(8,128)(2,1)S(1)}, bf16[2,4,3,192,128]{4,3,2,1,0:T(8,128)(2,1)S(1)}, u32[]{:S(2)}, u32[]{:S(2)}) collective-permute-start(bf16[2,4,3,192,128]{4,3,2,1,0:T(8,128)(2,1)S(1)} %get-tuple-element.61), channel_id=1, source_target_pairs={{0,16},{8,120},{16,32},{24,8},{32,48},{40,24},{48,64},{56,40},{64,... | collective-permute-start | bytes 3538952 | tf_op jit(solution)/shard_map/ppermute | solution.py:386
  116.5 12.0 %collective-permute-start.12 = (bf16[2,4,3,192,128]{4,3,2,1,0:T(8,128)(2,1)S(1)}, bf16[2,4,3,192,128]{4,3,2,1,0:T(8,128)(2,1)S(1)}, u32[]{:S(2)}, u32[]{:S(2)}) collective-permute-start(bf16[2,4,3,192,128]{4,3,2,1,0:T(8,128)(2,1)S(1)} %get-tuple-element.57), channel_id=1, source_target_pairs={{0,8},{8,0},{16,24},{24,16},{32,40},{40,32},{48,56},{56,48},{64,72... | collective-permute-start | bytes 3538952 | tf_op jit(solution)/shard_map/ppermute | solution.py:386
  116.6 17.9 %collective-permute-start.13 = (bf16[2,4,3,192,128]{4,3,2,1,0:T(8,128)(2,1)S(1)}, bf16[2,4,3,192,128]{4,3,2,1,0:T(8,128)(2,1)S(1)}, u32[]{:S(2)}, u32[]{:S(2)}) collective-permute-start(bf16[2,4,3,192,128]{4,3,2,1,0:T(8,128)(2,1)S(1)} %get-tuple-element.58), channel_id=1, source_target_pairs={{0,16},{8,120},{16,32},{24,8},{32,48},{40,24},{48,64},{56,40},{64,... | collective-permute-start | bytes 3538952 | tf_op jit(solution)/shard_map/ppermute | solution.py:386
  121.3 16.0 %collective-permute-start.10 = (bf16[2,1,3,192,128]{4,3,2,1,0:T(8,128)(2,1)S(1)}, bf16[2,1,3,192,128]{4,3,2,1,0:T(8,128)(2,1)S(1)}, u32[]{:S(2)}, u32[]{:S(2)}) collective-permute-start(bf16[2,1,3,192,128]{4,3,2,1,0:T(8,128)(2,1)S(1)} %get-tuple-element.54), channel_id=1, source_target_pairs={{0,8},{8,0},{16,24},{24,16},{32,40},{40,32},{48,56},{56,48},{64,72... | collective-permute-start | bytes 884744 | tf_op jit(solution)/shard_map/ppermute | solution.py:386
  125.2 12.2 %collective-permute-start.11 = (bf16[2,1,3,192,128]{4,3,2,1,0:T(8,128)(2,1)S(1)}, bf16[2,1,3,192,128]{4,3,2,1,0:T(8,128)(2,1)S(1)}, u32[]{:S(2)}, u32[]{:S(2)}) collective-permute-start(bf16[2,1,3,192,128]{4,3,2,1,0:T(8,128)(2,1)S(1)} %get-tuple-element.55), channel_id=1, source_target_pairs={{0,16},{8,120},{16,32},{24,8},{32,48},{40,24},{48,64},{56,40},{64,... | collective-permute-start | bytes 884744 | tf_op jit(solution)/shard_map/ppermute | solution.py:386
  128.5 10.4 %collective-permute-start.8 = (bf16[2,1,3,192,128]{4,3,2,1,0:T(8,128)(2,1)S(1)}, bf16[2,1,3,192,128]{4,3,2,1,0:T(8,128)(2,1)S(1)}, u32[]{:S(2)}, u32[]{:S(2)}) collective-permute-start(bf16[2,1,3,192,128]{4,3,2,1,0:T(8,128)(2,1)S(1)} %get-tuple-element.51), channel_id=1, source_target_pairs={{0,8},{8,0},{16,24},{24,16},{32,40},{40,32},{48,56},{56,48},{64,72... | collective-permute-start | bytes 884744 | tf_op jit(solution)/shard_map/ppermute | solution.py:386
  128.5 11.8 %collective-permute-start.9 = (bf16[2,1,3,192,128]{4,3,2,1,0:T(8,128)(2,1)S(1)}, bf16[2,1,3,192,128]{4,3,2,1,0:T(8,128)(2,1)S(1)}, u32[]{:S(2)}, u32[]{:S(2)}) collective-permute-start(bf16[2,1,3,192,128]{4,3,2,1,0:T(8,128)(2,1)S(1)} %get-tuple-element.52), channel_id=1, source_target_pairs={{0,16},{8,120},{16,32},{24,8},{32,48},{40,24},{48,64},{56,40},{64,... | collective-permute-start | bytes 884744 | tf_op jit(solution)/shard_map/ppermute | solution.py:386
